TPU v7x, 32 devices: a whole 2x2x4 slice. The times are simulated.
32 devices in a mesh: dp: 16 (over z, y, x), pair: 2 (over core).
Axes of the slice: x: 2, y: 2, z: 4, core: 2. Of those that a mesh axis runs over, the one named last changes fastest.
Arguments:
- tokens: bfloat16 [32768, 768], P(('dp', 'pair')), may hold values from -10 to 10
- mlm_grad: bfloat16 [32768, 768], P(('dp', 'pair')), may hold values from -6 to 6
- doc_ids: int32 [32, 8], P('dp'), may hold values from -1 to 127, as said below
- span_counts: int32 [32], P('dp'), may hold values from 1 to 8, as said below
- qkv_weight: float32 [768, 2304], P(('dp', 'pair')), may hold values from -0.21875 to 0.21875
- proj_weight: float32 [768, 768], P(('dp', 'pair')), may hold values from -0.625 to 0.625
- inner_weight: float32 [768, 3072], P(('dp', 'pair')), may hold values from -0.21875 to 0.21875
- outer_weight: float32 [3072, 768], P(('dp', 'pair')), may hold values from -0.109375 to 0.109375
- affine_params: float32 [12, 768], P(None, ('dp', 'pair')), may hold values from -0.5 to 2.5
- qkv_moment: float32 [768, 2304], P(('dp', 'pair')), may hold values from -0.625 to 0.625
- proj_moment: float32 [768, 768], P(('dp', 'pair')), may hold values from -0.625 to 0.625
- inner_moment: float32 [768, 3072], P(('dp', 'pair')), may hold values from -0.625 to 0.625
- outer_moment: float32 [3072, 768], P(('dp', 'pair')), may hold values from -0.625 to 0.625
- affine_moment: float32 [12, 768], P(None, ('dp', 'pair')), may hold values from -2.5 to 2.5
- qkv_square: float32 [768, 2304], P(('dp', 'pair')), may hold values from 0.00014124246 to 0.00056496984
- proj_square: float32 [768, 768], P(('dp', 'pair')), may hold values from 0.00014124246 to 0.00056496984
- inner_square: float32 [768, 3072], P(('dp', 'pair')), may hold values from 0.00014124246 to 0.00056496984
- outer_square: float32 [3072, 768], P(('dp', 'pair')), may hold values from 0.00014124246 to 0.00056496984
- affine_square: float32 [12, 768], P(None, ('dp', 'pair')), may hold values from 0.0022598794 to 0.0090395175
Outputs:
- weight_qkv: float32 [768, 2304], P(('dp', 'pair'))
- weight_proj: float32 [768, 768], P(('dp', 'pair'))
- weight_inner: float32 [768, 3072], P(('dp', 'pair'))
- weight_outer: float32 [3072, 768], P(('dp', 'pair'))
- weight_affine: float32 [12, 768], P(None, ('dp', 'pair'))
- moment_qkv: float32 [768, 2304], P(('dp', 'pair'))
- moment_proj: float32 [768, 768], P(('dp', 'pair'))
- moment_inner: float32 [768, 3072], P(('dp', 'pair'))
- moment_outer: float32 [3072, 768], P(('dp', 'pair'))
- moment_affine: float32 [12, 768], P(None, ('dp', 'pair'))
- square_qkv: float32 [768, 2304], P(('dp', 'pair'))
- square_proj: float32 [768, 768], P(('dp', 'pair'))
- square_inner: float32 [768, 3072], P(('dp', 'pair'))
- square_outer: float32 [3072, 768], P(('dp', 'pair'))
- square_affine: float32 [12, 768], P(None, ('dp', 'pair'))
- layer_out: bfloat16 [32768, 768], P(('dp', 'pair'))
- input_grad: float32 [32768, 768], P(('dp', 'pair'))
- grad_norm: float32 [], replicated
- mean_loss: float32 [], replicated
Inputs may be any that keep to these rules, and one draw needn't show every extreme that they name: `doc_ids`: row 2g+p holds the document of each span slot of pair index p in group g; live slots are the first span_counts[2g+p]; on pair index 0 the live slot s holds g * 8 + s; each live slot of pair index 1 holds the id of a distinct live slot of pair index 0 of the same group; slots past the live count hold -1. `span_counts`: entry 2g+1 is never larger than entry 2g.
All inputs are finite; a program needn't handle non-finite values.
Results may differ from a plain program's by a relative error of at most 0.018.
Values may be sent and summed in bfloat16 or wider, within the bound.
No kernel may reach another device: no remote copies, remote signals or barrier semaphores. Data moves between devices by JAX's collectives and lax.ppermute only.
A program may use at most 192 MiB of HBM per device.

v0:
```python
from functools import partial

import jax
import jax.numpy as jnp
from jax import lax
from jax.sharding import PartitionSpec as P

HEADS = 12
HD = 64
L = 128
STEP = 10


LN_EPS = 1e-12
LOSS_WEIGHT = 8.0
CLIP_NORM = 1000.0
BETA_ONE = 0.9
BETA_TWO = 0.999
ADAM_EPS = 1e-08
RATE_MATRIX = 0.05
DECAY_MATRIX = 0.01
RATE_AFFINE = 0.8
DECAY_AFFINE = 0.0


def swapped(block, axis, bit):
    count = lax.axis_size(axis)
    route = []
    for low in range(count):
        high = low | 1 << bit
        if high != low and high < count:
            route += [(low, high), (high, low)]
    return lax.ppermute(block, axis, route)


def contract_rows(left, right):
    return lax.dot_general(
        left, right, (((0,), (0,)), ((), ())), preferred_element_type=jnp.float32
    )


def contract_cols(left, right):
    return lax.dot_general(
        left, right, (((1,), (1,)), ((), ())), preferred_element_type=jnp.float32
    )


def normalize(total):
    centered = total - jnp.mean(total, axis=-1, keepdims=True)
    variance = jnp.mean(centered * centered, axis=-1, keepdims=True)
    scale_inv = lax.rsqrt(variance + LN_EPS)
    return (centered * scale_inv, scale_inv)


def normalize_back(upstream, normed, scale_inv, gain):
    scaled = upstream * gain
    return scale_inv * (
        scaled
        - jnp.mean(scaled, axis=-1, keepdims=True)
        - normed * jnp.mean(scaled * normed, axis=-1, keepdims=True)
    )


def attend(tokens, qkv_w, qkv_bias):
    rows, width = tokens.shape
    projected = (jnp.dot(tokens, qkv_w, preferred_element_type=jnp.float32) + qkv_bias).astype(
        jnp.bfloat16
    )
    split_heads = projected.reshape(rows // L, L, 3, HEADS, HD)
    queries, key_rows, values = (split_heads[:, :, 0], split_heads[:, :, 1], split_heads[:, :, 2])
    scores = jnp.einsum(
        "nqhe,nkhe->nhqk", queries, key_rows, preferred_element_type=jnp.float32
    ) * HD ** (-0.5)
    peak_score = jnp.max(scores, axis=-1, keepdims=True)
    exponent = jnp.exp(scores - peak_score)
    attention = exponent / jnp.sum(exponent, axis=-1, keepdims=True)
    attention_low = attention.astype(jnp.bfloat16)
    context = jnp.einsum(
        "nhqk,nkhe->nqhe", attention_low, values, preferred_element_type=jnp.float32
    )
    context = context.astype(jnp.bfloat16).reshape(rows, width)
    return (queries, key_rows, values, attention, attention_low, context)


def contrast(anchor, keys_side, anchor_ids, key_ids, anchor_live, key_live):
    sims = lax.dot_general(
        anchor,
        keys_side,
        (((1,), (1,)), ((), ())),
        precision=lax.Precision.HIGHEST,
        preferred_element_type=jnp.float32,
    ) * anchor.shape[1] ** (-0.5)
    masked = jnp.where(key_live[None, :], sims, -1000000000.0)
    peak_score = jnp.max(masked, axis=1, keepdims=True)
    weights_exp = jnp.where(key_live[None, :], jnp.exp(masked - peak_score), 0.0)
    log_total = peak_score[:, 0] + jnp.log(jnp.sum(weights_exp, axis=1))
    match = (anchor_ids[:, None] == key_ids[None, :]) & key_live[None, :] & anchor_live[:, None]
    active_rows = jnp.any(match, axis=1)
    hit_score = jnp.sum(jnp.where(match, sims, 0.0), axis=1)
    return jnp.sum(jnp.where(active_rows, log_total - hit_score, 0.0))


def adamw(master, moment, square, gradient, factor, rate, decay):
    clipped = gradient * factor
    moment_new = BETA_ONE * moment + (1.0 - BETA_ONE) * clipped
    square_new = BETA_TWO * square + (1.0 - BETA_TWO) * clipped * clipped
    mean_hat = moment_new / (1.0 - BETA_ONE**STEP)
    square_hat = square_new / (1.0 - BETA_TWO**STEP)
    master_new = master - rate * (mean_hat / (jnp.sqrt(square_hat) + ADAM_EPS) + decay * master)
    return (master_new, moment_new, square_new)


def body(
    tokens,
    mlm_grad,
    doc_ids,
    span_counts,
    qkv_weight,
    proj_weight,
    inner_weight,
    outer_weight,
    affine_params,
    qkv_moment,
    proj_moment,
    inner_moment,
    outer_moment,
    affine_moment,
    qkv_square,
    proj_square,
    inner_square,
    outer_square,
    affine_square,
):
    rows, width = tokens.shape
    spans = rows // L
    gathered = (
        lax.all_gather(qkv_weight.astype(jnp.bfloat16), ("dp", "pair"), axis=0, tiled=True),
        lax.all_gather(proj_weight.astype(jnp.bfloat16), ("dp", "pair"), axis=0, tiled=True),
        lax.all_gather(inner_weight.astype(jnp.bfloat16), ("dp", "pair"), axis=0, tiled=True),
        lax.all_gather(outer_weight.astype(jnp.bfloat16), ("dp", "pair"), axis=0, tiled=True),
        lax.all_gather(affine_params.astype(jnp.bfloat16), ("dp", "pair"), axis=1, tiled=True),
    )
    qkv_w, proj_w, inner_w, outer_w, affine_low = gathered
    affine = affine_low.astype(jnp.float32)
    hidden = inner_w.shape[1]
    gain_one, shift_one, gain_two, shift_two = (affine[0], affine[1], affine[2], affine[3])
    bias_query, bias_value, bias_proj, bias_outer = (affine[4], affine[5], affine[6], affine[7])
    bias_inner = affine[8:12].reshape(hidden)
    qkv_bias = jnp.concatenate([bias_query, jnp.zeros((width,), jnp.float32), bias_value])
    queries, key_rows, values, attention, attention_low, context = attend(tokens, qkv_w, qkv_bias)
    attended = jnp.dot(context, proj_w, preferred_element_type=jnp.float32) + bias_proj
    normed_one, inv_one = normalize(tokens.astype(jnp.float32) + attended)
    skip_rows = normed_one * gain_one + shift_one
    skip_low = skip_rows.astype(jnp.bfloat16)
    inner_pre = jnp.dot(skip_low, inner_w, preferred_element_type=jnp.float32) + bias_inner
    activated = jax.nn.gelu(inner_pre, approximate=False).astype(jnp.bfloat16)
    outer_out = jnp.dot(activated, outer_w, preferred_element_type=jnp.float32) + bias_outer
    normed_two, inv_two = normalize(skip_rows + outer_out)
    result = normed_two * gain_two + shift_two
    layer_out = result.astype(jnp.bfloat16)
    cls_rows = layer_out.reshape(spans, L, width)[:, 0, :]
    side = lax.axis_index("pair")
    own_ids = jnp.where(side == 0, doc_ids[0], doc_ids[1])
    other_ids = jnp.where(side == 0, doc_ids[1], doc_ids[0])
    own_count = jnp.where(side == 0, span_counts[0], span_counts[1])
    other_count = jnp.where(side == 0, span_counts[1], span_counts[0])
    slot_index = jnp.arange(spans)
    own_live = slot_index < own_count
    other_live = slot_index < other_count
    partner_cls = swapped(cls_rows, "pair", 0)

    def contrast_local(anchor, keys_side):
        return contrast(anchor, keys_side, own_ids, other_ids, own_live, other_live)

    loss_part, pull_back = jax.vjp(
        contrast_local, cls_rows.astype(jnp.float32), partner_cls.astype(jnp.float32)
    )
    grad_own, grad_other = pull_back(jnp.asarray(LOSS_WEIGHT, jnp.float32))
    grad_returned = swapped(grad_other, "pair", 0)
    grad_cls = grad_own + grad_returned
    row_live = jnp.repeat(own_live, L).astype(jnp.float32)
    upstream = mlm_grad.astype(jnp.float32) * row_live[:, None]
    upstream = upstream.reshape(spans, L, width).at[:, 0, :].add(grad_cls).reshape(rows, width)
    tokens_again, normed_again, upstream = lax.optimization_barrier((tokens, normed_one, upstream))
    queries, key_rows, values, attention, attention_low, context = attend(
        tokens_again, qkv_w, qkv_bias
    )
    skip_low = (normed_again * gain_one + shift_one).astype(jnp.bfloat16)
    inner_pre = jnp.dot(skip_low, inner_w, preferred_element_type=jnp.float32) + bias_inner
    activated = jax.nn.gelu(inner_pre, approximate=False).astype(jnp.bfloat16)
    gain_two_grad = jnp.sum(upstream * normed_two, axis=0)
    shift_two_grad = jnp.sum(upstream, axis=0)
    grad_two = normalize_back(upstream, normed_two, inv_two, gain_two)
    bias_outer_grad = jnp.sum(grad_two, axis=0)
    grad_two_low = grad_two.astype(jnp.bfloat16)
    outer_grad = contract_rows(activated, grad_two_low)
    act_grad = contract_cols(grad_two_low, outer_w)
    _, gelu_pull = jax.vjp(partial(jax.nn.gelu, approximate=False), inner_pre)
    inner_grad_pre = gelu_pull(act_grad)[0]
    bias_inner_grad = jnp.sum(inner_grad_pre, axis=0)
    inner_low = inner_grad_pre.astype(jnp.bfloat16)
    inner_grad = contract_rows(skip_low, inner_low)
    skip_grad = contract_cols(inner_low, inner_w) + grad_two
    gain_one_grad = jnp.sum(skip_grad * normed_one, axis=0)
    shift_one_grad = jnp.sum(skip_grad, axis=0)
    grad_one = normalize_back(skip_grad, normed_one, inv_one, gain_one)
    bias_proj_grad = jnp.sum(grad_one, axis=0)
    grad_one_low = grad_one.astype(jnp.bfloat16)
    proj_grad = contract_rows(context, grad_one_low)
    context_grad = (
        contract_cols(grad_one_low, proj_w).astype(jnp.bfloat16).reshape(spans, L, HEADS, HD)
    )
    attention_grad = jnp.einsum(
        "nqhe,nkhe->nhqk", context_grad, values, preferred_element_type=jnp.float32
    )
    value_grad = jnp.einsum(
        "nhqk,nqhe->nkhe", attention_low, context_grad, preferred_element_type=jnp.float32
    )
    score_grad = attention * (
        attention_grad - jnp.sum(attention_grad * attention, axis=-1, keepdims=True)
    )
    score_low = (score_grad * HD ** (-0.5)).astype(jnp.bfloat16)
    query_grad = jnp.einsum(
        "nhqk,nkhe->nqhe", score_low, key_rows, preferred_element_type=jnp.float32
    )
    key_grad = jnp.einsum("nhqk,nqhe->nkhe", score_low, queries, preferred_element_type=jnp.float32)
    qkv_rows_grad = jnp.stack([query_grad, key_grad, value_grad], axis=2).reshape(rows, 3 * width)
    bias_query_grad = jnp.sum(query_grad.reshape(rows, width), axis=0)
    bias_value_grad = jnp.sum(value_grad.reshape(rows, width), axis=0)
    qkv_low = qkv_rows_grad.astype(jnp.bfloat16)
    qkv_grad = contract_rows(tokens, qkv_low)
    input_grad = contract_cols(qkv_low, qkv_w) + grad_one
    affine_grad = jnp.concatenate(
        [
            jnp.stack(
                [
                    gain_one_grad,
                    shift_one_grad,
                    gain_two_grad,
                    shift_two_grad,
                    bias_query_grad,
                    bias_value_grad,
                    bias_proj_grad,
                    bias_outer_grad,
                ]
            ),
            bias_inner_grad.reshape(4, width),
        ],
        axis=0,
    )
    gradients = (qkv_grad, proj_grad, inner_grad, outer_grad, affine_grad)
    summed = (
        lax.psum_scatter(gradients[0], "dp", scatter_dimension=0, tiled=True),
        lax.psum_scatter(gradients[1], "dp", scatter_dimension=0, tiled=True),
        lax.psum_scatter(gradients[2], "dp", scatter_dimension=0, tiled=True),
        lax.psum_scatter(gradients[3], "dp", scatter_dimension=0, tiled=True),
        lax.psum_scatter(gradients[4], "dp", scatter_dimension=1, tiled=True),
    )
    shards = (
        lax.psum_scatter(
            summed[0].astype(jnp.bfloat16), "pair", scatter_dimension=0, tiled=True
        ).astype(jnp.float32),
        lax.psum_scatter(
            summed[1].astype(jnp.bfloat16), "pair", scatter_dimension=0, tiled=True
        ).astype(jnp.float32),
        lax.psum_scatter(
            summed[2].astype(jnp.bfloat16), "pair", scatter_dimension=0, tiled=True
        ).astype(jnp.float32),
        lax.psum_scatter(
            summed[3].astype(jnp.bfloat16), "pair", scatter_dimension=0, tiled=True
        ).astype(jnp.float32),
        lax.psum_scatter(
            summed[4].astype(jnp.bfloat16), "pair", scatter_dimension=1, tiled=True
        ).astype(jnp.float32),
    )
    local_squares = jnp.sum(jnp.stack([jnp.sum(shard_item * shard_item) for shard_item in shards]))
    totals = lax.psum((local_squares, loss_part), ("dp", "pair"))
    grad_norm = jnp.sqrt(totals[0])
    factor = jnp.minimum(1.0, CLIP_NORM / (grad_norm + 1e-06))
    mean_loss = totals[1] / (spans * lax.axis_size("dp") * lax.axis_size("pair"))
    masters = (qkv_weight, proj_weight, inner_weight, outer_weight, affine_params)
    moments = (qkv_moment, proj_moment, inner_moment, outer_moment, affine_moment)
    squares_old = (qkv_square, proj_square, inner_square, outer_square, affine_square)
    rates = (RATE_MATRIX, RATE_MATRIX, RATE_MATRIX, RATE_MATRIX, RATE_AFFINE)
    decays = (DECAY_MATRIX, DECAY_MATRIX, DECAY_MATRIX, DECAY_MATRIX, DECAY_AFFINE)
    updated = [
        adamw(
            masters[index],
            moments[index],
            squares_old[index],
            shards[index],
            factor,
            rates[index],
            decays[index],
        )
        for index in range(5)
    ]
    return (
        updated[0][0],
        updated[1][0],
        updated[2][0],
        updated[3][0],
        updated[4][0],
        updated[0][1],
        updated[1][1],
        updated[2][1],
        updated[3][1],
        updated[4][1],
        updated[0][2],
        updated[1][2],
        updated[2][2],
        updated[3][2],
        updated[4][2],
        layer_out,
        input_grad,
        grad_norm,
        mean_loss,
    )


def solution(mesh):
    placed = (
        P(("dp", "pair"), None),
        P(("dp", "pair"), None),
        P("dp", None),
        P("dp"),
        P(("dp", "pair"), None),
        P(("dp", "pair"), None),
        P(("dp", "pair"), None),
        P(("dp", "pair"), None),
        P(None, ("dp", "pair")),
        P(("dp", "pair"), None),
        P(("dp", "pair"), None),
        P(("dp", "pair"), None),
        P(("dp", "pair"), None),
        P(None, ("dp", "pair")),
        P(("dp", "pair"), None),
        P(("dp", "pair"), None),
        P(("dp", "pair"), None),
        P(("dp", "pair"), None),
        P(None, ("dp", "pair")),
    )
    return jax.shard_map(
        body,
        mesh=mesh,
        in_specs=placed,
        out_specs=(
            P(("dp", "pair"), None),
            P(("dp", "pair"), None),
            P(("dp", "pair"), None),
            P(("dp", "pair"), None),
            P(None, ("dp", "pair")),
            P(("dp", "pair"), None),
            P(("dp", "pair"), None),
            P(("dp", "pair"), None),
            P(("dp", "pair"), None),
            P(None, ("dp", "pair")),
            P(("dp", "pair"), None),
            P(("dp", "pair"), None),
            P(("dp", "pair"), None),
            P(("dp", "pair"), None),
            P(None, ("dp", "pair")),
            P(("dp", "pair"), None),
            P(("dp", "pair"), None),
            P(),
            P(),
        ),
        check_vma=False,
    )
```

profile of v0, /device:TPU:0, one launch (start us, length us, event | category | flops | bytes accessed | tf_op | source)
XLA Modules:
  0.0 1282.5 jit_solution(9597524986094519047)
XLA Ops:
  18.5 43.8 %all-gather = bf16[32,24,12]{1,2,0:T(8,128)(2,1)S(1)} all-gather(bf16[1,24,12]{1,2,0:T(8,128)(2,1)S(1)} %convert_bitcast_fusion), channel_id=1, replica_groups=mesh['dp'=16,'pair'=2] {'dp','pair'}, dimensions={0}, use_global_device_ids=true | all-gather | bytes 19008 | tf_op jit(solution)/shard_map/all_gather | solution.py:141
  63.7 10.8 all-gather.6.cloned.1.call-done
  74.5 8.4 add_convert_fusion.1
  82.9 6.6 copy.121
  89.5 3.6 copy.165
  94.5 5.9 fusion.183
  102.6 28.2 %all-gather.8.cloned.1.call-done = bf16[768,768]{1,0:T(8,128)(2,1)} async-done(((bf16[24,768]{1,0:T(8,128)(2,1)}), bf16[768,768]{1,0:T(8,128)(2,1)}) %all-gather.8.cloned.1.call-update) | async-done | bytes 1179664 | tf_op jit(solution)/shard_map/all_gather | solution.py:138
  130.9 3.0 fusion.184
  138.1 58.8 %all-gather.10.cloned.1.call-done = bf16[768,3072]{1,0:T(8,128)(2,1)} async-done(((bf16[24,3072]{1,0:T(8,128)(2,1)}), bf16[768,3072]{1,0:T(8,128)(2,1)}) %all-gather.10.cloned.1.call-update) | async-done | bytes 4718608 | tf_op jit(solution)/shard_map/all_gather | solution.py:139
  196.9 65.8 %all-gather.12.cloned.1.call-done = bf16[3072,768]{1,0:T(8,128)(2,1)} async-done(((bf16[96,768]{1,0:T(8,128)(2,1)}), bf16[3072,768]{1,0:T(8,128)(2,1)}) %all-gather.12.cloned.1.call-update) | async-done | bytes 4718608 | tf_op jit(solution)/shard_map/all_gather | solution.py:140
  262.8 39.2 %fusion.185 = (f32[1024]{0:T(1024)S(1)}, f32[1024,768]{1,0:T(8,128)S(1)}) fusion(f32[768]{0:T(1024)S(1)} %get-tuple-element.104, bf16[3072,768]{1,0:T(8,128)(2,1)} %all-gather.12.cloned.1.call-done, f32[3072]{0:T(1024)S(1)} %add.229, bf16[768,3072]{1,0:T(8,128)(2,1)} %all-gather.10.cloned.1.call-done, f32[1024,768]{1,0:T(8,128)} %subtract_multiply_fusion.3, ...), kind=kOutput, calls=%fused_computation.267 | convolution fusion | flops 9877584896 | bytes 15754240 | tf_op jit(solution)/shard_map/dot_general | solution.py:157
  310.0 3.7 multiply_reduce_fusion.3
  313.7 2.9 fusion.178
  316.5 33.4 %fusion.6 = (f32[1024,3072]{1,0:T(8,128)}, f32[1024,3072]{1,0:T(8,128)}) fusion(f32[3072]{0:T(1024)S(1)} %add.229, bf16[768,3072]{1,0:T(8,128)(2,1)} %all-gather.10.cloned.1.call-done, f32[1024,768]{1,0:T(8,128)S(1)} %copy-done.9, f32[768]{0:T(1024)S(1)} %get-tuple-element.105, f32[768]{0:T(1024)S(1)} %get-tuple-element.106), kind=kOutput, calls=%fused_computation.8 | convolution fusion | flops 5032378368 | bytes 33048576 | tf_op jit(solution)/shard_map/dot_general | solution.py:189
  349.9 18.9 %fusion.191 = (f32[3072]{0:T(1024)S(1)}, bf16[1024,3072]{1,0:T(8,128)(2,1)}) fusion(f32[1024,3072]{1,0:T(8,128)} %get-tuple-element.156, bf16[3072,768]{1,0:T(8,128)(2,1)} %all-gather.12.cloned.1.call-done, f32[1024,768]{1,0:T(8,128)} %get-tuple-element.132, f32[1024,3072]{1,0:T(8,128)} %get-tuple-element.157, f32[3072]{0:T(1024)S(1)} %add.229), kind=kOutput, calls=%fused_computation.269 | convolution fusion | flops 4882953216 | bytes 39346176 | tf_op jit(solution)/shard_map/dot_general | solution.py:43
  368.8 11.5 multiply_reduce_fusion.4
  380.4 5.4 add_convert_fusion
  385.8 6.6 copy.130
  392.5 3.6 copy.167
  397.6 5.9 fusion.188
  404.5 2.2 copy-done.5
  411.7 2.8 fusion.72
  414.6 4.8 convolution_convert_fusion.1
  419.4 2.8 copy.133
  425.2 5.1 fusion.93
  430.3 11.4 fusion.86
  441.7 11.1 bitcast_reduce_fusion.1
  454.4 5.3 bitcast_reduce_fusion
  460.6 9.3 copy.140
  469.8 2.2 copy-done.8
  472.1 5.9 convolution_bitcast_fusion
  477.9 8.0 copy.149
  487.9 10.5 fusion.46
  500.3 20.7 %fusion.19 = f32[3072,768]{1,0:T(8,128)} fusion(f32[1024,3072]{1,0:T(8,128)} %get-tuple-element.156, f32[1024,3072]{1,0:T(8,128)} %get-tuple-element.157, f32[3072]{0:T(1024)S(1)} %add.229, f32[1024,768]{1,0:T(8,128)S(1)} %copy-done.14), kind=kOutput, calls=%fused_computation.41 | convolution fusion | flops 4845207552 | bytes 37761024 | tf_op jit(solution)/shard_map/dot_general | solution.py:37
  522.8 19.0 %reduce-scatter.17.cloned.1.call-done = f32[48,768]{1,0:T(8,128)} async-done(((f32[768,768]{1,0:T(8,128)}), f32[48,768]{1,0:T(8,128)}) %reduce-scatter.17.cloned.1.call-update) | async-done | bytes 147472 | tf_op jit(solution)/shard_map/reduce_scatter | solution.py:254
  543.4 154.8 %reduce-scatter.29.cloned.1.call-done = f32[48,2304]{1,0:T(8,128)} async-done(((f32[768,2304]{1,0:T(8,128)}), f32[48,2304]{1,0:T(8,128)}) %reduce-scatter.29.cloned.1.call-update) | async-done | bytes 442384
  702.4 172.5 %reduce-scatter.21.cloned.1.call-done = f32[48,3072]{1,0:T(8,128)} async-done(((f32[768,3072]{1,0:T(8,128)}), f32[48,3072]{1,0:T(8,128)}) %reduce-scatter.21.cloned.1.call-update) | async-done | bytes 589840 | tf_op jit(solution)/shard_map/reduce_scatter | solution.py:255
  878.0 172.5 %reduce-scatter.25.cloned.1.call-done = f32[192,768]{1,0:T(8,128)} async-done(((f32[3072,768]{1,0:T(8,128)}), f32[192,768]{1,0:T(8,128)}) %reduce-scatter.25.cloned.1.call-update) | async-done | bytes 589840 | tf_op jit(solution)/shard_map/reduce_scatter | solution.py:256
  1052.4 9.0 fusion.61
  1061.4 115.1 %reduce-scatter.33.cloned.1.call-done = f32[48,12]{1,0:T(8,128)} async-done(((f32[768,12]{1,0:T(8,128)}), f32[48,12]{1,0:T(8,128)}) %reduce-scatter.33.cloned.1.call-update) | async-done | bytes 2320
  1177.3 2.5 all-reduce
  1180.4 5.2 reduce-scatter.19.cloned.1.call-done
  1187.0 10.2 reduce-scatter.31.cloned.1.call-done
  1200.2 8.6 reduce-scatter.23.cloned.1.call-done
  1211.0 9.4 reduce-scatter.27.cloned.1.call-done
  1223.3 40.8 %all-reduce.1 = (f32[]{:T(128)}, f32[]{:T(128)}) all-reduce(f32[]{:T(128)S(6)} %reduce_sum.321, f32[]{:T(128)} %get-tuple-element.141), channel_id=1, replica_groups=mesh['dp'=16,'pair'=2] {'dp','pair'}, use_global_device_ids=true, to_apply=%region_42.43 | all-reduce | flops 2 | bytes 16 | tf_op jit(solution)/shard_map/psum | solution.py:277
  1266.3 2.2 multiply_subtract_fusion
  1268.5 2.3 multiply_subtract_fusion.1
  (195 shorter events, 65.1 us)
Async XLA Ops:
  7.2 67.3 %all-gather.6.cloned.1.call-start = ((), (), s32[]{:S(2)}) async-start(), calls=%async_computation.9 | async-start | bytes 3649536 | tf_op jit(solution)/shard_map/all_gather | solution.py:137
  8.9 122.0 %all-gather.8.cloned.1.call-start = ((), (), s32[]{:S(2)}) async-start(), calls=%async_computation.10 | async-start | bytes 1216512 | tf_op jit(solution)/shard_map/all_gather | solution.py:138
  10.4 186.5 %all-gather.10.cloned.1.call-start = ((), (), s32[]{:S(2)}) async-start(), calls=%async_computation.11 | async-start | bytes 4866048 | tf_op jit(solution)/shard_map/all_gather | solution.py:139
  12.2 250.6 %all-gather.12.cloned.1.call-start = ((), (), s32[]{:S(2)}) async-start(), calls=%async_computation.12 | async-start | bytes 4866048 | tf_op jit(solution)/shard_map/all_gather | solution.py:140
  13.9 527.9 %reduce-scatter.17.cloned.1.call-start = ((), (), s32[]{:S(2)}) async-start(), calls=%async_computation.13 | async-start | bytes 2506752 | tf_op jit(solution)/shard_map/reduce_scatter | solution.py:254
  62.9 20.0 %copy-start.33 = (f32[2304]{0:T(1024)}, f32[2304]{0:T(1024)S(1)}, u32[]{:S(2)}) copy-start(f32[2304]{0:T(1024)S(1)} %pad_maximum_fusion.1) | copy-start | bytes 27652
  100.4 30.4 %copy-start.38 = (bf16[1024,768]{1,0:T(8,128)(2,1)S(1)}, bf16[1024,768]{1,0:T(8,128)(2,1)}, u32[]{:S(2)}) copy-start(bf16[1024,768]{1,0:T(8,128)(2,1)} %param.21) | copy-start | bytes 4718596
  302.0 3.8 copy-start.18
  303.1 4.8 copy-start.16
  303.1 1.2 collective-permute-start
  305.5 2.4 collective-permute-start.1
  310.0 3.7 copy-start.1
  313.7 2.9 copy-start.9
  349.9 18.9 %copy-start.10 = (f32[1024,768]{1,0:T(8,128)S(1)}, f32[1024,768]{1,0:T(8,128)}, u32[]{:S(2)}) copy-start(f32[1024,768]{1,0:T(8,128)} %subtract_multiply_fusion.3) | copy-start | bytes 9437188
  368.8 11.6 copy-start.34
  368.8 11.6 copy-start.37
  368.8 11.6 copy-start.39
  396.5 7.0 copy-start.4
  403.5 3.2 copy-start.5
  403.5 4.4 copy-start.15
  403.5 4.4 copy-start.26
  403.6 4.4 copy-start.28
  406.7 2.2 copy-start.3
  414.5 283.7 %reduce-scatter.29.cloned.1.call-start = ((), (), s32[]{:S(2)}) async-start(), calls=%async_computation.19 | async-start | bytes 7520256
  441.7 12.7 copy-start.7
  454.4 5.5 copy-start.17
  460.6 11.5 copy-start.40
  469.8 2.3 copy-start.8
  486.0 1.9 copy-start.11
  486.0 388.8 %reduce-scatter.21.cloned.1.call-start = ((), (), s32[]{:S(2)}) async-start(), calls=%async_computation.15 | async-start | bytes 10027008 | tf_op jit(solution)/shard_map/reduce_scatter | solution.py:255
  498.4 1.9 copy-start.14
  498.4 552.0 %reduce-scatter.25.cloned.1.call-start = ((), (), s32[]{:S(2)}) async-start(), calls=%async_computation.17 | async-start | bytes 10027008 | tf_op jit(solution)/shard_map/reduce_scatter | solution.py:256
  521.0 355.8 %copy-start.41 = (u32[32]{0:T(128)S(1)}, u32[32]{0:T(128)}, u32[]{:S(2)}) copy-start(u32[32]{0:T(128)} %constant.217) | copy-start | bytes 388
  521.0 531.3 %copy-start.13 = (f32[1024,768]{1,0:T(8,128)S(1)}, f32[1024,768]{1,0:T(8,128)}, u32[]{:S(2)}) copy-start(f32[1024,768]{1,0:T(8,128)} %copy-done.12) | copy-start | bytes 9437188
  521.0 655.5 %reduce-scatter.33.cloned.1.call-start = ((), (), s32[]{:S(2)}) async-start(), calls=%async_computation.21 | async-start | bytes 417792
  522.7 662.9 %reduce-scatter.19.cloned.1.call-start = ((), (), s32[]{:S(2)}) async-start(), calls=%async_computation.14 | async-start | bytes 110592 | tf_op jit(solution)/shard_map/reduce_scatter | solution.py:263
  543.4 653.9 %reduce-scatter.31.cloned.1.call-start = ((), (), s32[]{:S(2)}) async-start(), calls=%async_computation.20 | async-start | bytes 331776 | tf_op jit(solution)/shard_map/reduce_scatter | solution.py:260
  702.3 506.4 %reduce-scatter.23.cloned.1.call-start = ((), (), s32[]{:S(2)}) async-start(), calls=%async_computation.16 | async-start | bytes 442368 | tf_op jit(solution)/shard_map/reduce_scatter | solution.py:266
  876.7 343.8 %reduce-scatter.27.cloned.1.call-start = ((), (), s32[]{:S(2)}) async-start(), calls=%async_computation.18 | async-start | bytes 442368 | tf_op jit(solution)/shard_map/reduce_scatter | solution.py:269
  1052.3 213.2 %copy-start.29 = (f32[12,24]{1,0:T(8,128)S(1)}, f32[12,24]{1,0:T(8,128)}, u32[]{:S(2)}) copy-start(f32[12,24]{1,0:T(8,128)} %param.29) | copy-start | bytes 3460
  1052.3 213.2 %copy-start.35 = (f32[12,24]{1,0:T(8,128)S(1)}, f32[12,24]{1,0:T(8,128)}, u32[]{:S(2)}) copy-start(f32[12,24]{1,0:T(8,128)} %param.34) | copy-start | bytes 3460
  1052.3 213.2 %copy-start.36 = (f32[12,24]{1,0:T(8,128)S(1)}, f32[12,24]{1,0:T(8,128)}, u32[]{:S(2)}) copy-start(f32[12,24]{1,0:T(8,128)} %param.39) | copy-start | bytes 3460
  1052.3 213.9 %copy-start.19 = (f32[96,768]{1,0:T(8,128)S(1)}, f32[96,768]{1,0:T(8,128)}, u32[]{:S(2)}) copy-start(f32[96,768]{1,0:T(8,128)} %param.28) | copy-start | bytes 884740
  1052.4 218.4 %copy-start.22 = (f32[24,768]{1,0:T(8,128)S(1)}, f32[24,768]{1,0:T(8,128)}, u32[]{:S(2)}) copy-start(f32[24,768]{1,0:T(8,128)} %param.26) | copy-start | bytes 221188
  1061.4 211.0 %copy-start.20 = (f32[24,2304]{1,0:T(8,128)S(1)}, f32[24,2304]{1,0:T(8,128)}, u32[]{:S(2)}) copy-start(f32[24,2304]{1,0:T(8,128)} %param.25) | copy-start | bytes 663556
  1061.4 211.0 %copy-start.23 = (f32[24,2304]{1,0:T(8,128)S(1)}, f32[24,2304]{1,0:T(8,128)}, u32[]{:S(2)}) copy-start(f32[24,2304]{1,0:T(8,128)} %param.30) | copy-start | bytes 663556
  1061.4 211.0 %copy-start.24 = (f32[24,2304]{1,0:T(8,128)S(1)}, f32[24,2304]{1,0:T(8,128)}, u32[]{:S(2)}) copy-start(f32[24,2304]{1,0:T(8,128)} %param.35) | copy-start | bytes 663556
  1197.3 75.1 %copy-start.21 = (bf16[24,2304]{1,0:T(8,128)(2,1)S(1)}, bf16[24,2304]{1,0:T(8,128)(2,1)}, u32[]{:S(2)}) copy-start(bf16[24,2304]{1,0:T(8,128)(2,1)} %reduce-scatter.31.cloned.1.call-done) | copy-start | bytes 331780
  (9 other events, 10.6 us)
Sparse Core Ops, SparseCore 0:
  11.5 62.9 all-gather.5
  77.9 52.8 all-gather.7
  134.3 62.5 all-gather.9
  200.3 62.4 all-gather.11
  414.7 127.0 reduce-scatter.16
  547.8 150.3 reduce-scatter.28
  704.9 169.9 reduce-scatter.20
  880.5 169.9 reduce-scatter.24
  1055.8 120.6 reduce-scatter.32
  1179.1 6.4 reduce-scatter.18
  1188.4 8.7 reduce-scatter.30
  1199.9 8.8 reduce-scatter.22
  1211.6 8.8 reduce-scatter.26
where the time goes:
time: 1290 us; the launch traced here: 1280 us
  waiting for transfers between devices  832 us (64%)
  matrix products  211 us (16%)
  blocking collectives  87.1 us (7%)
  local copies, waits for them, and re-layouts  73.4 us (6%)
  other arithmetic  52.6 us (4%)
  between operations  25.2 us (2%)
    unnamed x15, waiting for transfers between devices  270 us
    reduce_scatter x1, waiting for transfers between devices, body(): lax.psum_scatter(gradients[3], 'dp', scatter_dimension=0, tiled=True)  172 us
    reduce_scatter x1, waiting for transfers between devices, body(): lax.psum_scatter(gradients[2], 'dp', scatter_dimension=0, tiled=True)  172 us
    all_gather x1, waiting for transfers between devices, body(): lax.all_gather(outer_weight.astype(jnp.bfloat16), ('dp', 'pair'), axis=0,...  65.8 us
    all_gather x1, waiting for transfers between devices, body(): lax.all_gather(inner_weight.astype(jnp.bfloat16), ('dp', 'pair'), axis=0,...  58.8 us
    dot_general x4, matrix products, contract_cols(): lax.dot_general(left, right, (((1,), (1,)), ((), ())), preferred_element_...  44.3 us
    all_gather x1, blocking collectives, body(): lax.all_gather(affine_params.astype(jnp.bfloat16), ('dp', 'pair'), axis=1...  43.8 us
    psum x1, blocking collectives, body(): totals = lax.psum((local_squares, loss_part), ('dp', 'pair'))  40.8 us
  transfers between devices with their start and end apart: 15, of which 14 were waited for; matrix products, arithmetic and copies ran while one was open for 13% of the time, Pallas kernels for 0%

commit v1 on v0

--- a/solution.py
+++ b/solution.py
@@ -3,12 +3,16 @@
 import jax
 import jax.numpy as jnp
 from jax import lax
+from jax.experimental import pallas as pl
+from jax.experimental.pallas import tpu as pltpu
 from jax.sharding import PartitionSpec as P
 
 HEADS = 12
 HD = 64
 L = 128
 STEP = 10
+LANES = 128
+AXES = ("dp", "pair")
 
 
 LN_EPS = 1e-12
@@ -22,15 +26,225 @@
 RATE_AFFINE = 0.8
 DECAY_AFFINE = 0.0
 
-
-def swapped(block, axis, bit):
-    count = lax.axis_size(axis)
-    route = []
-    for low in range(count):
-        high = low | 1 << bit
-        if high != low and high < count:
-            route += [(low, high), (high, low)]
-    return lax.ppermute(block, axis, route)
+BF16 = jnp.bfloat16
+F32 = jnp.float32
+
+
+def flip_steps(chips):
+    bits = chips.bit_length() - 1
+    if bits == 4:
+        return ((2, 3), (3, 2), (0, 1), (1, 0))
+    return tuple((bit, bit) for bit in reversed(range(bits)))
+
+
+def flip_route(chips, pair_of_bits):
+    return [
+        (2 * d + c, 2 * (d ^ (1 << pair_of_bits[c])) + c) for d in range(chips) for c in range(2)
+    ]
+
+
+def core_route(chips):
+    return [(2 * d + c, 2 * d + 1 - c) for d in range(chips) for c in range(2)]
+
+
+def flipped(block, bits):
+    chips = lax.axis_size("dp")
+    return lax.ppermute(block, AXES, flip_route(chips, bits))
+
+
+def core_swapped(block):
+    return lax.ppermute(block, AXES, core_route(lax.axis_size("dp")))
+
+
+def block_order():
+    chips = lax.axis_size("dp")
+    d, c = lax.axis_index("dp"), lax.axis_index("pair")
+    steps = flip_steps(chips)
+    rows = []
+    for core in range(2):
+        rows.append(
+            jnp.array(
+                [
+                    sum((place >> k & 1) << steps[k][core] for k in range(len(steps)))
+                    for place in range(chips)
+                ],
+                jnp.int32,
+            )
+            ^ d
+        )
+    own = jnp.where(c == 0, rows[0], rows[1])
+    other = jnp.where(c == 0, rows[1], rows[0])
+    return jnp.stack([own, other, jnp.full((chips,), c, jnp.int32)])
+
+
+def pick(core, first, second):
+    return jnp.where(core == 0, first, second)
+
+
+def halves_of(low, pieces):
+    core = lax.axis_index("pair")
+    first, second, at = [], [], 0
+    for width in pieces:
+        first.append(low[:, at : at + width])
+        second.append(low[:, at + width : at + 2 * width])
+        at += 2 * width
+    first, second = jnp.concatenate(first, 1), jnp.concatenate(second, 1)
+    return pick(core, first, second), pick(core, second, first)
+
+
+def chip_rows(low, pieces, extra=None):
+    core = lax.axis_index("pair")
+    own, other = halves_of(low, pieces)
+    if extra is not None:
+        own, other = (jnp.concatenate([half, extra], 1) for half in (own, other))
+    got = core_swapped(other)
+    return pick(core, jnp.concatenate([own, got]), jnp.concatenate([got, own]))
+
+
+def shard_of(half_rows, pieces, core):
+    rows = half_rows.shape[0] // 2
+    first, second = half_rows[:rows], half_rows[rows:]
+    own = pick(core, first, second)
+    got = core_swapped(pick(core, second, first).astype(BF16)).astype(F32)
+    low, high = pick(core, own, got), pick(core, got, own)
+    out, at = [], 0
+    for width in pieces:
+        out += [low[:, at : at + width], high[:, at : at + width]]
+        at += width
+    return jnp.concatenate(out, 1)
+
+
+def gather_blocks(block):
+    held = block[None]
+    for bits in flip_steps(lax.axis_size("dp")):
+        held = jnp.concatenate([held, flipped(held, bits)], axis=0)
+    return held, core_swapped(held)
+
+
+def reduce_blocks(own, other):
+    parts = [own, core_swapped(other)]
+    count = own.shape[0]
+    for bits in reversed(flip_steps(lax.axis_size("dp"))):
+        count //= 2
+        sent = sum(p[count : 2 * count].astype(F32) for p in parts).astype(BF16)
+        parts = parts + [flipped(sent, bits)]
+        parts = [p[:count] for p in parts]
+    return sum(p[0].astype(F32) for p in parts)
+
+
+def total_over_devices(value):
+    chips = lax.axis_size("dp")
+    value = value + core_swapped(value)
+    for bit in range(chips.bit_length() - 1):
+        value = value + flipped(value, (bit, bit))
+    return value
+
+
+def moved(order, own, other, whole_shapes, pieces):
+    chips, rows, _ = own.shape
+    if rows % 16:
+        core = order[2, 0]
+        lined = [
+            jnp.zeros(ref.shape, BF16).at[order[side]].set(ref).reshape(chips * rows, -1)
+            for side, ref in enumerate((own, other))
+        ]
+        low, high = pick(core, lined[0], lined[1]), pick(core, lined[1], lined[0])
+        return tuple(
+            jnp.concatenate(
+                [
+                    ref[:, lane : lane + width]
+                    for at, _, width, lane in pieces
+                    if at == whole
+                    for ref in (low, high)
+                ],
+                axis=1,
+            )
+            for whole in range(len(whole_shapes))
+        )
+
+    def kernel(order_ref, own_ref, other_ref, *rest):
+        wholes, sems = rest[:-1], rest[-1]
+        core = order_ref[2, 0]
+        copies = []
+        for side, ref in enumerate((own_ref, other_ref)):
+            half = core if side == 0 else 1 - core
+            for place in range(chips):
+                row = pl.multiple_of(order_ref[side, place] * rows, rows)
+                for whole, start, width, lane in pieces:
+                    col = pl.multiple_of(start + half * width, LANES)
+                    copies.append(
+                        pltpu.make_async_copy(
+                            ref.at[place, :, pl.ds(lane, width)],
+                            wholes[whole].at[pl.ds(row, rows), pl.ds(col, width)],
+                            sems.at[len(copies)],
+                        )
+                    )
+        for copy in copies:
+            copy.start()
+        for copy in copies:
+            copy.wait()
+
+    return pl.pallas_call(
+        kernel,
+        out_shape=tuple(jax.ShapeDtypeStruct(s, BF16) for s in whole_shapes),
+        in_specs=[
+            pl.BlockSpec(memory_space=pltpu.SMEM),
+            pl.BlockSpec(memory_space=pl.ANY),
+            pl.BlockSpec(memory_space=pl.ANY),
+        ],
+        out_specs=tuple(pl.BlockSpec(memory_space=pltpu.VMEM) for _ in whole_shapes),
+        scratch_shapes=[pltpu.SemaphoreType.DMA((2 * chips * len(pieces),))],
+    )(order, own, other)
+
+
+def parted(order, wholes, rows, cols, pieces):
+    chips = order.shape[1]
+    if rows % 16:
+        core = order[2, 0]
+        low, high = (
+            jnp.concatenate(
+                [
+                    wholes[at][:, start + half * width : start + (half + 1) * width]
+                    for at, start, width, _ in pieces
+                ],
+                axis=1,
+            ).reshape(chips, rows, cols)
+            for half in range(2)
+        )
+        own, other = pick(core, low, high), pick(core, high, low)
+        return own[order[0]], other[order[1]]
+    shape = jax.ShapeDtypeStruct((chips, rows, cols), BF16)
+
+    def kernel(order_ref, *rest):
+        wholes, (own_ref, other_ref, sems) = rest[:-3], rest[-3:]
+        core = order_ref[2, 0]
+        copies = []
+        for side, ref in enumerate((own_ref, other_ref)):
+            half = core if side == 0 else 1 - core
+            for place in range(chips):
+                row = pl.multiple_of(order_ref[side, place] * rows, rows)
+                for whole, start, width, lane in pieces:
+                    col = pl.multiple_of(start + half * width, LANES)
+                    copies.append(
+                        pltpu.make_async_copy(
+                            wholes[whole].at[pl.ds(row, rows), pl.ds(col, width)],
+                            ref.at[place, :, pl.ds(lane, width)],
+                            sems.at[len(copies)],
+                        )
+                    )
+        for copy in copies:
+            copy.start()
+        for copy in copies:
+            copy.wait()
+
+    return pl.pallas_call(
+        kernel,
+        out_shape=(shape, shape),
+        in_specs=[pl.BlockSpec(memory_space=pltpu.SMEM)]
+        + [pl.BlockSpec(memory_space=pltpu.VMEM) for _ in wholes],
+        out_specs=(pl.BlockSpec(memory_space=pl.ANY), pl.BlockSpec(memory_space=pl.ANY)),
+        scratch_shapes=[pltpu.SemaphoreType.DMA((2 * chips * len(pieces),))],
+    )(order, *wholes)
 
 
 def contract_rows(left, right):
@@ -133,16 +347,31 @@
 ):
     rows, width = tokens.shape
     spans = rows // L
-    gathered = (
-        lax.all_gather(qkv_weight.astype(jnp.bfloat16), ("dp", "pair"), axis=0, tiled=True),
-        lax.all_gather(proj_weight.astype(jnp.bfloat16), ("dp", "pair"), axis=0, tiled=True),
-        lax.all_gather(inner_weight.astype(jnp.bfloat16), ("dp", "pair"), axis=0, tiled=True),
-        lax.all_gather(outer_weight.astype(jnp.bfloat16), ("dp", "pair"), axis=0, tiled=True),
-        lax.all_gather(affine_params.astype(jnp.bfloat16), ("dp", "pair"), axis=1, tiled=True),
-    )
-    qkv_w, proj_w, inner_w, outer_w, affine_low = gathered
-    affine = affine_low.astype(jnp.float32)
-    hidden = inner_w.shape[1]
+    half = width // 2
+    order = block_order()
+    hidden = inner_weight.shape[1]
+    affine_cols = jnp.pad(affine_params.astype(BF16).T, ((0, 0), (0, LANES - affine_params.shape[0])))
+    block_one = chip_rows(qkv_weight.astype(BF16), (half, half, half), affine_cols)
+    block_two = chip_rows(
+        jnp.concatenate([proj_weight.astype(BF16), inner_weight.astype(BF16)], 1), (half, hidden // 2)
+    )
+    block_three = chip_rows(outer_weight.astype(BF16), (half,))
+    qkv_pieces = tuple((0, width * k, half, half * k) for k in range(3))
+    two_pieces = ((0, 0, half, 0), (1, 0, hidden // 2, half))
+    outer_pieces = ((0, 0, half, 0),)
+    own_one, other_one = gather_blocks(block_one)
+    own_two, other_two = gather_blocks(block_two)
+    own_three, other_three = gather_blocks(block_three)
+    qkv_w, = moved(order, own_one, other_one, ((width, 3 * width),), qkv_pieces)
+    affine = (
+        jnp.zeros(own_one.shape[:2] + (LANES,), BF16)
+        .at[order[0]]
+        .set(own_one[:, :, 3 * half :])
+        .reshape(width, LANES)
+        .T.astype(F32)
+    )
+    proj_w, inner_w = moved(order, own_two, other_two, ((width, width), (width, hidden)), two_pieces)
+    outer_w, = moved(order, own_three, other_three, ((hidden, width),), outer_pieces)
     gain_one, shift_one, gain_two, shift_two = (affine[0], affine[1], affine[2], affine[3])
     bias_query, bias_value, bias_proj, bias_outer = (affine[4], affine[5], affine[6], affine[7])
     bias_inner = affine[8:12].reshape(hidden)
@@ -167,7 +396,7 @@
     slot_index = jnp.arange(spans)
     own_live = slot_index < own_count
     other_live = slot_index < other_count
-    partner_cls = swapped(cls_rows, "pair", 0)
+    partner_cls = core_swapped(cls_rows)
 
     def contrast_local(anchor, keys_side):
         return contrast(anchor, keys_side, own_ids, other_ids, own_live, other_live)
@@ -176,18 +405,11 @@
         contrast_local, cls_rows.astype(jnp.float32), partner_cls.astype(jnp.float32)
     )
     grad_own, grad_other = pull_back(jnp.asarray(LOSS_WEIGHT, jnp.float32))
-    grad_returned = swapped(grad_other, "pair", 0)
+    grad_returned = core_swapped(grad_other)
     grad_cls = grad_own + grad_returned
     row_live = jnp.repeat(own_live, L).astype(jnp.float32)
     upstream = mlm_grad.astype(jnp.float32) * row_live[:, None]
     upstream = upstream.reshape(spans, L, width).at[:, 0, :].add(grad_cls).reshape(rows, width)
-    tokens_again, normed_again, upstream = lax.optimization_barrier((tokens, normed_one, upstream))
-    queries, key_rows, values, attention, attention_low, context = attend(
-        tokens_again, qkv_w, qkv_bias
-    )
-    skip_low = (normed_again * gain_one + shift_one).astype(jnp.bfloat16)
-    inner_pre = jnp.dot(skip_low, inner_w, preferred_element_type=jnp.float32) + bias_inner
-    activated = jax.nn.gelu(inner_pre, approximate=False).astype(jnp.bfloat16)
     gain_two_grad = jnp.sum(upstream * normed_two, axis=0)
     shift_two_grad = jnp.sum(upstream, axis=0)
     grad_two = normalize_back(upstream, normed_two, inv_two, gain_two)
@@ -248,36 +470,37 @@
         ],
         axis=0,
     )
-    gradients = (qkv_grad, proj_grad, inner_grad, outer_grad, affine_grad)
-    summed = (
-        lax.psum_scatter(gradients[0], "dp", scatter_dimension=0, tiled=True),
-        lax.psum_scatter(gradients[1], "dp", scatter_dimension=0, tiled=True),
-        lax.psum_scatter(gradients[2], "dp", scatter_dimension=0, tiled=True),
-        lax.psum_scatter(gradients[3], "dp", scatter_dimension=0, tiled=True),
-        lax.psum_scatter(gradients[4], "dp", scatter_dimension=1, tiled=True),
-    )
+    rows_chip = block_one.shape[0]
+    own, other = parted(order, (outer_grad.astype(BF16),), outer_weight.shape[0] * 2, half, outer_pieces)
+    sum_outer = reduce_blocks(own, other)
+    own, other = parted(order, (inner_grad.astype(BF16),), rows_chip, hidden // 2, ((0, 0, hidden // 2, 0),))
+    sum_inner = reduce_blocks(own, other)
+    own, other = parted(
+        order,
+        (proj_grad.astype(BF16), qkv_grad.astype(BF16)),
+        rows_chip,
+        4 * half,
+        ((0, 0, half, 0),) + tuple((1, width * k, half, half * (k + 1)) for k in range(3)),
+    )
+    sum_rest = reduce_blocks(own, other)
+    spread = jnp.pad(affine_grad, ((0, LANES - affine_grad.shape[0]), (0, 0))).T.astype(BF16)
+    spread = spread.reshape(-1, rows_chip, LANES)
+    sum_affine = reduce_blocks(spread[order[0]], spread[order[1]])
+    rest = shard_of(sum_rest, (half, half, half, half), side)
+    rows_own = qkv_weight.shape[0]
+    affine_shard = lax.dynamic_slice_in_dim(sum_affine, side * rows_own, rows_own).T[: affine_params.shape[0]]
     shards = (
-        lax.psum_scatter(
-            summed[0].astype(jnp.bfloat16), "pair", scatter_dimension=0, tiled=True
-        ).astype(jnp.float32),
-        lax.psum_scatter(
-            summed[1].astype(jnp.bfloat16), "pair", scatter_dimension=0, tiled=True
-        ).astype(jnp.float32),
-        lax.psum_scatter(
-            summed[2].astype(jnp.bfloat16), "pair", scatter_dimension=0, tiled=True
-        ).astype(jnp.float32),
-        lax.psum_scatter(
-            summed[3].astype(jnp.bfloat16), "pair", scatter_dimension=0, tiled=True
-        ).astype(jnp.float32),
-        lax.psum_scatter(
-            summed[4].astype(jnp.bfloat16), "pair", scatter_dimension=1, tiled=True
-        ).astype(jnp.float32),
+        rest[:, width:],
+        rest[:, :width],
+        shard_of(sum_inner, (hidden // 2,), side),
+        shard_of(sum_outer, (half,), side),
+        affine_shard,
     )
     local_squares = jnp.sum(jnp.stack([jnp.sum(shard_item * shard_item) for shard_item in shards]))
-    totals = lax.psum((local_squares, loss_part), ("dp", "pair"))
-    grad_norm = jnp.sqrt(totals[0])
+    totals = total_over_devices(jnp.stack([local_squares, loss_part])[:, None] * jnp.ones((1, LANES), F32))
+    grad_norm = jnp.sqrt(totals[0, 0])
     factor = jnp.minimum(1.0, CLIP_NORM / (grad_norm + 1e-06))
-    mean_loss = totals[1] / (spans * lax.axis_size("dp") * lax.axis_size("pair"))
+    mean_loss = totals[1, 0] / (spans * lax.axis_size("dp") * lax.axis_size("pair"))
     masters = (qkv_weight, proj_weight, inner_weight, outer_weight, affine_params)
     moments = (qkv_moment, proj_moment, inner_moment, outer_moment, affine_moment)
     squares_old = (qkv_square, proj_square, inner_square, outer_square, affine_square)

time: 1290 us -> 504 us (0.39)
  waiting for transfers between devices: 832 us -> 90.7 us
  starting transfers between devices: 1.15 us -> 90.1 us
  blocking collectives: 87.1 us -> 0 us
  matrix products: 211 us -> 156 us
  Pallas kernels: 0 us -> 33.1 us
  local copies, waits for them, and re-layouts: 73.4 us -> 54.5 us
  between operations: 25.2 us -> 11.7 us
    reduce_scatter x7 -> x0, waiting for transfers between devices: 397 us -> none  [the longest x1 172 us: body(): lax.psum_scatter(gradients[3], 'dp', scatter_dimension=0, tiled=True)]
    unnamed x15 -> x0, waiting for transfers between devices: 270 us -> none
    all_gather x4 -> x0, waiting for transfers between devices: 164 us -> none  [the longest x1 65.8 us: body(): lax.all_gather(outer_weight.astype(jnp.bfloat16), ('dp', 'pair'), axis=0,...]
    ppermute x2 -> x48, waiting for transfers between devices: 0.82 us -> 90.7 us  [the longest x32 85.5 us: flipped(): return lax.ppermute(block, AXES, flip_route(chips, bits))]
    ppermute x2 -> x48, starting transfers between devices: 0.61 us -> 90.1 us  [the longest x32 85.9 us: flipped(): return lax.ppermute(block, AXES, flip_route(chips, bits))]
    all_gather x1 -> x0, blocking collectives: 43.8 us -> none  [body(): lax.all_gather(affine_params.astype(jnp.bfloat16), ('dp', 'pair'), axis=1...]
    psum x1 -> x0, blocking collectives: 40.8 us -> none  [body(): totals = lax.psum((local_squares, loss_part), ('dp', 'pair'))]
    dot_general x1, matrix products: 39.2 us -> 5.46 us  [body(): jnp.dot(activated, outer_w, preferred_element_type=jnp.float32) + bias_outer]
  transfers between devices with their start and end apart: 15 -> 48, of which waited for: 14 -> 19; matrix products, arithmetic and copies ran while one was open for 13% -> 20% of each run, Pallas kernels for 0% -> 4%
where the time goes in v1:
time: 504 us; the launch traced here: 499 us
  matrix products  156 us (31%)
  waiting for transfers between devices  90.7 us (18%)
  starting transfers between devices  90.1 us (18%)
  other arithmetic  63.5 us (13%)
  local copies, waits for them, and re-layouts  54.5 us (11%)
  Pallas kernels  33.1 us (7%)
  between operations  11.7 us (2%)
    ppermute x32, starting transfers between devices, flipped(): return lax.ppermute(block, AXES, flip_route(chips, bits))  85.9 us
    ppermute x32, waiting for transfers between devices, flipped(): return lax.ppermute(block, AXES, flip_route(chips, bits))  85.5 us
    dot_general x4, matrix products, contract_cols(): lax.dot_general(left, right, (((1,), (1,)), ((), ())), preferred_element_...  39.7 us
    dot_general x1, matrix products, body(): jnp.dot(skip_low, inner_w, preferred_element_type=jnp.float32) + bias_inner  35.5 us
    dot_general x4, matrix products, contract_rows(): lax.dot_general(left, right, (((0,), (0,)), ((), ())), preferred_element_...  28.4 us
    convert_element_type x16, other arithmetic, reduce_blocks(): sent = sum((p[count:2 * count].astype(F32) for p in parts)).astype(BF16)  20.3 us
    unnamed x150, local copies, waits for them, and re-layouts  18 us
    pallas_call x3, Pallas kernels, moved(): pl.pallas_call(kernel, out_shape=tuple((jax.ShapeDtypeStruct(s, BF16) for...  17.7 us
  transfers between devices with their start and end apart: 48, of which 19 were waited for; matrix products, arithmetic and copies ran while one was open for 20% of the time, Pallas kernels for 4%

profile of v1, /device:TPU:0, one launch (start us, length us, event | category | flops | bytes accessed | tf_op | source)
XLA Modules:
  0.0 499.2 jit_solution(3691723296862788292)
XLA Ops:
  11.3 2.6 collective-permute-start.1
  17.9 2.7 collective-permute-start.2
  23.4 6.2 %collective-permute-done.2 = bf16[2,48,1280]{2,1,0:T(8,128)(2,1)S(1)} collective-permute-done((bf16[2,48,1280]{2,1,0:T(8,128)(2,1)S(1)}, bf16[2,48,1280]{2,1,0:T(8,128)(2,1)S(1)}, u32[]{:S(2)}, u32[]{:S(2)}) %collective-permute-start.2) | collective-permute-done | bytes 245792 | tf_op jit(solution)/shard_map/ppermute | solution.py:52
  29.7 3.9 collective-permute-start.3
  35.1 3.0 collective-permute-start.8
  38.1 4.3 collective-permute-done.3
  42.5 2.6 collective-permute-start.4
  45.1 8.0 %collective-permute-done.8 = bf16[2,48,1920]{2,1,0:T(8,128)(2,1)S(1)} collective-permute-done((bf16[2,48,1920]{2,1,0:T(8,128)(2,1)S(1)}, bf16[2,48,1920]{2,1,0:T(8,128)(2,1)S(1)}, u32[]{:S(2)}, u32[]{:S(2)}) %collective-permute-start.8) | collective-permute-done | bytes 368672 | tf_op jit(solution)/shard_map/ppermute | solution.py:52
  56.9 7.7 %collective-permute-done.4 = bf16[8,48,1280]{2,1,0:T(8,128)(2,1)S(1)} collective-permute-done((bf16[8,48,1280]{2,1,0:T(8,128)(2,1)S(1)}, bf16[8,48,1280]{2,1,0:T(8,128)(2,1)S(1)}, u32[]{:S(2)}, u32[]{:S(2)}) %collective-permute-start.4) | collective-permute-done | bytes 983072 | tf_op jit(solution)/shard_map/ppermute | solution.py:52
  81.6 18.4 %collective-permute-done.16 = bf16[8,192,384]{2,1,0:T(8,128)(2,1)} collective-permute-done((bf16[8,192,384]{2,1,0:T(8,128)(2,1)}, bf16[8,192,384]{2,1,0:T(8,128)(2,1)}, u32[]{:S(2)}, u32[]{:S(2)}) %collective-permute-start.16) | collective-permute-done | bytes 1179680 | tf_op jit(solution)/shard_map/ppermute | solution.py:52
  104.5 5.3 %shard_map.348 = bf16[768,2304]{1,0:T(8,128)(2,1)} custom-call(s32[3,16]{1,0:T(4,128)} %add_add_fusion.5.order_ref, bf16[16,48,1280]{2,1,0:T(8,128)(2,1)} %constant_dynamic-update-slice_fusion.own_ref, bf16[16,48,1280]{2,1,0:T(8,128)(2,1)} %collective-permute-done.5.other_ref), custom_call_target="tpu_custom_call" | custom-call | tf_op jit(solution)/shard_map/pallas_call | solution.py:187
  109.8 7.1 %fusion.36 = bf16[288,8,8,128]{3,1,2,0:T(8,128)(2,1)S(1)} fusion(f32[2304]{0:T(1024)S(1)} %pad_maximum_fusion.17, bf16[768,2304]{1,0:T(8,128)(2,1)} %shard_map.348, bf16[1024,768]{1,0:T(8,128)(2,1)} %param.23), kind=kOutput, calls=%fused_computation.75 | convolution fusion | flops 3628597248 | bytes 9839616 | tf_op jit(solution)/shard_map/dot_general | solution.py:280
  121.2 6.1 %fusion.122 = (f32[8,12,128]{2,1,0:T(8,128)S(1)}, f32[8,12,128,128]{2,3,1,0:T(8,128)S(1)}) fusion(f32[8,12,128,128]{2,3,1,0:T(8,128)S(1)} %fusion.64), kind=kOutput, calls=%fused_computation.291 | output fusion | flops 6291583 | bytes 12632064 | tf_op jit(solution)/shard_map/sub | solution.py:289
  132.5 5.6 %shard_map.350 = bf16[3072,768]{1,0:T(8,128)(2,1)} custom-call(s32[3,16]{1,0:T(4,128)} %add_add_fusion.5.order_ref, bf16[16,192,384]{2,1,0:T(8,128)(2,1)} %constant_dynamic-update-slice_fusion.10.own_ref, bf16[16,192,384]{2,1,0:T(8,128)(2,1)} %collective-permute-done.17.other_ref), custom_call_target="tpu_custom_call" | custom-call | tf_op jit(solution)/shard_map/pallas_call | solution.py:187
  138.1 6.8 %shard_map.349 = (bf16[768,768]{1,0:T(8,128)(2,1)}, bf16[768,3072]{1,0:T(8,128)(2,1)}) custom-call(s32[3,16]{1,0:T(4,128)} %add_add_fusion.5.order_ref, bf16[16,48,1920]{2,1,0:T(8,128)(2,1)} %copy-done.11, bf16[16,48,1920]{2,1,0:T(8,128)(2,1)} %collective-permute-done.11.other_ref), custom_call_target="tpu_custom_call" | custom-call | tf_op jit(solution)/shard_map/pallas_call | solution.py:187
  144.9 3.1 fusion.123
  148.6 35.5 %multiply_convert_fusion = (bf16[1024,3072]{1,0:T(8,128)(2,1)S(1)}, f32[1024,3072]{1,0:T(8,128)}, f32[1024,3072]{1,0:T(8,128)}) fusion(f32[3072]{0:T(1024)S(1)} %add.418, bf16[768,3072]{1,0:T(8,128)(2,1)S(1)} %bitcast.191, f32[1024,768]{1,0:T(8,128)S(1)} %get-tuple-element.160, f32[768]{0:T(1024)S(1)} %get-tuple-element.77, f32[768]{0:T(1024)S(1)} %get-tuple-element.78, ...), kind=kOutput, calls=%fused_computation.8 | convolution fusion | flops 5043388416 | bytes 39348224 | tf_op jit(solution)/shard_map/dot_general | solution.py:384
  184.2 5.5 %fusion.124 = (f32[1024]{0:T(1024)S(1)}, f32[1024,768]{1,0:T(8,128)S(1)}) fusion(f32[768]{0:T(1024)S(1)} %get-tuple-element.76, bf16[1024,3072]{1,0:T(8,128)(2,1)S(1)} %get-tuple-element.107, bf16[3072,768]{1,0:T(8,128)(2,1)S(1)} %bitcast.173, f32[768]{0:T(1024)S(1)} %get-tuple-element.77, f32[768]{0:T(1024)S(1)} %get-tuple-element.78, ...), kind=kOutput, calls=%fused_computation.293 | convolution fusion | flops 4837342208 | bytes 17323008 | tf_op jit(solution)/shard_map/dot_general | solution.py:386
  198.2 2.7 fusion.111
  200.9 18.9 %fusion.127 = (bf16[3072]{0:T(1024)(128)(2,1)S(1)}, bf16[1024,3072]{1,0:T(8,128)(2,1)}) fusion(f32[1024,3072]{1,0:T(8,128)} %get-tuple-element.108, bf16[3072,768]{1,0:T(8,128)(2,1)} %shard_map.350, f32[1024,768]{1,0:T(8,128)} %get-tuple-element.102, f32[1024,3072]{1,0:T(8,128)} %get-tuple-element.161, f32[3072]{0:T(1024)S(1)} %add.418), kind=kOutput, calls=%fused_computation.294 | convolution fusion | flops 4882953216 | bytes 39340032 | tf_op jit(solution)/shard_map/dot_general | solution.py:257
  219.8 10.0 %multiply_reduce_fusion.2 = (bf16[768]{0:T(1024)(128)(2,1)S(1)}, f32[1024]{0:T(1024)S(1)}, f32[1024]{0:T(1024)S(1)}, bf16[768]{0:T(1024)(128)(2,1)S(1)}, f32[1024,768]{1,0:T(8,128)S(1)}) fusion(f32[1024,768]{1,0:T(8,128)S(1)} %copy-done.3, f32[1024]{0:T(1024)S(1)} %add_rsqrt_fusion.1, f32[1024]{0:T(1024)S(1)} %broadcast_multiply_fusion.4, ...), kind=kOutput, calls=%fused_computation.48 | convolution fusion | flops 4839698432 | bytes 20469760 | tf_op jit(solution)/shard_map/dot_general | solution.py:257
  232.6 2.6 convolution_convert_fusion.3
  235.2 2.8 copy.105
  241.2 3.7 fusion.63
  244.9 12.3 %bitcast_reduce_fusion.1 = (bf16[12,64]{1,0:T(8,128)(2,1)S(1)}, bf16[8,12,64,128]{3,2,1,0:T(8,128)(2,1)}) fusion(f32[8,12,128,128]{2,3,1,0:T(8,128)} %fusion.63, f32[8,12,128,128]{2,3,1,0:T(8,128)} %copy-done.8, f32[8,12,128]{2,1,0:T(8,128)S(1)} %copy-done.45, bf16[8,128,1,12,64]{1,0,4,3,2:T(8,128)(2,1)} %copy-done.5), kind=kOutput, calls=%fused_computation.43 | convolution fusion | flops 213921152 | bytes 15779328 | tf_op jit(solution)/shard_map/nhqk,nkhe->nqhe/dot_general | solution.py:445
  257.2 12.0 %fusion.57 = bf16[8,128,1,12,64]{1,4,3,0,2:T(8,128)(2,1)} fusion(f32[8,12,128,128]{2,3,1,0:T(8,128)} %fusion.63, bf16[8,128,1,12,64]{1,0,4,3,2:T(8,128)(2,1)} %copy-done.4, f32[8,12,128,128]{2,3,1,0:T(8,128)} %copy-done.8, f32[8,12,128]{2,1,0:T(8,128)S(1)} %copy-done.45), kind=kOutput, calls=%fused_computation.93 | convolution fusion | flops 213135488 | bytes 15777792 | tf_op jit(solution)/shard_map/nhqk,nqhe->nkhe/dot_general | solution.py:448
  269.2 5.8 %bitcast_reduce_fusion = (bf16[12,64]{1,0:T(8,128)(2,1)S(1)}, bf16[8,12,64,128]{3,2,1,0:T(8,128)(2,1)S(1)}) fusion(f32[8,12,128,128]{2,3,1,0:T(8,128)} %copy-done.8, f32[8,12,128]{2,1,0:T(8,128)S(1)} %copy-done.45, bf16[8,128,12,64]{1,0,3,2:T(8,128)(2,1)} %bitcast.170), kind=kOutput, calls=%fused_computation.41 | convolution fusion | flops 206044416 | bytes 9487872 | tf_op jit(solution)/shard_map/nhqk,nqhe->nkhe/dot_general | solution.py:438
  275.0 10.1 %convolution_convert_fusion.rest_0_ = bf16[3072,768]{1,0:T(8,128)(2,1)} fusion(bf16[1024,3072]{1,0:T(8,128)(2,1)} %copy-done.60, f32[1024,768]{1,0:T(8,128)S(1)} %copy-done.14), kind=kOutput, calls=%fused_computation.29 | convolution fusion | flops 4834983936 | bytes 14155776 | tf_op jit(solution)/shard_map/dot_general | solution.py:251
  285.0 7.8 %convolution_convert_fusion.1.rest_0_ = bf16[768,3072]{1,0:T(8,128)(2,1)} fusion(bf16[1024,3072]{1,0:T(8,128)(2,1)S(1)} %bitcast.193, f32[1024,768]{1,0:T(8,128)S(1)} %copy-done.3, f32[768]{0:T(1024)S(1)} %get-tuple-element.77, f32[768]{0:T(1024)S(1)} %get-tuple-element.78, f32[1024]{0:T(1024)S(1)} %add_rsqrt_fusion.1, f32[1024]{0:T(1024)S(1)} %broadcast_multiply_fusion.4), kind=kOutput, calls=%fused_computation.30 | convolution fusion | flops 4838129664 | bytes 14170112 | tf_op jit(solution)/shard_map/dot_general | solution.py:251
  295.2 11.4 %copy.111 = bf16[8,128,3,12,64]{1,0,4,3,2:T(8,128)(2,1)} copy(bf16[8,128,3,12,64]{1,4,3,0,2:T(8,128)(2,1)S(1)} %pad_maximum_fusion) | data formatting | bytes 9437184 | tf_op jit(solution)/shard_map/stack | solution.py:449
  306.6 4.8 shard_map.353
  311.7 5.0 shard_map.352
  317.0 8.1 %fusion.13.rest_1_ = bf16[768,2304]{1,0:T(8,128)(2,1)} fusion(bf16[1024,768]{1,0:T(8,128)(2,1)S(1)} %copy-done.58, bf16[288,8,8,128]{3,2,1,0:T(8,128)(2,1)} %bitcast.174), kind=kOutput, calls=%fused_computation.36 | convolution fusion | flops 3625648128 | bytes 9830400 | tf_op jit(solution)/shard_map/dot_general | solution.py:251
  327.5 5.7 %shard_map.351 = (bf16[16,48,1536]{2,1,0:T(8,128)(2,1)}, bf16[16,48,1536]{2,1,0:T(8,128)(2,1)}) custom-call(s32[3,16]{1,0:T(4,128)} %add_add_fusion.5.order_ref, bf16[768,768]{1,0:T(8,128)(2,1)} %fusion.54.rest_0_, bf16[768,2304]{1,0:T(8,128)(2,1)} %fusion.13.rest_1_), custom_call_target="tpu_custom_call" | custom-call | tf_op jit(solution)/shard_map/pallas_call | solution.py:240
  335.6 2.5 collective-permute-done.38
  340.2 2.6 collective-permute-done.39
  351.3 2.6 add_convert_fusion.3
  354.0 2.7 add_convert_fusion.4
  360.1 9.8 %collective-permute-start.42 = (bf16[1,48,128]{2,1,0:T(8,128)(2,1)}, bf16[1,48,128]{2,1,0:T(8,128)(2,1)}, u32[]{:S(2)}, u32[]{:S(2)}) collective-permute-start(bf16[1,48,128]{2,1,0:T(8,128)(2,1)} %add_convert_fusion.17), channel_id=1, source_target_pairs={{0,8},{1,17},{2,10},{3,19},{4,12},{5,21},{6,14},{7,23},{8,0},{9,25... | collective-permute-start | bytes 36872 | tf_op jit(solution)/shard_map/ppermute | solution.py:52
  382.9 20.2 %collective-permute-done.21 = bf16[8,48,1536]{2,1,0:T(8,128)(2,1)} collective-permute-done((bf16[8,48,1536]{2,1,0:T(8,128)(2,1)}, bf16[8,48,1536]{2,1,0:T(8,128)(2,1)}, u32[]{:S(2)}, u32[]{:S(2)}) %collective-permute-start.21) | collective-permute-done | bytes 1179680 | tf_op jit(solution)/shard_map/ppermute | solution.py:52
  404.5 2.5 collective-permute-start.22
  408.3 3.0 collective-permute-start.35
  416.1 3.0 collective-permute-start.23
  420.2 21.3 %collective-permute-start.36 = (bf16[1,192,384]{2,1,0:T(8,128)(2,1)S(1)}, bf16[1,192,384]{2,1,0:T(8,128)(2,1)S(1)}, u32[]{:S(2)}, u32[]{:S(2)}) collective-permute-start(bf16[1,192,384]{2,1,0:T(8,128)(2,1)S(1)} %add_convert_fusion.11), channel_id=1, source_target_pairs={{0,8},{1,17},{2,10},{3,19},{4,12},{5,21},{6,14},{7,23},{8,0},{9,25... | collective-permute-start | bytes 442376 | tf_op jit(solution)/shard_map/ppermute | solution.py:52
  442.6 3.8 collective-permute-start.30
  464.6 3.6 collective-permute-done.44
  475.4 3.5 collective-permute-start.47
  478.9 8.2 %fusion.40 = f32[1024,768]{1,0:T(8,128)} fusion(f32[1024,768]{1,0:T(8,128)} %copy-done.12, bf16[768,2304]{1,0:T(8,128)(2,1)S(1)} %copy-done.10, bf16[288,8,8,128]{3,2,1,0:T(8,128)(2,1)} %bitcast.175), kind=kOutput, calls=%fused_computation.77 | convolution fusion | flops 3624665088 | bytes 14548992 | tf_op jit(solution)/shard_map/dot_general | solution.py:257
  (376 shorter events, 140.4 us)
Async XLA Ops:
  1.7 18.8 %collective-permute-start.12 = (bf16[96,384]{1,0:T(8,128)(2,1)S(1)}, bf16[96,384]{1,0:T(8,128)(2,1)S(1)}, u32[]{:S(2)}, u32[]{:S(2)}) collective-permute-start(bf16[96,384]{1,0:T(8,128)(2,1)S(1)} %get-tuple-element.128), channel_id=1, source_target_pairs={{0,1},{1,0},{2,3},{3,2},{4,5},{5,4},{6,7},{7,6},{8,9},{9,8},{10,11... | collective-permute-start | bytes 221192 | tf_op jit(solution)/shard_map/ppermute | solution.py:56
  4.2 18.8 %collective-permute-start.6 = (bf16[24,1920]{1,0:T(8,128)(2,1)S(1)}, bf16[24,1920]{1,0:T(8,128)(2,1)S(1)}, u32[]{:S(2)}, u32[]{:S(2)}) collective-permute-start(bf16[24,1920]{1,0:T(8,128)(2,1)S(1)} %get-tuple-element.122), channel_id=1, source_target_pairs={{0,1},{1,0},{2,3},{3,2},{4,5},{5,4},{6,7},{7,6},{8,9},{9,8},{10,11... | collective-permute-start | bytes 276488 | tf_op jit(solution)/shard_map/ppermute | solution.py:56
  6.1 4.5 collective-permute-start
  11.3 6.6 %collective-permute-start.1 = (bf16[1,48,1280]{2,1,0:T(8,128)(2,1)S(1)}, bf16[1,48,1280]{2,1,0:T(8,128)(2,1)S(1)}, u32[]{:S(2)}, u32[]{:S(2)}) collective-permute-start(bf16[1,48,1280]{2,1,0:T(8,128)(2,1)S(1)} %get-tuple-element.112), channel_id=1, source_target_pairs={{0,8},{1,17},{2,10},{3,19},{4,12},{5,21},{6,14},{7,23},{8,0},{9,25... | collective-permute-start | bytes 368648 | tf_op jit(solution)/shard_map/ppermute | solution.py:52
  17.9 11.8 %collective-permute-start.2 = (bf16[2,48,1280]{2,1,0:T(8,128)(2,1)S(1)}, bf16[2,48,1280]{2,1,0:T(8,128)(2,1)S(1)}, u32[]{:S(2)}, u32[]{:S(2)}) collective-permute-start(bf16[2,48,1280]{2,1,0:T(8,128)(2,1)S(1)} %pad_maximum_fusion.11), channel_id=1, source_target_pairs={{0,16},{1,9},{2,18},{3,11},{4,20},{5,13},{6,22},{7,15},{8,24},{9,1... | collective-permute-start | bytes 737288 | tf_op jit(solution)/shard_map/ppermute | solution.py:52
  21.3 13.0 %collective-permute-start.13 = (bf16[1,192,384]{2,1,0:T(8,128)(2,1)S(1)}, bf16[1,192,384]{2,1,0:T(8,128)(2,1)S(1)}, u32[]{:S(2)}, u32[]{:S(2)}) collective-permute-start(bf16[1,192,384]{2,1,0:T(8,128)(2,1)S(1)} %get-tuple-element.106), channel_id=1, source_target_pairs={{0,8},{1,17},{2,10},{3,19},{4,12},{5,21},{6,14},{7,23},{8,0},{9,25... | collective-permute-start | bytes 442376 | tf_op jit(solution)/shard_map/ppermute | solution.py:52
  23.0 12.0 %collective-permute-start.7 = (bf16[1,48,1920]{2,1,0:T(8,128)(2,1)S(1)}, bf16[1,48,1920]{2,1,0:T(8,128)(2,1)S(1)}, u32[]{:S(2)}, u32[]{:S(2)}) collective-permute-start(bf16[1,48,1920]{2,1,0:T(8,128)(2,1)S(1)} %get-tuple-element.110), channel_id=1, source_target_pairs={{0,8},{1,17},{2,10},{3,19},{4,12},{5,21},{6,14},{7,23},{8,0},{9,25... | collective-permute-start | bytes 552968 | tf_op jit(solution)/shard_map/ppermute | solution.py:52
  29.7 12.7 %collective-permute-start.3 = (bf16[4,48,1280]{2,1,0:T(8,128)(2,1)S(1)}, bf16[4,48,1280]{2,1,0:T(8,128)(2,1)S(1)}, u32[]{:S(2)}, u32[]{:S(2)}) collective-permute-start(bf16[4,48,1280]{2,1,0:T(8,128)(2,1)S(1)} %pad_maximum_fusion.6), channel_id=1, source_target_pairs={{0,2},{1,5},{2,0},{3,7},{4,6},{5,1},{6,4},{7,3},{8,10},{9,13},{10,... | collective-permute-start | bytes 1474568 | tf_op jit(solution)/shard_map/ppermute | solution.py:52
  34.3 19.7 %collective-permute-start.14 = (bf16[2,192,384]{2,1,0:T(8,128)(2,1)S(1)}, bf16[2,192,384]{2,1,0:T(8,128)(2,1)S(1)}, u32[]{:S(2)}, u32[]{:S(2)}) collective-permute-start(bf16[2,192,384]{2,1,0:T(8,128)(2,1)S(1)} %pad_maximum_fusion.8), channel_id=1, source_target_pairs={{0,16},{1,9},{2,18},{3,11},{4,20},{5,13},{6,22},{7,15},{8,24},{9,1... | collective-permute-start | bytes 884744 | tf_op jit(solution)/shard_map/ppermute | solution.py:52
  35.1 18.0 %collective-permute-start.8 = (bf16[2,48,1920]{2,1,0:T(8,128)(2,1)S(1)}, bf16[2,48,1920]{2,1,0:T(8,128)(2,1)S(1)}, u32[]{:S(2)}, u32[]{:S(2)}) collective-permute-start(bf16[2,48,1920]{2,1,0:T(8,128)(2,1)S(1)} %pad_maximum_fusion.7), channel_id=1, source_target_pairs={{0,16},{1,9},{2,18},{3,11},{4,20},{5,13},{6,22},{7,15},{8,24},{9,1... | collective-permute-start | bytes 1105928 | tf_op jit(solution)/shard_map/ppermute | solution.py:52
  42.5 22.1 %collective-permute-start.4 = (bf16[8,48,1280]{2,1,0:T(8,128)(2,1)S(1)}, bf16[8,48,1280]{2,1,0:T(8,128)(2,1)S(1)}, u32[]{:S(2)}, u32[]{:S(2)}) collective-permute-start(bf16[8,48,1280]{2,1,0:T(8,128)(2,1)S(1)} %pad_maximum_fusion.3), channel_id=1, source_target_pairs={{0,4},{1,3},{2,6},{3,1},{4,0},{5,7},{6,2},{7,5},{8,12},{9,11},{10,... | collective-permute-start | bytes 2949128 | tf_op jit(solution)/shard_map/ppermute | solution.py:52
  53.2 12.5 %collective-permute-start.9 = (bf16[4,48,1920]{2,1,0:T(8,128)(2,1)S(1)}, bf16[4,48,1920]{2,1,0:T(8,128)(2,1)S(1)}, u32[]{:S(2)}, u32[]{:S(2)}) collective-permute-start(bf16[4,48,1920]{2,1,0:T(8,128)(2,1)S(1)} %pad_maximum_fusion.4), channel_id=1, source_target_pairs={{0,2},{1,5},{2,0},{3,7},{4,6},{5,1},{6,4},{7,3},{8,10},{9,13},{10,... | collective-permute-start | bytes 2211848 | tf_op jit(solution)/shard_map/ppermute | solution.py:52
  54.1 17.6 %collective-permute-start.15 = (bf16[4,192,384]{2,1,0:T(8,128)(2,1)S(1)}, bf16[4,192,384]{2,1,0:T(8,128)(2,1)S(1)}, u32[]{:S(2)}, u32[]{:S(2)}) collective-permute-start(bf16[4,192,384]{2,1,0:T(8,128)(2,1)S(1)} %pad_maximum_fusion.5), channel_id=1, source_target_pairs={{0,2},{1,5},{2,0},{3,7},{4,6},{5,1},{6,4},{7,3},{8,10},{9,13},{10,... | collective-permute-start | bytes 1769480 | tf_op jit(solution)/shard_map/ppermute | solution.py:52
  65.7 38.8 %collective-permute-start.5 = (bf16[16,48,1280]{2,1,0:T(8,128)(2,1)}, bf16[16,48,1280]{2,1,0:T(8,128)(2,1)}, u32[]{:S(2)}, u32[]{:S(2)}) collective-permute-start(bf16[16,48,1280]{2,1,0:T(8,128)(2,1)} %constant_dynamic-update-slice_fusion.own_ref), channel_id=1, source_target_pairs={{0,1},{1,0},{2,3},{3,2},{4,5},{5,4},{6,7},{7,6},{8,9},{9,8},{10,11... | collective-permute-start | bytes 5898248 | tf_op jit(solution)/shard_map/ppermute | solution.py:56
  67.0 35.4 %collective-permute-start.10 = (bf16[8,48,1920]{2,1,0:T(8,128)(2,1)}, bf16[8,48,1920]{2,1,0:T(8,128)(2,1)}, u32[]{:S(2)}, u32[]{:S(2)}) collective-permute-start(bf16[8,48,1920]{2,1,0:T(8,128)(2,1)} %pad_maximum_fusion.1), channel_id=1, source_target_pairs={{0,4},{1,3},{2,6},{3,1},{4,0},{5,7},{6,2},{7,5},{8,12},{9,11},{10,... | collective-permute-start | bytes 4423688 | tf_op jit(solution)/shard_map/ppermute | solution.py:52
  72.8 27.1 %collective-permute-start.16 = (bf16[8,192,384]{2,1,0:T(8,128)(2,1)}, bf16[8,192,384]{2,1,0:T(8,128)(2,1)}, u32[]{:S(2)}, u32[]{:S(2)}) collective-permute-start(bf16[8,192,384]{2,1,0:T(8,128)(2,1)} %pad_maximum_fusion.2), channel_id=1, source_target_pairs={{0,4},{1,3},{2,6},{3,1},{4,0},{5,7},{6,2},{7,5},{8,12},{9,11},{10,... | collective-permute-start | bytes 3538952 | tf_op jit(solution)/shard_map/ppermute | solution.py:52
  102.3 30.1 %collective-permute-start.17 = (bf16[16,192,384]{2,1,0:T(8,128)(2,1)}, bf16[16,192,384]{2,1,0:T(8,128)(2,1)}, u32[]{:S(2)}, u32[]{:S(2)}) collective-permute-start(bf16[16,192,384]{2,1,0:T(8,128)(2,1)} %constant_dynamic-update-slice_fusion.10.own_ref), channel_id=1, source_target_pairs={{0,1},{1,0},{2,3},{3,2},{4,5},{5,4},{6,7},{7,6},{8,9},{9,8},{10,11... | collective-permute-start | bytes 7077896 | tf_op jit(solution)/shard_map/ppermute | solution.py:56
  103.9 34.1 %collective-permute-start.11 = (bf16[16,48,1920]{2,1,0:T(8,128)(2,1)S(1)}, bf16[16,48,1920]{2,1,0:T(8,128)(2,1)}, u32[]{:S(2)}, u32[]{:S(2)}) collective-permute-start(bf16[16,48,1920]{2,1,0:T(8,128)(2,1)S(1)} %constant_dynamic-update-slice_fusion.5.own_ref), channel_id=1, source_target_pairs={{0,1},{1,0},{2,3},{3,2},{4,5},{5,4},{6,7},{7,6},{8,9},{9,8},{10,11... | collective-permute-start | bytes 8847368 | tf_op jit(solution)/shard_map/ppermute | solution.py:56
  191.3 1.2 collective-permute-start.18
  193.7 1.2 collective-permute-start.19
  311.4 35.7 %collective-permute-start.32 = (bf16[16,192,384]{2,1,0:T(8,128)(2,1)}, bf16[16,192,384]{2,1,0:T(8,128)(2,1)}, u32[]{:S(2)}, u32[]{:S(2)}) collective-permute-start(bf16[16,192,384]{2,1,0:T(8,128)(2,1)} %get-tuple-element.46), channel_id=1, source_target_pairs={{0,1},{1,0},{2,3},{3,2},{4,5},{5,4},{6,7},{7,6},{8,9},{9,8},{10,11... | collective-permute-start | bytes 7077896 | tf_op jit(solution)/shard_map/ppermute | solution.py:56
  316.6 34.7 %collective-permute-start.26 = (bf16[16,48,1536]{2,1,0:T(8,128)(2,1)}, bf16[16,48,1536]{2,1,0:T(8,128)(2,1)}, u32[]{:S(2)}, u32[]{:S(2)}) collective-permute-start(bf16[16,48,1536]{2,1,0:T(8,128)(2,1)} %get-tuple-element.44), channel_id=1, source_target_pairs={{0,1},{1,0},{2,3},{3,2},{4,5},{5,4},{6,7},{7,6},{8,9},{9,8},{10,11... | collective-permute-start | bytes 7077896 | tf_op jit(solution)/shard_map/ppermute | solution.py:56
  333.2 20.8 %collective-permute-start.20 = (bf16[16,48,1536]{2,1,0:T(8,128)(2,1)}, bf16[16,48,1536]{2,1,0:T(8,128)(2,1)}, u32[]{:S(2)}, u32[]{:S(2)}) collective-permute-start(bf16[16,48,1536]{2,1,0:T(8,128)(2,1)} %get-tuple-element.42), channel_id=1, source_target_pairs={{0,1},{1,0},{2,3},{3,2},{4,5},{5,4},{6,7},{7,6},{8,9},{9,8},{10,11... | collective-permute-start | bytes 7077896 | tf_op jit(solution)/shard_map/ppermute | solution.py:56
  334.7 3.5 collective-permute-start.38
  338.2 4.7 collective-permute-start.39
  342.9 4.2 collective-permute-start.40
  347.1 11.7 %collective-permute-start.41 = (bf16[2,48,128]{2,1,0:T(8,128)(2,1)S(1)}, bf16[2,48,128]{2,1,0:T(8,128)(2,1)S(1)}, u32[]{:S(2)}, u32[]{:S(2)}) collective-permute-start(bf16[2,48,128]{2,1,0:T(8,128)(2,1)S(1)} %add_convert_fusion.16), channel_id=1, source_target_pairs={{0,16},{1,9},{2,18},{3,11},{4,20},{5,13},{6,22},{7,15},{8,24},{9,1... | collective-permute-start | bytes 73736 | tf_op jit(solution)/shard_map/ppermute | solution.py:52
  349.2 27.6 %collective-permute-start.33 = (bf16[8,192,384]{2,1,0:T(8,128)(2,1)S(1)}, bf16[8,192,384]{2,1,0:T(8,128)(2,1)}, u32[]{:S(2)}, u32[]{:S(2)}) collective-permute-start(bf16[8,192,384]{2,1,0:T(8,128)(2,1)S(1)} %add_convert_fusion.2), channel_id=1, source_target_pairs={{0,4},{1,3},{2,6},{3,1},{4,0},{5,7},{6,2},{7,5},{8,12},{9,11},{10,... | collective-permute-start | bytes 3538952 | tf_op jit(solution)/shard_map/ppermute | solution.py:52
  354.0 26.6 %collective-permute-start.27 = (bf16[8,48,1536]{2,1,0:T(8,128)(2,1)}, bf16[8,48,1536]{2,1,0:T(8,128)(2,1)}, u32[]{:S(2)}, u32[]{:S(2)}) collective-permute-start(bf16[8,48,1536]{2,1,0:T(8,128)(2,1)} %add_convert_fusion.3), channel_id=1, source_target_pairs={{0,4},{1,3},{2,6},{3,1},{4,0},{5,7},{6,2},{7,5},{8,12},{9,11},{10,... | collective-permute-start | bytes 3538952 | tf_op jit(solution)/shard_map/ppermute | solution.py:52
  356.7 46.4 %collective-permute-start.21 = (bf16[8,48,1536]{2,1,0:T(8,128)(2,1)}, bf16[8,48,1536]{2,1,0:T(8,128)(2,1)}, u32[]{:S(2)}, u32[]{:S(2)}) collective-permute-start(bf16[8,48,1536]{2,1,0:T(8,128)(2,1)} %add_convert_fusion.4), channel_id=1, source_target_pairs={{0,4},{1,3},{2,6},{3,1},{4,0},{5,7},{6,2},{7,5},{8,12},{9,11},{10,... | collective-permute-start | bytes 3538952 | tf_op jit(solution)/shard_map/ppermute | solution.py:52
  360.1 12.6 %collective-permute-start.42 = (bf16[1,48,128]{2,1,0:T(8,128)(2,1)}, bf16[1,48,128]{2,1,0:T(8,128)(2,1)}, u32[]{:S(2)}, u32[]{:S(2)}) collective-permute-start(bf16[1,48,128]{2,1,0:T(8,128)(2,1)} %add_convert_fusion.17), channel_id=1, source_target_pairs={{0,8},{1,17},{2,10},{3,19},{4,12},{5,21},{6,14},{7,23},{8,0},{9,25... | collective-permute-start | bytes 36872 | tf_op jit(solution)/shard_map/ppermute | solution.py:52
  378.5 28.5 %collective-permute-start.34 = (bf16[4,192,384]{2,1,0:T(8,128)(2,1)S(1)}, bf16[4,192,384]{2,1,0:T(8,128)(2,1)S(1)}, u32[]{:S(2)}, u32[]{:S(2)}) collective-permute-start(bf16[4,192,384]{2,1,0:T(8,128)(2,1)S(1)} %add_convert_fusion.5), channel_id=1, source_target_pairs={{0,2},{1,5},{2,0},{3,7},{4,6},{5,1},{6,4},{7,3},{8,10},{9,13},{10,... | collective-permute-start | bytes 1769480 | tf_op jit(solution)/shard_map/ppermute | solution.py:52
  382.1 29.3 %collective-permute-start.28 = (bf16[4,48,1536]{2,1,0:T(8,128)(2,1)S(1)}, bf16[4,48,1536]{2,1,0:T(8,128)(2,1)S(1)}, u32[]{:S(2)}, u32[]{:S(2)}) collective-permute-start(bf16[4,48,1536]{2,1,0:T(8,128)(2,1)S(1)} %add_convert_fusion.6), channel_id=1, source_target_pairs={{0,2},{1,5},{2,0},{3,7},{4,6},{5,1},{6,4},{7,3},{8,10},{9,13},{10,... | collective-permute-start | bytes 1769480 | tf_op jit(solution)/shard_map/ppermute | solution.py:52
  404.5 10.4 %collective-permute-start.22 = (bf16[4,48,1536]{2,1,0:T(8,128)(2,1)S(1)}, bf16[4,48,1536]{2,1,0:T(8,128)(2,1)S(1)}, u32[]{:S(2)}, u32[]{:S(2)}) collective-permute-start(bf16[4,48,1536]{2,1,0:T(8,128)(2,1)S(1)} %add_convert_fusion.7), channel_id=1, source_target_pairs={{0,2},{1,5},{2,0},{3,7},{4,6},{5,1},{6,4},{7,3},{8,10},{9,13},{10,... | collective-permute-start | bytes 1769480 | tf_op jit(solution)/shard_map/ppermute | solution.py:52
  408.3 10.7 %collective-permute-start.35 = (bf16[2,192,384]{2,1,0:T(8,128)(2,1)S(1)}, bf16[2,192,384]{2,1,0:T(8,128)(2,1)S(1)}, u32[]{:S(2)}, u32[]{:S(2)}) collective-permute-start(bf16[2,192,384]{2,1,0:T(8,128)(2,1)S(1)} %add_convert_fusion.8), channel_id=1, source_target_pairs={{0,16},{1,9},{2,18},{3,11},{4,20},{5,13},{6,22},{7,15},{8,24},{9,1... | collective-permute-start | bytes 884744 | tf_op jit(solution)/shard_map/ppermute | solution.py:52
  412.5 29.1 %collective-permute-start.29 = (bf16[2,48,1536]{2,1,0:T(8,128)(2,1)S(1)}, bf16[2,48,1536]{2,1,0:T(8,128)(2,1)S(1)}, u32[]{:S(2)}, u32[]{:S(2)}) collective-permute-start(bf16[2,48,1536]{2,1,0:T(8,128)(2,1)S(1)} %add_convert_fusion.9), channel_id=1, source_target_pairs={{0,16},{1,9},{2,18},{3,11},{4,20},{5,13},{6,22},{7,15},{8,24},{9,1... | collective-permute-start | bytes 884744 | tf_op jit(solution)/shard_map/ppermute | solution.py:52
  416.1 30.4 %collective-permute-start.23 = (bf16[2,48,1536]{2,1,0:T(8,128)(2,1)S(1)}, bf16[2,48,1536]{2,1,0:T(8,128)(2,1)S(1)}, u32[]{:S(2)}, u32[]{:S(2)}) collective-permute-start(bf16[2,48,1536]{2,1,0:T(8,128)(2,1)S(1)} %add_convert_fusion.10), channel_id=1, source_target_pairs={{0,16},{1,9},{2,18},{3,11},{4,20},{5,13},{6,22},{7,15},{8,24},{9,1... | collective-permute-start | bytes 884744 | tf_op jit(solution)/shard_map/ppermute | solution.py:52
  420.2 29.5 %collective-permute-start.36 = (bf16[1,192,384]{2,1,0:T(8,128)(2,1)S(1)}, bf16[1,192,384]{2,1,0:T(8,128)(2,1)S(1)}, u32[]{:S(2)}, u32[]{:S(2)}) collective-permute-start(bf16[1,192,384]{2,1,0:T(8,128)(2,1)S(1)} %add_convert_fusion.11), channel_id=1, source_target_pairs={{0,8},{1,17},{2,10},{3,19},{4,12},{5,21},{6,14},{7,23},{8,0},{9,25... | collective-permute-start | bytes 442376 | tf_op jit(solution)/shard_map/ppermute | solution.py:52
  442.6 11.4 %collective-permute-start.30 = (bf16[1,48,1536]{2,1,0:T(8,128)(2,1)S(1)}, bf16[1,48,1536]{2,1,0:T(8,128)(2,1)S(1)}, u32[]{:S(2)}, u32[]{:S(2)}) collective-permute-start(bf16[1,48,1536]{2,1,0:T(8,128)(2,1)S(1)} %add_convert_fusion.12), channel_id=1, source_target_pairs={{0,8},{1,17},{2,10},{3,19},{4,12},{5,21},{6,14},{7,23},{8,0},{9,25... | collective-permute-start | bytes 442376 | tf_op jit(solution)/shard_map/ppermute | solution.py:52
  447.6 5.2 %collective-permute-start.24 = (bf16[1,48,1536]{2,1,0:T(8,128)(2,1)S(1)}, bf16[1,48,1536]{2,1,0:T(8,128)(2,1)S(1)}, u32[]{:S(2)}, u32[]{:S(2)}) collective-permute-start(bf16[1,48,1536]{2,1,0:T(8,128)(2,1)S(1)} %add_convert_fusion.13), channel_id=1, source_target_pairs={{0,8},{1,17},{2,10},{3,19},{4,12},{5,21},{6,14},{7,23},{8,0},{9,25... | collective-permute-start | bytes 442376 | tf_op jit(solution)/shard_map/ppermute | solution.py:52
  450.9 5.0 %collective-permute-start.37 = (bf16[96,384]{1,0:T(8,128)(2,1)S(1)}, bf16[96,384]{1,0:T(8,128)(2,1)S(1)}, u32[]{:S(2)}, u32[]{:S(2)}) collective-permute-start(bf16[96,384]{1,0:T(8,128)(2,1)S(1)} %fusion.82), channel_id=1, source_target_pairs={{0,1},{1,0},{2,3},{3,2},{4,5},{5,4},{6,7},{7,6},{8,9},{9,8},{10,11... | collective-permute-start | bytes 221192 | tf_op jit(solution)/shard_map/ppermute | solution.py:56
  453.9 1.8 collective-permute-start.25
  455.2 2.1 collective-permute-start.31
  463.4 1.1 collective-permute-start.43
  464.6 3.6 collective-permute-start.44
  468.2 3.6 collective-permute-start.45
  471.8 3.6 collective-permute-start.46
  475.4 11.8 %collective-permute-start.47 = (f32[2,128]{1,0:T(2,128)S(1)}, f32[2,128]{1,0:T(2,128)S(1)}, u32[]{:S(2)}, u32[]{:S(2)}) collective-permute-start(f32[2,128]{1,0:T(2,128)S(1)} %add.502), channel_id=1, source_target_pairs={{0,16},{1,17},{2,18},{3,19},{4,20},{5,21},{6,22},{7,23},{8,24},{9,... | collective-permute-start | bytes 3080 | tf_op jit(solution)/shard_map/ppermute | solution.py:52
  (68 other events, 586.4 us)

commit v2 on v0

v2 whole, which is shorter than its diff:
```python
from functools import partial

import jax
import jax.numpy as jnp
from jax import lax
from jax.experimental import pallas as pl
from jax.experimental.pallas import tpu as pltpu
from jax.sharding import PartitionSpec as P

HEADS = 12
HD = 64
L = 128
STEP = 10
LANES = 128
AXES = ("dp", "pair")


LN_EPS = 1e-12
LOSS_WEIGHT = 8.0
CLIP_NORM = 1000.0
BETA_ONE = 0.9
BETA_TWO = 0.999
ADAM_EPS = 1e-08
RATE_MATRIX = 0.05
DECAY_MATRIX = 0.01
RATE_AFFINE = 0.8
DECAY_AFFINE = 0.0

BF16 = jnp.bfloat16
F32 = jnp.float32


def flip_steps(chips):
    bits = chips.bit_length() - 1
    if bits == 4:
        return ((2, 3), (3, 2), (0, 1), (1, 0))
    return tuple((bit, bit) for bit in reversed(range(bits)))


def flip_route(chips, pair_of_bits):
    return [
        (2 * d + c, 2 * (d ^ (1 << pair_of_bits[c])) + c) for d in range(chips) for c in range(2)
    ]


def core_route(chips):
    return [(2 * d + c, 2 * d + 1 - c) for d in range(chips) for c in range(2)]


def flipped(block, bits):
    chips = lax.axis_size("dp")
    return lax.ppermute(block, AXES, flip_route(chips, bits))


def core_swapped(block):
    return lax.ppermute(block, AXES, core_route(lax.axis_size("dp")))


def block_order():
    chips = lax.axis_size("dp")
    d, c = lax.axis_index("dp"), lax.axis_index("pair")
    steps = flip_steps(chips)
    index = jnp.arange(chips, dtype=jnp.int32)
    blocks, places = [], []
    for core in range(2):
        blocks.append(sum((index >> k & 1) << step[core] for k, step in enumerate(steps)) ^ d)
        places.append(sum(((index ^ d) >> step[core] & 1) << k for k, step in enumerate(steps)))
    rows = []
    for pairs in (blocks, places):
        rows += [pick(c, pairs[0], pairs[1]), pick(c, pairs[1], pairs[0])]
    return jnp.stack(rows + [jnp.full((chips,), c, jnp.int32)])


def kernel_order(order, rows):
    if rows % 16 == 0:
        return order
    index = jnp.arange(16, dtype=jnp.int32)
    return jnp.stack([index] * 4 + [jnp.full((16,), order[4, 0], jnp.int32)])


def in_order(order, own, other, rows):
    if rows % 16 == 0:
        return own, other
    return tuple(
        blocks.reshape(order.shape[1], rows, -1)[order[side]] for side, blocks in enumerate((own, other))
    )


def pick(core, first, second):
    return jnp.where(core == 0, first, second)


def halves_of(low, pieces):
    core = lax.axis_index("pair")
    first, second, at = [], [], 0
    for width in pieces:
        first.append(low[:, at : at + width])
        second.append(low[:, at + width : at + 2 * width])
        at += 2 * width
    first, second = jnp.concatenate(first, 1), jnp.concatenate(second, 1)
    return pick(core, first, second), pick(core, second, first)


def chip_rows(low, pieces, extra=None):
    core = lax.axis_index("pair")
    own, other = halves_of(low, pieces)
    if extra is not None:
        own, other = (jnp.concatenate([half, extra], 1) for half in (own, other))
    got = core_swapped(other)
    return pick(core, jnp.concatenate([own, got]), jnp.concatenate([got, own]))


def tied(value, *others):
    return lax.optimization_barrier((value, *others))[0]


class Gather:
    def __init__(self, block):
        self.held, self.got, self.left = block[None], None, list(flip_steps(lax.axis_size("dp")))

    def step(self, *others):
        if self.got is not None:
            self.held = jnp.concatenate([self.held, self.got], axis=0)
        self.got = flipped(tied(self.held, *others), self.left.pop(0))
        return self.got

    def finish(self, order, rows, *others):
        while self.left:
            self.step()
        own = tied(jnp.concatenate([self.held, self.got], axis=0), *others)
        other = core_swapped(own)
        if rows % 16:
            own, other = (
                jnp.zeros(ref.shape, BF16).at[order[side]].set(ref).reshape(16, -1, ref.shape[2])
                for side, ref in enumerate((own, other))
            )
        return own, other


class Reduce:
    def __init__(self, own, other):
        self.count, self.left = own.shape[0], list(reversed(flip_steps(lax.axis_size("dp"))))
        self.parts = [own, core_swapped(other)]

    def last(self):
        return self.parts[-1]

    def step(self, *others):
        self.count //= 2
        sent = sum(p[self.count : 2 * self.count].astype(F32) for p in self.parts).astype(BF16)
        self.parts.append(flipped(tied(sent, *others), self.left.pop(0)))
        return self.parts[-1]

    def finish(self):
        while self.left:
            self.step()
        return self.parts


def total_over_devices(value):
    chips = lax.axis_size("dp")
    value = value + core_swapped(value)
    for bit in range(chips.bit_length() - 1):
        value = value + flipped(value, (bit, bit))
    return value


TILE = 256
PART = 256
PAIR_LANES = 2 * HD
VMEM_LIMIT = 32 * 1024 * 1024
SMEM = pl.BlockSpec(memory_space=pltpu.SMEM)
ANY = pl.BlockSpec(memory_space=pl.ANY)


def call(kernel, grid, ins, outs, scratch=(), micros=10, after=(), order=None):
    count = len(ins) + (order is not None)

    def body(*refs):
        kernel(*refs[:count], *refs[count + len(after) :])

    in_specs = [spec for _, spec in ins] + [ANY] * len(after)
    operands = [array for array, _ in ins] + list(after)
    if order is not None:
        operands = [order] + operands
    return pl.pallas_call(
        body,
        grid_spec=pltpu.PrefetchScalarGridSpec(
            num_scalar_prefetch=int(order is not None),
            grid=grid,
            in_specs=in_specs,
            out_specs=tuple(spec for _, spec in outs),
            scratch_shapes=list(scratch),
        ),
        out_shape=tuple(shape for shape, _ in outs),
        compiler_params=pltpu.CompilerParams(
            vmem_limit_bytes=VMEM_LIMIT, dimension_semantics=("arbitrary",) * len(grid)
        ),
        cost_estimate=pl.CostEstimate(
            flops=micros * 10_000_000_000, bytes_accessed=micros * 10_000_000, transcendentals=0
        ),
    )(*operands)


def whole(shape):
    return pl.BlockSpec(shape, lambda i, *_: (0,) * len(shape))


def rows_of(count, width):
    return pl.BlockSpec((count, width), lambda i, *_: (i, 0))


def cols_of(height, count):
    return pl.BlockSpec((height, count), lambda i, *_: (0, i))


def struct(shape, dtype):
    return jax.ShapeDtypeStruct(shape, dtype)


def dot(left, right):
    return jnp.dot(left, right, preferred_element_type=F32)


def contract_rows(left, right):
    return lax.dot_general(left, right, (((0,), (0,)), ((), ())), preferred_element_type=F32)


def contract_cols(left, right):
    return lax.dot_general(left, right, (((1,), (1,)), ((), ())), preferred_element_type=F32)


def normalize(total):
    centered = total - jnp.mean(total, axis=-1, keepdims=True)
    variance = jnp.mean(centered * centered, axis=-1, keepdims=True)
    scale_inv = lax.rsqrt(variance + LN_EPS)
    return (centered * scale_inv, scale_inv)


def normalize_back(upstream, normed, scale_inv, gain):
    scaled = upstream * gain
    return scale_inv * (
        scaled
        - jnp.mean(scaled, axis=-1, keepdims=True)
        - normed * jnp.mean(scaled * normed, axis=-1, keepdims=True)
    )


def gelu_and_slope(pre):
    below = 0.5 + 0.5 * lax.erf(pre * 0.5**0.5)
    return pre * below, below + pre * jnp.exp(pre * pre * -0.5) * (2 * jnp.pi) ** -0.5


def two_heads(block, lane_low):
    zero = jnp.zeros_like(block)
    return jnp.concatenate([jnp.where(lane_low, block, zero), jnp.where(lane_low, zero, block)], 0)


def lane_is_low(rows):
    return lax.broadcasted_iota(jnp.int32, (rows, PAIR_LANES), 1) < HD


def column_sum(value):
    return jnp.sum(value, axis=0, keepdims=True)


def fetches(order_ref, own_ref, other_ref, target, sems, rows, width, start=0, lane=0):
    core = order_ref[4, 0]
    copies = []
    for b in range(sems.shape[0]):
        pair = []
        for side, ref in enumerate((own_ref, other_ref)):
            half = core if side == 0 else 1 - core
            pair.append(
                pltpu.make_async_copy(
                    ref.at[order_ref[2 + side, b], :, pl.ds(lane, width)],
                    target.at[pl.ds(b * rows, rows), pl.ds(pl.multiple_of(start + half * width, LANES), width)],
                    sems.at[b, side],
                )
            )
        copies.append(pair)
    return copies


def begin(copies):
    for pair in copies:
        for copy in pair:
            copy.start()


def finish(copies):
    for pair in copies:
        for copy in pair:
            copy.wait()


def in_turn(count, *stages):
    held = stages[0](0)
    for n in range(count):
        value, held = held, stages[0](n + 1) if n + 1 < count else None
        for stage in stages[1:]:
            value = stage(n, value)


def projection_forward(order, tokens, own, other, affine_rows, after=()):
    rows, width = tokens.shape
    half = width // 2
    chips, block = own.shape[0], own.shape[1]

    def kernel(
        order_ref, tokens_ref, own_ref, other_ref, w_ref, proj_ref, affine_ref, out_ref, columns, sems, column_sems
    ):
        step = pl.program_id(0)
        params = [
            pltpu.make_async_copy(
                own_ref.at[order_ref[2, b], :, pl.ds(4 * half, LANES)],
                columns.at[pl.ds(b * block, block), :],
                column_sems.at[b],
            )
            for b in range(chips)
        ]
        parts = [
            fetches(order_ref, own_ref, other_ref, w_ref, sems.at[k], block, half, k * width, k * half)
            for k in range(3)
        ]
        parts.append(fetches(order_ref, own_ref, other_ref, proj_ref, sems.at[3], block, half, 0, 3 * half))

        @pl.when(step == 0)
        def _():
            for copy in params:
                copy.start()
            for copies in parts:
                begin(copies)
            for copy in params:
                copy.wait()
            affine_ref[...] = columns[...].astype(F32).T[:affine_rows]

        for k in range(3):

            @pl.when(step == k)
            def _():
                finish(parts[k])
                for n in range(width // TILE):
                    cols = slice(n * TILE, (n + 1) * TILE)
                    value = dot(tokens_ref[...], w_ref[:, k * width + n * TILE : k * width + (n + 1) * TILE])
                    if k != 1:
                        value += affine_ref[4 + k // 2 : 5 + k // 2, cols]
                    out_ref[:, cols] = value.astype(BF16)

        @pl.when(step == 2)
        def _():
            finish(parts[3])

    return call(
        kernel,
        (3,),
        [(tokens, whole(tokens.shape)), (own, ANY), (other, ANY)],
        [
            (struct((width, 3 * width), BF16), whole((width, 3 * width))),
            (struct((width, width), BF16), whole((width, width))),
            (struct((affine_rows, width), F32), whole((affine_rows, width))),
            (struct((rows, 3 * width), BF16), cols_of(rows, width)),
        ],
        [
            pltpu.VMEM((width, LANES), BF16),
            pltpu.SemaphoreType.DMA((4, chips, 2)),
            pltpu.SemaphoreType.DMA((chips,)),
        ],
        8,
        after,
        order,
    )


def attention_forward(tokens, projected, proj_w, affine, after=()):
    rows, width = tokens.shape
    spans, pairs = rows // L, width // PAIR_LANES
    each = PART // L

    def kernel(
        tokens_ref, projected_ref, proj_ref, affine_ref,
        attention_ref, context_ref, normed_ref, inv_ref, skip_ref,
    ):
        lane_low = lane_is_low(L)

        def read(n, part):
            s, p = divmod(n, pairs)
            at = part * width + p * PAIR_LANES
            return projected_ref[s * L : (s + 1) * L, at : at + PAIR_LANES]

        def scored(n):
            return contract_cols(two_heads(read(n, 0) * jnp.asarray(HD**-0.5, BF16), lane_low), read(n, 1))

        def weighed(n, scores):
            s, p = divmod(n, pairs)
            exponent = jnp.exp(scores - jnp.max(scores, axis=-1, keepdims=True))
            low = (exponent * (1.0 / jnp.sum(exponent, axis=-1, keepdims=True))).astype(BF16)
            attention_ref[s, p] = low
            both = dot(low, read(n, 2))
            context_ref[s * L : (s + 1) * L, p * PAIR_LANES : (p + 1) * PAIR_LANES] = jnp.where(
                lane_low, both[:L], both[L:]
            ).astype(BF16)

        in_turn(each * pairs, scored, weighed)
        total = dot(context_ref[...], proj_ref[...]) + affine_ref[6:7, :]
        normed, inv = normalize(tokens_ref[...].astype(F32) + total)
        normed_ref[...] = normed
        inv_ref[...] = jnp.broadcast_to(inv, (PART, LANES))
        skip_ref[...] = (normed * affine_ref[0:1, :] + affine_ref[1:2, :]).astype(BF16)

    return call(
        kernel,
        (rows // PART,),
        [
            (tokens, rows_of(PART, width)),
            (projected, rows_of(PART, 3 * width)),
            (proj_w, whole(proj_w.shape)),
            (affine, whole(affine.shape)),
        ],
        [
            (
                struct((spans, pairs, 2 * L, L), BF16),
                pl.BlockSpec((each, pairs, 2 * L, L), lambda i, *_: (i, 0, 0, 0)),
            ),
            (struct((rows, width), BF16), rows_of(PART, width)),
            (struct((rows, width), F32), rows_of(PART, width)),
            (struct((rows, LANES), F32), rows_of(PART, LANES)),
            (struct((rows, width), BF16), rows_of(PART, width)),
        ],
        (),
        12,
        after,
    )


def inner_forward(order, side, skip_low, blocks, affine, after=()):
    rows, width = skip_low.shape
    chips, block, half = blocks.shape

    def kernel(order_ref, skip_ref, blocks_ref, affine_ref, w_ref, act_ref, slope_ref, sems):
        step = pl.program_id(0)

        def copies(b):
            return pltpu.make_async_copy(
                blocks_ref.at[order_ref[2 + side, b]], w_ref.at[pl.ds(b * block, block), :], sems.at[b]
            )

        @pl.when(step == 0)
        def _():
            for b in range(chips):
                copies(b).start()
            for b in range(chips):
                copies(b).wait()

        first = order_ref[4, 0] if side == 0 else 1 - order_ref[4, 0]
        bias = affine_ref[pl.ds(8 + first * (half // width) + step, 1), :]
        parts = rows // PART

        def entered(n):
            k, r = divmod(n, parts)
            weight = w_ref[:, pl.ds(pl.multiple_of(step * width + k * TILE, LANES), TILE)]
            return dot(skip_ref[r * PART : (r + 1) * PART, :], weight)

        def activated(n, value):
            k, r = divmod(n, parts)
            at, cols = slice(r * PART, (r + 1) * PART), slice(k * TILE, (k + 1) * TILE)
            act, slope = gelu_and_slope(value + bias[:, cols])
            act_ref[at, cols] = act.astype(BF16)
            slope_ref[at, cols] = slope.astype(BF16)

        in_turn(width // TILE * parts, entered, activated)

    return call(
        kernel,
        (half // width,),
        [(skip_low, whole(skip_low.shape)), (blocks, ANY), (affine, whole(affine.shape))],
        [
            (struct((width, half), BF16), whole((width, half))),
            (struct((rows, half), BF16), cols_of(rows, width)),
            (struct((rows, half), BF16), cols_of(rows, width)),
        ],
        [pltpu.SemaphoreType.DMA((chips,))],
        10,
        after,
        order,
    )


def outer_forward(order, act_own, act_other, own, other, normed_one, affine, mlm_grad, live_rows, after=()):
    rows, wide = act_own.shape
    hidden, width = 2 * wide, normed_one.shape[1]
    chips, block = own.shape[0], own.shape[1]
    spans = rows // L
    many = 2
    tile = many * PART

    def kernel(
        order_ref, act_own_ref, act_other_ref, own_ref, other_ref, normed_one_ref, affine_ref, mlm_ref, live_ref,
        w_ref, out_ref, grad_ref, low_ref, sums_ref, cls_ref, cls_normed_ref, cls_inv_ref, sems,
    ):
        step = pl.program_id(0)

        core = order_ref[4, 0]

        def entered(n):
            at = slice(n * PART, (n + 1) * PART)
            total = 0.0
            for k, ref in enumerate((act_own_ref, act_other_ref)):
                start = (core if k == 0 else 1 - core) * wide
                total = total + dot(ref[at, :], w_ref[pl.ds(pl.multiple_of(start, LANES), wide), :])
            return total

        def ended(n, total):
            at = slice(n * PART, (n + 1) * PART)
            skip = normed_one_ref[at, :] * affine_ref[0:1, :] + affine_ref[1:2, :]
            normed, inv = normalize(skip + (total + affine_ref[7:8, :]))
            out = (normed * affine_ref[2:3, :] + affine_ref[3:4, :]).astype(BF16)
            out_ref[at, :] = out
            line = lax.broadcasted_iota(jnp.int32, (PART, 1), 0)
            live = line < live_ref[0] - (step * many + n) * PART
            upstream = jnp.where(live, mlm_ref[at, :].astype(F32), 0.0)
            grad = normalize_back(upstream, normed, inv, affine_ref[2:3, :])
            grad_ref[at, :] = grad
            low_ref[at, :] = grad.astype(BF16)
            for k, value in enumerate((upstream * normed, upstream, grad)):
                sums_ref[k : k + 1, :] += column_sum(value)
            for s in range(PART // L):
                row, to = slice(s * L, s * L + 1), pl.ds((step * many + n) * (PART // L) + s, 1)
                cls_ref[to, :] = out[s * L : s * L + 16].astype(F32)[:1]
                cls_normed_ref[to, :] = normed[row]
                cls_inv_ref[to, :] = jnp.broadcast_to(inv[row], (1, LANES))

        copies = fetches(order_ref, own_ref, other_ref, w_ref, sems, block, width // 2)

        @pl.when(step == 0)
        def _():
            begin(copies)
            sums_ref[...] = jnp.zeros_like(sums_ref)
            finish(copies)

        in_turn(many, entered, ended)

    return call(
        kernel,
        (rows // tile,),
        [
            (act_own, rows_of(tile, wide)),
            (act_other, rows_of(tile, wide)),
            (own, ANY),
            (other, ANY),
            (normed_one, rows_of(tile, width)),
            (affine, whole(affine.shape)),
            (mlm_grad, rows_of(tile, width)),
            (live_rows, SMEM),
        ],
        [
            (struct((hidden, width), BF16), whole((hidden, width))),
            (struct((rows, width), BF16), rows_of(tile, width)),
            (struct((rows, width), F32), rows_of(tile, width)),
            (struct((rows, width), BF16), rows_of(tile, width)),
            (struct((8, width), F32), whole((8, width))),
            (struct((spans, width), F32), whole((spans, width))),
            (struct((spans, width), F32), whole((spans, width))),
            (struct((spans, LANES), F32), whole((spans, LANES))),
        ],
        [pltpu.SemaphoreType.DMA((chips, 2))],
        8,
        after,
        order,
    )


def loss_and_gradient(own, other, match, key_live, anchor_live):
    scale = own.shape[1] ** -0.5
    sims = contract_cols(own.astype(BF16), other.astype(BF16)) * scale
    step = jnp.zeros_like(sims)
    loss = None
    for axis, live in ((1, key_live), (0, anchor_live)):
        masked = jnp.where(live > 0, sims, -1000000000.0)
        peak = jnp.max(masked, axis=axis, keepdims=True)
        weights = jnp.where(live > 0, jnp.exp(masked - peak), 0.0)
        total = jnp.sum(weights, axis=axis, keepdims=True)
        active = jnp.max(match, axis=axis, keepdims=True)
        step += active * (weights / total - match)
        if loss is None:
            hit = jnp.sum(match * sims, axis=axis, keepdims=True)
            loss = jnp.sum(jnp.where(active > 0, peak + jnp.log(total) - hit, 0.0), axis=0, keepdims=True)
    step *= LOSS_WEIGHT * scale
    gradient = jnp.zeros_like(own)
    for k in range(other.shape[0]):
        gradient += step[:, k : k + 1] * other[k : k + 1, :]
    return loss, gradient


def outer_backward(order, grad_low, sums, cls, cls_other, masks, cls_normed, cls_inv, act_own, act_other, affine, after=()):
    rows, width = grad_low.shape
    hidden = 2 * act_own.shape[1]
    chips = order.shape[1]
    block, half = hidden // chips, width // 2
    tile = 4 * block
    turn = chips // 8
    spans = rows // L

    def kernel(
        order_ref, low_in_ref, sums_in_ref, cls_ref, cls_other_ref, masks_ref, normed_ref, inv_ref, act_own_ref, act_other_ref, affine_ref,
        low_ref, more_ref, sums_ref, loss_ref, own_ref, other_ref, own_held, other_held, sems,
    ):
        step = pl.program_id(0)

        @pl.when(step == 0)
        def _():
            loss, up = loss_and_gradient(
                cls_ref[...], cls_other_ref[...], masks_ref[0], masks_ref[1], masks_ref[2]
            )
            normed = normed_ref[...]
            more = normalize_back(up, normed, inv_ref[:, :1], affine_ref[2:3, :])
            more_ref[...] = more
            loss_ref[...] = jnp.broadcast_to(loss, loss_ref.shape)
            for k, value in enumerate((up * normed, up, more)):
                sums_ref[k : k + 1, :] = sums_in_ref[k : k + 1, :] + column_sum(value)
            low_ref[...] = low_in_ref[...]
            line = lax.broadcasted_iota(jnp.int32, (16, 1), 0)
            for s in range(spans):
                at = slice(s * L, s * L + 16)
                changed = low_in_ref[at, :].astype(F32) + jnp.where(line == 0, more[s : s + 1], 0.0)
                low_ref[at, :] = changed.astype(BF16)

        core = order_ref[4, 0]

        def gradient(act_ref, first):
            def entered(n):
                return contract_rows(act_ref[:, n * 2 * block : (n + 1) * 2 * block], low_ref[...])

            def ended(n, value):
                low, high = value[:, :half], value[:, half:]
                parts = (jnp.where(core == 0, low, high), jnp.where(core == 0, high, low))
                for side, (part, held, out) in enumerate(
                    zip(parts, (own_held, other_held), (own_ref, other_ref))
                ):
                    for k in range(2):
                        b = first + 2 * n + k
                        held[b] = part[k * block : (k + 1) * block].astype(BF16)
                        pltpu.make_async_copy(
                            held.at[b], out.at[order_ref[2 + side, b]], sems.at[side, b]
                        ).start()

            in_turn(2, entered, ended)

        @pl.when(step < turn)
        def _():
            gradient(act_own_ref, core * (chips // 2) + 4 * step)

        @pl.when(step >= turn)
        def _():
            gradient(act_other_ref, (1 - core) * (chips // 2) + 4 * (step - turn))

        @pl.when(step == 2 * turn - 1)
        def _():
            for side, (held, out) in enumerate(((own_held, own_ref), (other_held, other_ref))):
                for b in range(chips):
                    pltpu.make_async_copy(
                        held.at[b], out.at[order_ref[2 + side, b]], sems.at[side, b]
                    ).wait()

    shape = (chips, block, half)
    return call(
        kernel,
        (hidden // tile,),
        [
            (grad_low, whole(grad_low.shape)),
            (sums, whole(sums.shape)),
            (cls, whole(cls.shape)),
            (cls_other, whole(cls.shape)),
            (masks, whole(masks.shape)),
            (cls_normed, whole(cls.shape)),
            (cls_inv, whole(cls_inv.shape)),
            (act_own, pl.BlockSpec((rows, tile), lambda i, *_: (0, jnp.minimum(i, turn - 1)))),
            (act_other, pl.BlockSpec((rows, tile), lambda i, *_: (0, jnp.maximum(i - turn, 0)))),
            (affine, whole(affine.shape)),
        ],
        [
            (struct((rows, width), BF16), whole((rows, width))),
            (struct((spans, width), F32), whole((spans, width))),
            (struct((8, width), F32), whole((8, width))),
            (struct((8, LANES), F32), whole((8, LANES))),
            (struct(shape, BF16), ANY),
            (struct(shape, BF16), ANY),
        ],
        [
            pltpu.VMEM(shape, BF16),
            pltpu.VMEM(shape, BF16),
            pltpu.SemaphoreType.DMA((2, chips)),
        ],
        8,
        after,
        order,
    )


def inner_backward(order, side, low, slope, outer_w, skip_low, after=()):
    rows, width = low.shape
    hidden = 2 * slope.shape[1]
    chips = order.shape[1]
    block = width // chips
    steps = hidden // 2 // width

    def kernel(order_ref, low_ref, slope_ref, outer_ref, skip_ref, inner_ref, bias_ref, out_ref):
        step = pl.program_id(0)

        def entered(n):
            return contract_cols(low_ref[...], outer_ref[n * TILE : (n + 1) * TILE, :])

        def sloped(n, value):
            cols = slice(n * TILE, (n + 1) * TILE)
            inner_grad = value * slope_ref[:, cols].astype(F32)
            bias_ref[pl.ds(step, 1), cols] = column_sum(inner_grad)
            inner_low = inner_grad.astype(BF16)
            inner_ref[:, cols] = inner_low
            return contract_rows(skip_ref[...], inner_low).astype(BF16)

        def stored(n, value):
            for b in range(chips):
                out_ref[order_ref[2 + side, b], :, n * TILE : (n + 1) * TILE] = value[b * block : (b + 1) * block]

        in_turn(width // TILE, entered, sloped, stored)

    def place(i, table):
        half = table[4, 0] if side == 0 else 1 - table[4, 0]
        return half * steps + i

    return call(
        kernel,
        (steps,),
        [
            (low, whole(low.shape)),
            (slope, cols_of(rows, width)),
            (outer_w, pl.BlockSpec((width, width), lambda i, table: (place(i, table), 0))),
            (skip_low, whole(skip_low.shape)),
        ],
        [
            (struct((rows, hidden // 2), BF16), cols_of(rows, width)),
            (struct((8, width), F32), whole((8, width))),
            (
                struct((chips, block, hidden // 2), BF16),
                pl.BlockSpec((chips, block, width), lambda i, *_: (0, 0, i)),
            ),
        ],
        (),
        8,
        after,
        order,
    )


def skip_backward(inner_own, inner_other, w_own, w_other, grad_two, more, normed_one, inv_one, affine, proj_w, after=()):
    rows, width = grad_two.shape
    half = w_own.shape[1]
    many = 2
    tile = many * PART

    def kernel(
        own_ref, other_ref, w_own_ref, w_other_ref, grad_two_ref, more_ref, normed_ref, inv_ref, affine_ref, proj_ref,
        grad_ref, low_ref, sums_ref, context_ref,
    ):
        step = pl.program_id(0)

        @pl.when(step == 0)
        def _():
            sums_ref[...] = jnp.zeros_like(sums_ref)

        def entered(n):
            at = slice(n * PART, (n + 1) * PART)
            up = grad_two_ref[at, :]
            for ref, weight in ((own_ref, w_own_ref), (other_ref, w_other_ref)):
                up = up + contract_cols(ref[at, :], weight[...])
            return up

        def ended(n, up):
            at = slice(n * PART, (n + 1) * PART)
            line = lax.broadcasted_iota(jnp.int32, (PART, 1), 0)
            for s in range(PART // L):
                row = pl.ds((step * many + n) * (PART // L) + s, 1)
                up = up + jnp.where(line == s * L, more_ref[row, :], 0.0)
            normed = normed_ref[at, :]
            grad = normalize_back(up, normed, inv_ref[at, :1], affine_ref[0:1, :])
            grad_ref[at, :] = grad
            low = grad.astype(BF16)
            low_ref[at, :] = low
            for k, value in enumerate((up * normed, up, grad)):
                sums_ref[k : k + 1, :] += column_sum(value)
            context_ref[at, :] = contract_cols(low, proj_ref[...]).astype(BF16)

        in_turn(many, entered, ended)

    return call(
        kernel,
        (rows // tile,),
        [
            (inner_own, rows_of(tile, half)),
            (inner_other, rows_of(tile, half)),
            (w_own, whole(w_own.shape)),
            (w_other, whole(w_other.shape)),
            (grad_two, rows_of(tile, width)),
            (more, whole(more.shape)),
            (normed_one, rows_of(tile, width)),
            (inv_one, rows_of(tile, LANES)),
            (affine, whole(affine.shape)),
            (proj_w, whole(proj_w.shape)),
        ],
        [
            (struct((rows, width), F32), rows_of(tile, width)),
            (struct((rows, width), BF16), rows_of(tile, width)),
            (struct((8, width), F32), whole((8, width))),
            (struct((rows, width), BF16), rows_of(tile, width)),
        ],
        (),
        8,
        after,
    )


def attention_backward(pairs, context_grad, projected, attention, after=()):
    rows, width = context_grad.shape
    spans, count = rows // L, len(pairs)
    wide = 3 * count * PAIR_LANES
    each = 2

    def kernel(grad_ref, projected_ref, attention_ref, out_ref, sums_ref):
        @pl.when(pl.program_id(0) == 0)
        def _():
            sums_ref[...] = jnp.zeros_like(sums_ref)

        lane_low = lane_is_low(L)
        def entered(m):
            s, n = divmod(m, count)
            at, line = pairs[n] * PAIR_LANES, slice(s * L, (s + 1) * L)
            grads = two_heads(grad_ref[line, at : at + PAIR_LANES], lane_low)
            v = projected_ref[line, 2 * width + at : 2 * width + at + PAIR_LANES]
            return grads, contract_cols(grads, v)

        def ended(m, value):
            s, n = divmod(m, count)
            at, line = pairs[n] * PAIR_LANES, slice(s * L, (s + 1) * L)
            q, k = (
                projected_ref[line, part * width + at : part * width + at + PAIR_LANES] for part in range(2)
            )
            grads, back = value
            low = attention_ref[s, pairs[n]]
            weights = low.astype(F32)
            product = back * weights
            score = (product - weights * jnp.sum(product, axis=-1, keepdims=True)) * HD**-0.5
            score_low = score.astype(BF16)
            both = dot(score_low, k)
            parts = (
                jnp.where(lane_low, both[:L], both[L:]),
                contract_rows(score_low, two_heads(q, lane_low)),
                contract_rows(low, grads),
            )
            for part, value in enumerate(parts):
                to = slice((part * count + n) * PAIR_LANES, (part * count + n + 1) * PAIR_LANES)
                out_ref[line, to] = value.astype(BF16)
                sums_ref[:, to] += column_sum(value)

        in_turn(each * count, entered, ended)

    return call(
        kernel,
        (spans // each,),
        [
            (context_grad, rows_of(each * L, width)),
            (projected, rows_of(each * L, 3 * width)),
            (attention, pl.BlockSpec((each, width // PAIR_LANES, 2 * L, L), lambda i, *_: (i, 0, 0, 0))),
        ],
        [
            (struct((rows, wide), BF16), rows_of(each * L, wide)),
            (struct((1, wide), F32), whole((1, wide))),
        ],
        (),
        3 * count,
        after,
    )


def store_blocks(order_ref, low, high, rows, own_ref, other_ref, lane):
    core = order_ref[4, 0]
    own = jnp.where(core == 0, low, high).astype(BF16)
    other = jnp.where(core == 0, high, low).astype(BF16)
    width = low.shape[1]
    for b in range(low.shape[0] // rows):
        at = slice(b * rows, (b + 1) * rows)
        own_ref[order_ref[2, b], :, lane : lane + width] = own[at]
        other_ref[order_ref[3, b], :, lane : lane + width] = other[at]


def qkv_backward(order, tokens, qkv_low, proj=None, sums=None, after=()):
    rows, width = tokens.shape
    chips = order.shape[1]
    block, half = width // chips, width // 2
    each = qkv_low.shape[1] // 6
    extra = half if proj is not None else LANES

    def affine_rows(sums_one, sums_two, first, second, bias_own, bias_other, lines, core):
        lines[...] = jnp.zeros_like(lines)
        lines[0:2, :] = sums_one[0:2, :]
        lines[2:4, :] = sums_two[0:2, :]
        for row, part in ((4, 0), (5, 2)):
            for h in range(2):
                at = h * half
                for ref in (first, second):
                    wide = ref.shape[1] // 6
                    lines[row : row + 1, at : at + wide] = ref[:, (2 * part + h) * wide : (2 * part + h + 1) * wide]
                    at += wide
        lines[6:7, :] = sums_one[2:3, :]
        lines[7:8, :] = sums_two[2:3, :]
        lines[8:10, :] = jnp.where(core == 0, bias_own[0:2, :], bias_other[0:2, :])
        lines[10:12, :] = jnp.where(core == 0, bias_other[0:2, :], bias_own[0:2, :])
        return lines[...].T

    def kernel(order_ref, tokens_ref, qkv_ref, *rest):
        rest, (own_ref, other_ref, lines) = rest[:-3], rest[-3:]

        def entered(k):
            if k < 3:
                return contract_rows(tokens_ref[...], qkv_ref[:, 2 * k * each : 2 * (k + 1) * each])
            if proj is not None:
                return contract_rows(rest[0][...], rest[1][...])
            value = affine_rows(*rest, lines, order_ref[4, 0])
            return jnp.concatenate([value, value], axis=1)

        def ended(k, value):
            middle = value.shape[1] // 2
            store_blocks(order_ref, value[:, :middle], value[:, middle:], block, own_ref, other_ref, k * each)

        in_turn(4, entered, ended)

    shape = (chips, block, 3 * each + extra)
    more = list(proj if proj is not None else sums)
    return call(
        kernel,
        (1,),
        [(array, whole(array.shape)) for array in (tokens, qkv_low, *more)],
        [(struct(shape, BF16), whole(shape)), (struct(shape, BF16), whole(shape))],
        [pltpu.VMEM((LANES, width), F32)],
        5,
        after,
        order,
    )


def tokens_backward(groups, qkv_lows, qkv_w, grad_one, after=()):
    rows, width = grad_one.shape

    def kernel(*refs):
        lows, (w_ref, grad_ref, out_ref, held) = refs[: len(groups)], refs[len(groups) :]
        for pairs, ref in zip(groups, lows):
            for part in range(3):
                for n, p in enumerate(pairs):
                    held[:, part * width + p * PAIR_LANES : part * width + (p + 1) * PAIR_LANES] = ref[
                        :, (part * len(pairs) + n) * PAIR_LANES : (part * len(pairs) + n + 1) * PAIR_LANES
                    ]
        out_ref[...] = contract_cols(held[...], w_ref[...]) + grad_ref[...]

    return call(
        kernel,
        (rows // PART,),
        [(low, rows_of(PART, low.shape[1])) for low in qkv_lows]
        + [(qkv_w, whole(qkv_w.shape)), (grad_one, rows_of(PART, width))],
        [(struct((rows, width), F32), rows_of(PART, width))],
        [pltpu.VMEM((PART, 3 * width), BF16)],
        8,
        after,
    )[0]


def summed(order, chunks, doubled=(), loss=None, before=None):
    counts = [len(parts) for parts in chunks]
    shapes = [(parts[0].shape[1] // 2, parts[0].shape[2]) for parts in chunks]
    extras = [loss] if loss is not None else []
    extras += [before] if before is not None else []
    arrays = [p for parts in chunks for p in parts]

    def kernel(order_ref, *refs):
        core = order_ref[4, 0]
        squares = 0.0
        outs = refs[len(arrays) + len(extras) :]
        at = 0
        for n, count in enumerate(counts):
            rows, cols = shapes[n]
            total = sum(ref[0].astype(F32) for ref in refs[at : at + count])
            at += count
            first, second = total[:rows], total[rows:]
            mine, theirs = jnp.where(core == 0, first, second), jnp.where(core == 0, second, first)
            outs[2 * n][...] = mine
            outs[2 * n + 1][...] = theirs
            squares += jnp.sum(mine * mine)
            theirs = theirs[:, : cols - LANES] if n in doubled else theirs
            squares += jnp.sum(theirs * theirs)
        line = lax.broadcasted_iota(jnp.int32, (8, LANES), 0)
        result = jnp.where(line == 0, squares, 0.0)
        if loss is not None:
            result += jnp.where(line == 1, refs[len(arrays)][0:1, :], 0.0)
        if before is not None:
            result += refs[len(arrays) + len(extras) - 1][...]
        outs[-1][...] = result

    return call(
        kernel,
        (1,),
        [(p, pl.BlockSpec((1, *p.shape[1:]), lambda i, *_: (0, 0, 0))) for p in arrays]
        + [(x, whole(x.shape)) for x in extras],
        [(struct(s, F32), whole(s)) for s in shapes for _ in range(2)]
        + [(struct((8, LANES), F32), whole((8, LANES)))],
        (),
        2,
        (),
        order,
    )


def adamw(order, totals, grads, weights, moments, squares, slots):
    count = len(weights)
    shapes = [w.shape for w in weights]
    rates = (RATE_MATRIX,) * (count - 1) + (RATE_AFFINE,)
    decays = (DECAY_MATRIX,) * (count - 1) + (DECAY_AFFINE,)

    def kernel(order_ref, totals_ref, *refs):
        core = order_ref[4, 0]
        grad_refs, refs = refs[: len(grads)], refs[len(grads) :]
        olds, outs = refs[: 3 * count], refs[3 * count :]
        norm = jnp.sqrt(totals_ref[0:1, :])
        outs[-1][...] = jnp.concatenate([norm, totals_ref[1:2, :] / slots, jnp.zeros((6, LANES), F32)], 0)
        factor = jnp.minimum(1.0, CLIP_NORM / (norm[:, 0:1] + 1e-06))

        def update(n, at, gradient):
            master, moment, square = (olds[3 * n + k][at] for k in range(3))
            clipped = gradient * factor
            moment = BETA_ONE * moment + (1.0 - BETA_ONE) * clipped
            square = BETA_TWO * square + (1.0 - BETA_TWO) * clipped * clipped
            mean_hat = moment / (1.0 - BETA_ONE**STEP)
            square_hat = square / (1.0 - BETA_TWO**STEP)
            master = master - rates[n] * (mean_hat / (jnp.sqrt(square_hat) + ADAM_EPS) + decays[n] * master)
            for k, value in enumerate((master, moment, square)):
                outs[3 * n + k][at] = value

        def pieces(n, start, chunk, lane, width):
            mine, got = grad_refs[2 * chunk], grad_refs[2 * chunk + 1]
            for h in range(2):
                first, second = mine[:, lane : lane + width], got[:, lane : lane + width]
                value = jnp.where(core == h, first, second)
                update(n, (slice(None), slice(start[h], start[h] + width)), value)

        width = shapes[0][1] // 3
        half = width // 2
        each = half // 3
        for k in range(3):
            at = k * width
            pieces(0, (at, at + half), 3, k * each, each)
            pieces(0, (at + each, at + half + each), 2, 2 * k * each, 2 * each)
        pieces(1, (0, half), 2, 6 * each, half)
        pieces(2, (0, shapes[2][1] // 2), 1, 0, shapes[2][1] // 2)
        pieces(3, (0, half), 0, 0, half)
        update(4, (slice(None), slice(None)), grad_refs[-1][...])

    olds = [array for n in range(count) for array in (weights[n], moments[n], squares[n])]
    return call(
        kernel,
        (1,),
        [(a, whole(a.shape)) for a in (totals, *grads, *olds)],
        [(struct(s, F32), whole(s)) for s in shapes for _ in range(3)]
        + [(struct((8, LANES), F32), whole((8, LANES)))],
        (),
        4,
        (),
        order,
    )


def body(
    tokens,
    mlm_grad,
    doc_ids,
    span_counts,
    qkv_weight,
    proj_weight,
    inner_weight,
    outer_weight,
    affine_params,
    qkv_moment,
    proj_moment,
    inner_moment,
    outer_moment,
    affine_moment,
    qkv_square,
    proj_square,
    inner_square,
    outer_square,
    affine_square,
):
    rows, width = tokens.shape
    spans = rows // L
    half = width // 2
    order = block_order()
    hidden = inner_weight.shape[1]
    pairs = width // PAIR_LANES
    affine_rows = affine_params.shape[0]
    affine_cols = jnp.pad(affine_params.astype(BF16).T, ((0, 0), (0, LANES - affine_rows)))
    block_one = chip_rows(
        jnp.concatenate([qkv_weight.astype(BF16), proj_weight.astype(BF16)], 1), (half,) * 4, affine_cols
    )
    block_two = chip_rows(inner_weight.astype(BF16), (hidden // 2,))
    block_three = chip_rows(outer_weight.astype(BF16), (half,))
    rows_chip, rows_outer = block_one.shape[0], block_three.shape[0]
    table = kernel_order(order, rows_chip)

    side = lax.axis_index("pair")
    own_ids, other_ids = pick(side, doc_ids[0], doc_ids[1]), pick(side, doc_ids[1], doc_ids[0])
    own_count, other_count = (
        pick(side, span_counts[0], span_counts[1]),
        pick(side, span_counts[1], span_counts[0]),
    )
    slot = jnp.arange(spans)
    anchor_live = jnp.broadcast_to((slot < own_count)[:, None], (spans, spans))
    key_live = jnp.broadcast_to((slot < other_count)[None, :], (spans, spans))
    match = (own_ids[:, None] == other_ids[None, :]) & anchor_live & key_live
    masks = jnp.stack([match, key_live, anchor_live]).astype(F32)
    live_rows = (own_count * L)[None]

    one, two, three = Gather(block_one), Gather(block_two), Gather(block_three)
    one.step()
    first = one.step()
    one.step()
    two.step(first)
    second = (one.got, two.got)
    one.step(*second)
    two.step(*second)
    three.step(*second)
    third = (one.got, two.got, three.got)
    own, other = one.finish(order, rows_chip, *third)
    two.step(*third)
    three.step(*third)
    fourth = (two.got, three.got)
    two.step(*fourth, other)
    qkv_w, proj_w, affine, projected = projection_forward(table, tokens, own, other, affine_rows)
    three.step(two.got, projected)
    attention, context, normed_one, inv_one, skip_low = attention_forward(tokens, projected, proj_w, affine)
    own, other = two.finish(order, rows_chip)
    three.step(skip_low)
    w_own, act_own, slope_own = inner_forward(table, 0, skip_low, own, affine)
    w_other, act_other, slope_other = inner_forward(table, 1, skip_low, other, affine)
    own, other = three.finish(order, rows_outer, act_own)
    outer_w, layer_out, grad_two, low, sums_two, cls, cls_normed, cls_inv = outer_forward(
        table, act_own, act_other, own, other, normed_one, affine, mlm_grad, live_rows
    )
    low, more, sums_two, loss, own, other = outer_backward(
        table, low, sums_two, cls, core_swapped(cls), masks, cls_normed, cls_inv, act_own, act_other, affine
    )

    red_outer = Reduce(*in_order(order, own, other, rows_outer))
    inner_other, bias_other, blocks_other = inner_backward(table, 1, low, slope_other, outer_w, skip_low)
    got = red_outer.last()
    inner_own, bias_own, blocks_own = inner_backward(table, 0, low, slope_own, outer_w, skip_low, (got,))
    red_outer.step()
    red_inner = Reduce(*in_order(order, blocks_own, blocks_other, rows_chip))
    grad_one, grad_one_low, sums_one, context_grad = skip_backward(
        inner_own, inner_other, w_own, w_other, grad_two, more, normed_one, inv_one, affine, proj_w,
        (red_inner.last(),),
    )
    groups = (
        tuple(p for p in range(pairs) if p % (pairs // 2)),
        tuple(p for p in range(pairs) if not p % (pairs // 2)),
    )
    qkv_low, qkv_sums = [None, None], [None, None]
    qkv_low[0], qkv_sums[0] = attention_backward(
        groups[0], context_grad, projected, attention, (red_outer.last(),)
    )
    red_outer.step()
    red_inner.step()
    own, other = qkv_backward(
        table, tokens, qkv_low[0], (context, grad_one_low), None, (red_outer.last(),)
    )
    red_first = Reduce(*in_order(order, own, other, rows_chip))
    red_outer.step()
    qkv_low[1], qkv_sums[1] = attention_backward(
        groups[1], context_grad, projected, attention, (red_inner.last(), red_outer.last(), red_first.last())
    )
    red_first.step()
    red_inner.step()
    own, other = qkv_backward(
        table, tokens, qkv_low[1], None, (sums_one, sums_two, qkv_sums[1], qkv_sums[0], bias_own, bias_other)
    )
    red_second = Reduce(*in_order(order, own, other, rows_chip))
    red_second.step()
    input_grad = tokens_backward(groups, qkv_low, qkv_w, grad_one)
    red_second.step(input_grad)
    outer_mine, outer_theirs, inner_mine, inner_theirs, squares = summed(
        table, (red_outer.finish(), red_inner.finish())
    )
    first_mine, first_theirs, second_mine, second_theirs, squares = summed(
        table, (red_first.finish(), red_second.finish()), (1,), loss, squares
    )
    totals = total_over_devices(squares)
    grads = []
    for mine, theirs in (
        (outer_mine, outer_theirs),
        (inner_mine, inner_theirs),
        (first_mine, first_theirs),
        (second_mine, second_theirs),
    ):
        grads += [mine, core_swapped(theirs)]
    grads.append(second_mine[:, half : half + affine_rows].T)
    slots = spans * lax.axis_size("dp") * lax.axis_size("pair")
    updated = adamw(
        table,
        totals,
        grads,
        (qkv_weight, proj_weight, inner_weight, outer_weight, affine_params),
        (qkv_moment, proj_moment, inner_moment, outer_moment, affine_moment),
        (qkv_square, proj_square, inner_square, outer_square, affine_square),
        slots,
    )
    state = [updated[3 * n + k] for k in range(3) for n in range(5)]
    return (*state, layer_out, input_grad, updated[-1][0, 0], updated[-1][1, 0])


def solution(mesh):
    placed = (
        P(("dp", "pair"), None),
        P(("dp", "pair"), None),
        P("dp", None),
        P("dp"),
        P(("dp", "pair"), None),
        P(("dp", "pair"), None),
        P(("dp", "pair"), None),
        P(("dp", "pair"), None),
        P(None, ("dp", "pair")),
        P(("dp", "pair"), None),
        P(("dp", "pair"), None),
        P(("dp", "pair"), None),
        P(("dp", "pair"), None),
        P(None, ("dp", "pair")),
        P(("dp", "pair"), None),
        P(("dp", "pair"), None),
        P(("dp", "pair"), None),
        P(("dp", "pair"), None),
        P(None, ("dp", "pair")),
    )
    return jax.shard_map(
        body,
        mesh=mesh,
        in_specs=placed,
        out_specs=(
            P(("dp", "pair"), None),
            P(("dp", "pair"), None),
            P(("dp", "pair"), None),
            P(("dp", "pair"), None),
            P(None, ("dp", "pair")),
            P(("dp", "pair"), None),
            P(("dp", "pair"), None),
            P(("dp", "pair"), None),
            P(("dp", "pair"), None),
            P(None, ("dp", "pair")),
            P(("dp", "pair"), None),
            P(("dp", "pair"), None),
            P(("dp", "pair"), None),
            P(("dp", "pair"), None),
            P(None, ("dp", "pair")),
            P(("dp", "pair"), None),
            P(("dp", "pair"), None),
            P(),
            P(),
        ),
        check_vma=False,
    )
```

time: 1290 us -> 338 us (0.26)
  waiting for transfers between devices: 832 us -> 87.9 us
  matrix products: 211 us -> 0 us
  Pallas kernels: 0 us -> 110 us
  blocking collectives: 87.1 us -> 0 us
  starting transfers between devices: 1.15 us -> 59.9 us
  other arithmetic: 52.6 us -> 16.8 us
  between operations: 25.2 us -> 4.76 us
  local copies, waits for them, and re-layouts: 73.4 us -> 54.8 us
    reduce_scatter x7 -> x0, waiting for transfers between devices: 397 us -> none  [the longest x1 172 us: body(): lax.psum_scatter(gradients[3], 'dp', scatter_dimension=0, tiled=True)]
    unnamed x15 -> x0, waiting for transfers between devices: 270 us -> none
    dot_general x24 -> x0, matrix products: 211 us -> none  [the longest x4 44.3 us: contract_cols(): lax.dot_general(left, right, (((1,), (1,)), ((), ())), preferred_element_...]
    all_gather x4 -> x0, waiting for transfers between devices: 164 us -> none  [the longest x1 65.8 us: body(): lax.all_gather(outer_weight.astype(jnp.bfloat16), ('dp', 'pair'), axis=0,...]
    pallas_call x0 -> x17, Pallas kernels: none -> 110 us  [call(): pl.pallas_call(body, grid_spec=pltpu.PrefetchScalarGridSpec(num_scalar_pr...]
    ppermute x2 -> x48, waiting for transfers between devices: 0.82 us -> 87.9 us  [the longest x32 82.6 us: flipped(): return lax.ppermute(block, AXES, flip_route(chips, bits))]
    ppermute x2 -> x48, starting transfers between devices: 0.61 us -> 59.9 us  [the longest x32 56.6 us: flipped(): return lax.ppermute(block, AXES, flip_route(chips, bits))]
    all_gather x1 -> x0, blocking collectives: 43.8 us -> none  [body(): lax.all_gather(affine_params.astype(jnp.bfloat16), ('dp', 'pair'), axis=1...]
  transfers between devices with their start and end apart: 15 -> 48, of which waited for: 14 -> 26; matrix products, arithmetic and copies ran while one was open for 13% -> 6% of each run, Pallas kernels for 0% -> 24%
where the time goes in v2:
time: 338 us; the launch traced here: 334 us
  Pallas kernels  110 us (33%)
  waiting for transfers between devices  87.9 us (26%)
  starting transfers between devices  59.9 us (18%)
  local copies, waits for them, and re-layouts  54.8 us (16%)
  other arithmetic  16.8 us (5%)
  between operations  4.76 us (1%)
    pallas_call x17, Pallas kernels, call(): pl.pallas_call(body, grid_spec=pltpu.PrefetchScalarGridSpec(num_scalar_pr...  110 us
    ppermute x32, waiting for transfers between devices, flipped(): return lax.ppermute(block, AXES, flip_route(chips, bits))  82.6 us
    ppermute x32, starting transfers between devices, flipped(): return lax.ppermute(block, AXES, flip_route(chips, bits))  56.6 us
    unnamed x219, local copies, waits for them, and re-layouts  50.2 us
    convert_element_type x16, other arithmetic, step(): sum((p[self.count:2 * self.count].astype(F32) for p in self.parts))  9.21 us
  transfers between devices with their start and end apart: 48, of which 26 were waited for; matrix products, arithmetic and copies ran while one was open for 6% of the time, Pallas kernels for 24%

profile of v2, /device:TPU:0, one launch (start us, length us, event | category | flops | bytes accessed | tf_op | source)
XLA Modules:
  0.0 333.8 jit_solution(15477596458445974395)
XLA Ops:
  4.9 3.0 collective-permute-start.1
  7.9 4.5 %collective-permute-done.1 = bf16[1,48,1664]{2,1,0:T(8,128)(2,1)S(1)} collective-permute-done((bf16[1,48,1664]{2,1,0:T(8,128)(2,1)S(1)}, bf16[1,48,1664]{2,1,0:T(8,128)(2,1)S(1)}, u32[]{:S(2)}, u32[]{:S(2)}) %collective-permute-start.1) | collective-permute-done | bytes 159776 | tf_op jit(solution)/shard_map/ppermute | solution.py:52
  12.5 2.6 collective-permute-start.2
  15.1 7.2 %collective-permute-done.2 = bf16[2,48,1664]{2,1,0:T(8,128)(2,1)S(1)} collective-permute-done((bf16[2,48,1664]{2,1,0:T(8,128)(2,1)S(1)}, bf16[2,48,1664]{2,1,0:T(8,128)(2,1)S(1)}, u32[]{:S(2)}, u32[]{:S(2)}) %collective-permute-start.2) | collective-permute-done | bytes 319520 | tf_op jit(solution)/shard_map/ppermute | solution.py:52
  22.4 3.1 collective-permute-start.3
  29.0 4.9 %collective-permute-done.3 = bf16[4,48,1664]{2,1,0:T(8,128)(2,1)S(1)} collective-permute-done((bf16[4,48,1664]{2,1,0:T(8,128)(2,1)S(1)}, bf16[4,48,1664]{2,1,0:T(8,128)(2,1)S(1)}, u32[]{:S(2)}, u32[]{:S(2)}) %collective-permute-start.3) | collective-permute-done | bytes 639008 | tf_op jit(solution)/shard_map/ppermute | solution.py:52
  35.1 2.0 collective-permute-start.6
  41.9 3.1 collective-permute-start.7
  45.0 7.7 %collective-permute-done.6 = bf16[8,48,1664]{2,1,0:T(8,128)(2,1)} collective-permute-done((bf16[8,48,1664]{2,1,0:T(8,128)(2,1)}, bf16[8,48,1664]{2,1,0:T(8,128)(2,1)}, u32[]{:S(2)}, u32[]{:S(2)}) %collective-permute-start.6) | collective-permute-done | bytes 1277984 | tf_op jit(solution)/shard_map/ppermute | solution.py:52
  64.3 5.1 %collective-permute-done.12 = bf16[2,192,384]{2,1,0:T(8,128)(2,1)S(1)} collective-permute-done((bf16[2,192,384]{2,1,0:T(8,128)(2,1)S(1)}, bf16[2,192,384]{2,1,0:T(8,128)(2,1)S(1)}, u32[]{:S(2)}, u32[]{:S(2)}) %collective-permute-start.12) | collective-permute-done | bytes 294944 | tf_op jit(solution)/shard_map/ppermute | solution.py:52
  73.9 8.0 %shard_map.330 = (bf16[768,2304]{1,0:T(8,128)(2,1)S(1)}, bf16[768,768]{1,0:T(8,128)(2,1)S(1)}, f32[12,768]{1,0:T(8,128)S(1)}, bf16[1024,2304]{1,0:T(8,128)(2,1)S(1)}) custom-call(s32[5,16]{1,0:T(8,128)S(1)} %stack.4.refs_0_, bf16[1024,768]{1,0:T(8,128)(2,1)S(1)} %copy-done.26, bf16[16,48,1664]{2,1,0:T(8,128)(2,1)S(1)} %constant_dynamic-update-slice_fusion.refs_2_, ...), custom_call_target="tpu_custom_call" | custom-call | flops 80000000000 | bytes 80000000 | tf_op jit(solution)/shard_map/pallas_call | solution.py:186
  83.7 4.9 %collective-permute-done.13 = bf16[8,48,1536]{2,1,0:T(8,128)(2,1)S(1)} collective-permute-done((bf16[8,48,1536]{2,1,0:T(8,128)(2,1)S(1)}, bf16[8,48,1536]{2,1,0:T(8,128)(2,1)S(1)}, u32[]{:S(2)}, u32[]{:S(2)}) %collective-permute-start.13) | collective-permute-done | bytes 1179680 | tf_op jit(solution)/shard_map/ppermute | solution.py:52
  90.0 7.3 %shard_map.331 = (bf16[8,6,256,128]{3,2,1,0:T(8,128)(2,1)S(1)}, bf16[1024,768]{1,0:T(8,128)(2,1)S(1)}, f32[1024,768]{1,0:T(8,128)S(1)}, f32[1024,128]{1,0:T(8,128)S(1)}, bf16[1024,768]{1,0:T(8,128)(2,1)S(1)}) custom-call(bf16[1024,768]{1,0:T(8,128)(2,1)S(1)} %copy-done.26, bf16[1024,2304]{1,0:T(8,128)(2,1)S(1)} %get-tuple-element.109.refs_1_, ...), custom_call_target="tpu_custom_call" | custom-call | flops 120000004096 | bytes 120000000 | tf_op jit(solution)/shard_map/pallas_call | solution.py:186
  102.4 8.6 %shard_map.332 = (bf16[768,1536]{1,0:T(8,128)(2,1)S(1)}, bf16[1024,1536]{1,0:T(8,128)(2,1)S(1)}, bf16[1024,1536]{1,0:T(8,128)(2,1)S(1)}) custom-call(s32[5,16]{1,0:T(8,128)S(1)} %stack.4.refs_0_, bf16[1024,768]{1,0:T(8,128)(2,1)S(1)} %get-tuple-element.112.refs_1_.refs_4_, bf16[16,48,1536]{2,1,0:T(8,128)(2,1)S(1)} %constant_dynamic-update-slice_fusion.5.refs_2_, ...), custom_call_target="tpu_custom_call" | custom-call | flops 99999997952 | bytes 100000000 | tf_op jit(solution)/shard_map/pallas_call | solution.py:186
  114.3 2.8 collective-permute-done.16
  117.4 8.8 %shard_map.333 = (bf16[768,1536]{1,0:T(8,128)(2,1)S(1)}, bf16[1024,1536]{1,0:T(8,128)(2,1)S(1)}, bf16[1024,1536]{1,0:T(8,128)(2,1)S(1)}) custom-call(s32[5,16]{1,0:T(8,128)S(1)} %stack.4.refs_0_, bf16[1024,768]{1,0:T(8,128)(2,1)S(1)} %get-tuple-element.112.refs_1_.refs_4_, bf16[16,48,1536]{2,1,0:T(8,128)(2,1)S(1)} %collective-permute-done.14.refs_2_, ...), custom_call_target="tpu_custom_call" | custom-call | flops 99999997952 | bytes 100000000 | tf_op jit(solution)/shard_map/pallas_call | solution.py:186
  129.7 2.7 copy-done.62
  134.4 10.8 %shard_map.334 = (bf16[3072,768]{1,0:T(8,128)(2,1)}, bf16[1024,768]{1,0:T(8,128)(2,1)}, f32[1024,768]{1,0:T(8,128)S(1)}, bf16[1024,768]{1,0:T(8,128)(2,1)S(1)}, ...) custom-call(s32[5,16]{1,0:T(8,128)S(1)} %stack.4.refs_0_, ...), custom_call_target="tpu_custom_call" | custom-call | flops 80000000000 | bytes 80000000 | tf_op jit(solution)/shard_map/pallas_call | solution.py:186
  148.2 1.9 copy-done.63
  150.1 14.8 %shard_map.335 = (bf16[1024,768]{1,0:T(8,128)(2,1)S(1)}, f32[8,768]{1,0:T(8,128)S(1)}, f32[8,768]{1,0:T(8,128)S(1)}, f32[8,128]{1,0:T(8,128)S(1)}, bf16[16,192,3...) custom-call(s32[5,16]{1,0:T(8,128)S(1)} %stack.4.refs_0_, bf16[1024,768]{1,0:T(8,128)(2,1)S(1)} %get-tuple-element.122.refs_1_, ...), custom_call_target="tpu_custom_call" | custom-call | flops 80000000000 | bytes 80000000 | tf_op jit(solution)/shard_map/pallas_call | solution.py:186
  165.3 2.7 copy-done.42
  170.0 6.7 %shard_map.337 = (bf16[1024,1536]{1,0:T(8,128)(2,1)S(1)}, f32[8,768]{1,0:T(8,128)S(1)}, bf16[16,48,1536]{2,1,0:T(8,128)(2,1)S(1)}) custom-call(s32[5,16]{1,0:T(8,128)S(1)} %stack.4.refs_0_, bf16[1024,768]{1,0:T(8,128)(2,1)S(1)} %get-tuple-element.127.refs_1_, bf16[1024,1536]{1,0:T(8,128)(2,1)S(1)} %copy-done.69, bf16[3072,768]{1,0:T(8,128)(2,1)S(1)} %copy-done.42, ...), custom_call_target="tpu_custom_call" | custom-call | flops 80000000000 | bytes 80000000 | tf_op jit(solution)/shard_map/pallas_call | solution.py:186
  178.7 3.2 copy-done.43
  183.8 7.1 %shard_map.336 = (bf16[1024,1536]{1,0:T(8,128)(2,1)S(1)}, f32[8,768]{1,0:T(8,128)S(1)}, bf16[16,48,1536]{2,1,0:T(8,128)(2,1)S(1)}) custom-call(s32[5,16]{1,0:T(8,128)S(1)} %stack.4.refs_0_, bf16[1024,768]{1,0:T(8,128)(2,1)S(1)} %get-tuple-element.127.refs_1_, bf16[1024,1536]{1,0:T(8,128)(2,1)S(1)} %copy-done.67, bf16[3072,768]{1,0:T(8,128)(2,1)S(1)} %copy-done.43, ...), custom_call_target="tpu_custom_call" | custom-call | flops 80000000000 | bytes 80000000 | tf_op jit(solution)/shard_map/pallas_call | solution.py:186
  197.4 1.9 copy-done.56
  201.0 9.0 %shard_map.338 = (f32[1024,768]{1,0:T(8,128)S(1)}, bf16[1024,768]{1,0:T(8,128)(2,1)S(1)}, f32[8,768]{1,0:T(8,128)S(1)}, bf16[1024,768]{1,0:T(8,128)(2,1)S(1)}) custom-call(bf16[1024,1536]{1,0:T(8,128)(2,1)S(1)} %copy-done.56, bf16[1024,1536]{1,0:T(8,128)(2,1)S(1)} %copy-done.54, bf16[768,1536]{1,0:T(8,128)(2,1)S(1)} %copy-done.73, ...), custom_call_target="tpu_custom_call" | custom-call | flops 80000000000 | bytes 80000000 | tf_op jit(solution)/shard_map/pallas_call | solution.py:186
  214.4 11.4 %collective-permute-done.21.refs_3_ = bf16[8,192,384]{2,1,0:T(8,128)(2,1)S(1)} collective-permute-done((bf16[8,192,384]{2,1,0:T(8,128)(2,1)}, bf16[8,192,384]{2,1,0:T(8,128)(2,1)S(1)}, u32[]{:S(2)}, u32[]{:S(2)}) %collective-permute-start.21) | collective-permute-done | bytes 1179680 | tf_op jit(solution)/shard_map/ppermute | solution.py:52
  226.7 2.3 copy-done.39
  229.0 6.8 %shard_map.339 = (bf16[1024,1536]{1,0:T(8,128)(2,1)S(1)}, f32[1,1536]{1,0:T(1,128)S(1)}) custom-call(bf16[1024,768]{1,0:T(8,128)(2,1)S(1)} %copy-done.71, bf16[1024,2304]{1,0:T(8,128)(2,1)S(1)} %copy-done.39, bf16[8,6,256,128]{3,2,1,0:T(8,128)(2,1)S(1)} %copy-done.41, bf16[8,192,384]{2,1,0:T(8,128)(2,1)S(1)} %collective-permute-done.21.refs_3_), custom_call_target="tpu_custom_call" | custom-call | flops 120000004096 | bytes 120000000 | tf_op jit(solution)/shard_map/pallas_call | solution.py:186
  236.0 4.5 %shard_map.340 = (bf16[16,48,1152]{2,1,0:T(8,128)(2,1)S(1)}, bf16[16,48,1152]{2,1,0:T(8,128)(2,1)S(1)}) custom-call(s32[5,16]{1,0:T(8,128)S(1)} %stack.4.refs_0_, bf16[1024,768]{1,0:T(8,128)(2,1)S(1)} %copy-done.27, bf16[1024,1536]{1,0:T(8,128)(2,1)S(1)} %get-tuple-element.143.refs_2_.refs_0_, bf16[1024,768]{1,0:T(8,128)(2,1)S(1)} %get-tuple-element.144.refs_3_, ...), custom_call_target="tpu_custom_call" | custom-call | flops 49999998976 | bytes 50000000 | tf_op jit(solution)/shard_map/pallas_call | solution.py:186
  241.9 2.2 collective-permute-start.37
  246.2 3.5 %collective-permute-done.37.refs_11_ = bf16[2,48,1536]{2,1,0:T(8,128)(2,1)S(1)} collective-permute-done((bf16[2,48,1536]{2,1,0:T(8,128)(2,1)S(1)}, bf16[2,48,1536]{2,1,0:T(8,128)(2,1)S(1)}, u32[]{:S(2)}, u32[]{:S(2)}) %collective-permute-start.37) | collective-permute-done | bytes 294944 | tf_op jit(solution)/shard_map/ppermute | solution.py:52
  249.7 1.9 add_convert_fusion.11
  251.6 7.4 %collective-permute-start.38 = (bf16[1,48,1536]{2,1,0:T(8,128)(2,1)}, bf16[1,48,1536]{2,1,0:T(8,128)(2,1)}, u32[]{:S(2)}, u32[]{:S(2)}) collective-permute-start(bf16[1,48,1536]{2,1,0:T(8,128)(2,1)} %add_convert_fusion.11), channel_id=1, source_target_pairs={{0,8},{1,17},{2,10},{3,19},{4,12},{5,21},{6,14},{7,23},{8,0},{9,25... | collective-permute-start | bytes 442376 | tf_op jit(solution)/shard_map/ppermute | solution.py:52
  259.1 4.1 %shard_map.341 = (bf16[1024,768]{1,0:T(8,128)(2,1)S(1)}, f32[1,768]{1,0:T(1,128)S(1)}) custom-call(bf16[1024,768]{1,0:T(8,128)(2,1)S(1)} %copy-done.71, bf16[1024,2304]{1,0:T(8,128)(2,1)S(1)} %bitcast.22, bf16[8,6,256,128]{3,2,1,0:T(8,128)(2,1)S(1)} %copy-done.41, bf16[8,48,1536]{2,1,0:T(8,128)(2,1)S(1)} %copy-done.9, ...), custom_call_target="tpu_custom_call" | custom-call | flops 60000002048 | bytes 60000000 | tf_op jit(solution)/shard_map/pallas_call | solution.py:186
  263.2 2.1 shard_map.342
  267.2 5.4 %shard_map.343 = f32[1024,768]{1,0:T(8,128)} custom-call(bf16[1024,1536]{1,0:T(8,128)(2,1)S(1)} %get-tuple-element.143.refs_2_.refs_0_, bf16[1024,768]{1,0:T(8,128)(2,1)S(1)} %get-tuple-element.149.refs_2_.refs_1_, bf16[768,2304]{1,0:T(8,128)(2,1)S(1)} %copy-done.47, f32[1024,768]{1,0:T(8,128)S(1)} %copy-done.51), custom_call_target="tpu_custom_call" | custom-call | flops 80000000000 | bytes 80000000 | tf_op jit(solution)/shard_map/pallas_call | solution.py:186
  273.3 5.4 %collective-permute-done.24.refs_3_ = bf16[8,48,1152]{2,1,0:T(8,128)(2,1)S(1)} collective-permute-done((bf16[8,48,1152]{2,1,0:T(8,128)(2,1)S(1)}, bf16[8,48,1152]{2,1,0:T(8,128)(2,1)S(1)}, u32[]{:S(2)}, u32[]{:S(2)}) %collective-permute-start.24) | collective-permute-done | bytes 884768 | tf_op jit(solution)/shard_map/ppermute | solution.py:52
  280.3 4.3 %collective-permute-done.31.refs_9_ = bf16[8,48,512]{2,1,0:T(8,128)(2,1)S(1)} collective-permute-done((bf16[8,48,512]{2,1,0:T(8,128)(2,1)S(1)}, bf16[8,48,512]{2,1,0:T(8,128)(2,1)S(1)}, u32[]{:S(2)}, u32[]{:S(2)}) %collective-permute-start.31) | collective-permute-done | bytes 393248 | tf_op jit(solution)/shard_map/ppermute | solution.py:52
  287.7 2.7 collective-permute-done.32.refs_10_
  293.6 2.8 collective-permute-done.33.refs_11_
  296.5 1.9 collective-permute-start.34
  298.4 6.1 %collective-permute-done.26.refs_5_ = bf16[2,48,1152]{2,1,0:T(8,128)(2,1)S(1)} collective-permute-done((bf16[2,48,1152]{2,1,0:T(8,128)(2,1)S(1)}, bf16[2,48,1152]{2,1,0:T(8,128)(2,1)S(1)}, u32[]{:S(2)}, u32[]{:S(2)}) %collective-permute-start.26) | collective-permute-done | bytes 221216 | tf_op jit(solution)/shard_map/ppermute | solution.py:52
  305.6 2.1 shard_map.344
  313.7 2.2 collective-permute-done.40
  317.5 2.1 collective-permute-done.41
  323.2 2.5 collective-permute-start.43
  330.6 2.5 shard_map.346
  (346 shorter events, 98.6 us)
Async XLA Ops:
  3.5 1.4 collective-permute-start
  4.9 7.5 %collective-permute-start.1 = (bf16[1,48,1664]{2,1,0:T(8,128)(2,1)S(1)}, bf16[1,48,1664]{2,1,0:T(8,128)(2,1)S(1)}, u32[]{:S(2)}, u32[]{:S(2)}) collective-permute-start(bf16[1,48,1664]{2,1,0:T(8,128)(2,1)S(1)} %get-tuple-element.194), channel_id=1, source_target_pairs={{0,8},{1,17},{2,10},{3,19},{4,12},{5,21},{6,14},{7,23},{8,0},{9,25... | collective-permute-start | bytes 479240 | tf_op jit(solution)/shard_map/ppermute | solution.py:52
  12.5 9.8 %collective-permute-start.2 = (bf16[2,48,1664]{2,1,0:T(8,128)(2,1)S(1)}, bf16[2,48,1664]{2,1,0:T(8,128)(2,1)S(1)}, u32[]{:S(2)}, u32[]{:S(2)}) collective-permute-start(bf16[2,48,1664]{2,1,0:T(8,128)(2,1)S(1)} %pad_maximum_fusion.6), channel_id=1, source_target_pairs={{0,16},{1,9},{2,18},{3,11},{4,20},{5,13},{6,22},{7,15},{8,24},{9,1... | collective-permute-start | bytes 958472 | tf_op jit(solution)/shard_map/ppermute | solution.py:52
  22.4 11.4 %collective-permute-start.3 = (bf16[4,48,1664]{2,1,0:T(8,128)(2,1)S(1)}, bf16[4,48,1664]{2,1,0:T(8,128)(2,1)S(1)}, u32[]{:S(2)}, u32[]{:S(2)}) collective-permute-start(bf16[4,48,1664]{2,1,0:T(8,128)(2,1)S(1)} %pad_maximum_fusion.3), channel_id=1, source_target_pairs={{0,2},{1,5},{2,0},{3,7},{4,6},{5,1},{6,4},{7,3},{8,10},{9,13},{10,... | collective-permute-start | bytes 1916936 | tf_op jit(solution)/shard_map/ppermute | solution.py:52
  25.5 1.3 collective-permute-start.4
  27.5 7.6 %collective-permute-start.5 = (bf16[1,48,1536]{2,1,0:T(8,128)(2,1)S(1)}, bf16[1,48,1536]{2,1,0:T(8,128)(2,1)S(1)}, u32[]{:S(2)}, u32[]{:S(2)}) collective-permute-start(bf16[1,48,1536]{2,1,0:T(8,128)(2,1)S(1)} %get-tuple-element.104), channel_id=1, source_target_pairs={{0,8},{1,17},{2,10},{3,19},{4,12},{5,21},{6,14},{7,23},{8,0},{9,25... | collective-permute-start | bytes 442376 | tf_op jit(solution)/shard_map/ppermute | solution.py:52
  35.1 17.6 %collective-permute-start.6 = (bf16[8,48,1664]{2,1,0:T(8,128)(2,1)}, bf16[8,48,1664]{2,1,0:T(8,128)(2,1)}, u32[]{:S(2)}, u32[]{:S(2)}) collective-permute-start(bf16[8,48,1664]{2,1,0:T(8,128)(2,1)} %pad_maximum_fusion), channel_id=1, source_target_pairs={{0,4},{1,3},{2,6},{3,1},{4,0},{5,7},{6,2},{7,5},{8,12},{9,11},{10,... | collective-permute-start | bytes 3833864 | tf_op jit(solution)/shard_map/ppermute | solution.py:52
  37.2 1.3 collective-permute-start.8
  40.3 13.9 %collective-permute-start.9 = (bf16[1,192,384]{2,1,0:T(8,128)(2,1)S(1)}, bf16[1,192,384]{2,1,0:T(8,128)(2,1)S(1)}, u32[]{:S(2)}, u32[]{:S(2)}) collective-permute-start(bf16[1,192,384]{2,1,0:T(8,128)(2,1)S(1)} %get-tuple-element.107), channel_id=1, source_target_pairs={{0,8},{1,17},{2,10},{3,19},{4,12},{5,21},{6,14},{7,23},{8,0},{9,25... | collective-permute-start | bytes 442376 | tf_op jit(solution)/shard_map/ppermute | solution.py:52
  41.9 12.3 %collective-permute-start.7 = (bf16[2,48,1536]{2,1,0:T(8,128)(2,1)S(1)}, bf16[2,48,1536]{2,1,0:T(8,128)(2,1)S(1)}, u32[]{:S(2)}, u32[]{:S(2)}) collective-permute-start(bf16[2,48,1536]{2,1,0:T(8,128)(2,1)S(1)} %pad_maximum_fusion.7), channel_id=1, source_target_pairs={{0,16},{1,9},{2,18},{3,11},{4,20},{5,13},{6,22},{7,15},{8,24},{9,1... | collective-permute-start | bytes 884744 | tf_op jit(solution)/shard_map/ppermute | solution.py:52
  54.2 18.0 %collective-permute-start.10 = (bf16[16,48,1664]{2,1,0:T(8,128)(2,1)S(1)}, bf16[16,48,1664]{2,1,0:T(8,128)(2,1)}, u32[]{:S(2)}, u32[]{:S(2)}) collective-permute-start(bf16[16,48,1664]{2,1,0:T(8,128)(2,1)S(1)} %constant_dynamic-update-slice_fusion.refs_2_), channel_id=1, source_target_pairs={{0,1},{1,0},{2,3},{3,2},{4,5},{5,4},{6,7},{7,6},{8,9},{9,8},{10,11... | collective-permute-start | bytes 7667720 | tf_op jit(solution)/shard_map/ppermute | solution.py:56
  60.0 9.4 %collective-permute-start.12 = (bf16[2,192,384]{2,1,0:T(8,128)(2,1)S(1)}, bf16[2,192,384]{2,1,0:T(8,128)(2,1)S(1)}, u32[]{:S(2)}, u32[]{:S(2)}) collective-permute-start(bf16[2,192,384]{2,1,0:T(8,128)(2,1)S(1)} %pad_maximum_fusion.8), channel_id=1, source_target_pairs={{0,16},{1,9},{2,18},{3,11},{4,20},{5,13},{6,22},{7,15},{8,24},{9,1... | collective-permute-start | bytes 884744 | tf_op jit(solution)/shard_map/ppermute | solution.py:52
  61.4 9.9 %collective-permute-start.11 = (bf16[4,48,1536]{2,1,0:T(8,128)(2,1)S(1)}, bf16[4,48,1536]{2,1,0:T(8,128)(2,1)S(1)}, u32[]{:S(2)}, u32[]{:S(2)}) collective-permute-start(bf16[4,48,1536]{2,1,0:T(8,128)(2,1)S(1)} %pad_maximum_fusion.4), channel_id=1, source_target_pairs={{0,2},{1,5},{2,0},{3,7},{4,6},{5,1},{6,4},{7,3},{8,10},{9,13},{10,... | collective-permute-start | bytes 1769480 | tf_op jit(solution)/shard_map/ppermute | solution.py:52
  72.3 16.3 %collective-permute-start.13 = (bf16[8,48,1536]{2,1,0:T(8,128)(2,1)S(1)}, bf16[8,48,1536]{2,1,0:T(8,128)(2,1)S(1)}, u32[]{:S(2)}, u32[]{:S(2)}) collective-permute-start(bf16[8,48,1536]{2,1,0:T(8,128)(2,1)S(1)} %pad_maximum_fusion.1), channel_id=1, source_target_pairs={{0,4},{1,3},{2,6},{3,1},{4,0},{5,7},{6,2},{7,5},{8,12},{9,11},{10,... | collective-permute-start | bytes 3538952 | tf_op jit(solution)/shard_map/ppermute | solution.py:52
  88.5 10.7 %collective-permute-start.15 = (bf16[4,192,384]{2,1,0:T(8,128)(2,1)S(1)}, bf16[4,192,384]{2,1,0:T(8,128)(2,1)S(1)}, u32[]{:S(2)}, u32[]{:S(2)}) collective-permute-start(bf16[4,192,384]{2,1,0:T(8,128)(2,1)S(1)} %pad_maximum_fusion.5), channel_id=1, source_target_pairs={{0,2},{1,5},{2,0},{3,7},{4,6},{5,1},{6,4},{7,3},{8,10},{9,13},{10,... | collective-permute-start | bytes 1769480 | tf_op jit(solution)/shard_map/ppermute | solution.py:52
  99.1 18.3 %collective-permute-start.14 = (bf16[16,48,1536]{2,1,0:T(8,128)(2,1)S(1)}, bf16[16,48,1536]{2,1,0:T(8,128)(2,1)S(1)}, u32[]{:S(2)}, u32[]{:S(2)}) collective-permute-start(bf16[16,48,1536]{2,1,0:T(8,128)(2,1)S(1)} %constant_dynamic-update-slice_fusion.5.refs_2_), channel_id=1, source_target_pairs={{0,1},{1,0},{2,3},{3,2},{4,5},{5,4},{6,7},{7,6},{8,9},{9,8},{10,11... | collective-permute-start | bytes 7077896 | tf_op jit(solution)/shard_map/ppermute | solution.py:56
  100.8 16.3 %collective-permute-start.16 = (bf16[8,192,384]{2,1,0:T(8,128)(2,1)S(1)}, bf16[8,192,384]{2,1,0:T(8,128)(2,1)S(1)}, u32[]{:S(2)}, u32[]{:S(2)}) collective-permute-start(bf16[8,192,384]{2,1,0:T(8,128)(2,1)S(1)} %pad_maximum_fusion.2), channel_id=1, source_target_pairs={{0,4},{1,3},{2,6},{3,1},{4,0},{5,7},{6,2},{7,5},{8,12},{9,11},{10,... | collective-permute-start | bytes 3538952 | tf_op jit(solution)/shard_map/ppermute | solution.py:52
  117.3 12.4 %collective-permute-start.17 = (bf16[16,192,384]{2,1,0:T(8,128)(2,1)S(1)}, bf16[16,192,384]{2,1,0:T(8,128)(2,1)S(1)}, u32[]{:S(2)}, u32[]{:S(2)}) collective-permute-start(bf16[16,192,384]{2,1,0:T(8,128)(2,1)S(1)} %constant_dynamic-update-slice_fusion.10.refs_3_), channel_id=1, source_target_pairs={{0,1},{1,0},{2,3},{3,2},{4,5},{5,4},{6,7},{7,6},{8,9},{9,8},{10,11... | collective-permute-start | bytes 7077896 | tf_op jit(solution)/shard_map/ppermute | solution.py:56
  146.8 1.3 collective-permute-start.18
  164.9 13.8 %collective-permute-start.19 = (bf16[16,192,384]{2,1,0:T(8,128)(2,1)S(1)}, bf16[16,192,384]{2,1,0:T(8,128)(2,1)S(1)}, u32[]{:S(2)}, u32[]{:S(2)}) collective-permute-start(bf16[16,192,384]{2,1,0:T(8,128)(2,1)S(1)} %get-tuple-element.130), channel_id=1, source_target_pairs={{0,1},{1,0},{2,3},{3,2},{4,5},{5,4},{6,7},{7,6},{8,9},{9,8},{10,11... | collective-permute-start | bytes 7077896 | tf_op jit(solution)/shard_map/ppermute | solution.py:56
  178.4 12.5 %collective-permute-start.20 = (bf16[16,48,1536]{2,1,0:T(8,128)(2,1)S(1)}, bf16[16,48,1536]{2,1,0:T(8,128)(2,1)S(1)}, u32[]{:S(2)}, u32[]{:S(2)}) collective-permute-start(bf16[16,48,1536]{2,1,0:T(8,128)(2,1)S(1)} %get-tuple-element.139), channel_id=1, source_target_pairs={{0,1},{1,0},{2,3},{3,2},{4,5},{5,4},{6,7},{7,6},{8,9},{9,8},{10,11... | collective-permute-start | bytes 7077896 | tf_op jit(solution)/shard_map/ppermute | solution.py:56
  192.3 20.5 %collective-permute-start.28 = (bf16[8,48,1536]{2,1,0:T(8,128)(2,1)}, bf16[8,48,1536]{2,1,0:T(8,128)(2,1)S(1)}, u32[]{:S(2)}, u32[]{:S(2)}) collective-permute-start(bf16[8,48,1536]{2,1,0:T(8,128)(2,1)} %add_convert_fusion), channel_id=1, source_target_pairs={{0,4},{1,3},{2,6},{3,1},{4,0},{5,7},{6,2},{7,5},{8,12},{9,11},{10,... | collective-permute-start | bytes 3538952 | tf_op jit(solution)/shard_map/ppermute | solution.py:52
  195.1 30.7 %collective-permute-start.21 = (bf16[8,192,384]{2,1,0:T(8,128)(2,1)}, bf16[8,192,384]{2,1,0:T(8,128)(2,1)S(1)}, u32[]{:S(2)}, u32[]{:S(2)}) collective-permute-start(bf16[8,192,384]{2,1,0:T(8,128)(2,1)} %add_convert_fusion.1), channel_id=1, source_target_pairs={{0,4},{1,3},{2,6},{3,1},{4,0},{5,7},{6,2},{7,5},{8,12},{9,11},{10,... | collective-permute-start | bytes 3538952 | tf_op jit(solution)/shard_map/ppermute | solution.py:52
  213.9 26.8 %collective-permute-start.36 = (bf16[4,48,1536]{2,1,0:T(8,128)(2,1)}, bf16[4,48,1536]{2,1,0:T(8,128)(2,1)}, u32[]{:S(2)}, u32[]{:S(2)}) collective-permute-start(bf16[4,48,1536]{2,1,0:T(8,128)(2,1)} %add_convert_fusion.3), channel_id=1, source_target_pairs={{0,2},{1,5},{2,0},{3,7},{4,6},{5,1},{6,4},{7,3},{8,10},{9,13},{10,... | collective-permute-start | bytes 1769480 | tf_op jit(solution)/shard_map/ppermute | solution.py:52
  226.1 9.9 %collective-permute-start.22 = (bf16[4,192,384]{2,1,0:T(8,128)(2,1)S(1)}, bf16[4,192,384]{2,1,0:T(8,128)(2,1)S(1)}, u32[]{:S(2)}, u32[]{:S(2)}) collective-permute-start(bf16[4,192,384]{2,1,0:T(8,128)(2,1)S(1)} %add_convert_fusion.4), channel_id=1, source_target_pairs={{0,2},{1,5},{2,0},{3,7},{4,6},{5,1},{6,4},{7,3},{8,10},{9,13},{10,... | collective-permute-start | bytes 1769480 | tf_op jit(solution)/shard_map/ppermute | solution.py:52
  240.5 18.5 %collective-permute-start.23 = (bf16[16,48,1152]{2,1,0:T(8,128)(2,1)S(1)}, bf16[16,48,1152]{2,1,0:T(8,128)(2,1)S(1)}, u32[]{:S(2)}, u32[]{:S(2)}) collective-permute-start(bf16[16,48,1152]{2,1,0:T(8,128)(2,1)S(1)} %get-tuple-element.147), channel_id=1, source_target_pairs={{0,1},{1,0},{2,3},{3,2},{4,5},{5,4},{6,7},{7,6},{8,9},{9,8},{10,11... | collective-permute-start | bytes 5308424 | tf_op jit(solution)/shard_map/ppermute | solution.py:56
  241.9 7.8 %collective-permute-start.37 = (bf16[2,48,1536]{2,1,0:T(8,128)(2,1)S(1)}, bf16[2,48,1536]{2,1,0:T(8,128)(2,1)S(1)}, u32[]{:S(2)}, u32[]{:S(2)}) collective-permute-start(bf16[2,48,1536]{2,1,0:T(8,128)(2,1)S(1)} %add_convert_fusion.7), channel_id=1, source_target_pairs={{0,16},{1,9},{2,18},{3,11},{4,20},{5,13},{6,22},{7,15},{8,24},{9,1... | collective-permute-start | bytes 884744 | tf_op jit(solution)/shard_map/ppermute | solution.py:52
  245.3 13.7 %collective-permute-start.29 = (bf16[2,192,384]{2,1,0:T(8,128)(2,1)S(1)}, bf16[2,192,384]{2,1,0:T(8,128)(2,1)S(1)}, u32[]{:S(2)}, u32[]{:S(2)}) collective-permute-start(bf16[2,192,384]{2,1,0:T(8,128)(2,1)S(1)} %add_convert_fusion.8), channel_id=1, source_target_pairs={{0,16},{1,9},{2,18},{3,11},{4,20},{5,13},{6,22},{7,15},{8,24},{9,1... | collective-permute-start | bytes 884744 | tf_op jit(solution)/shard_map/ppermute | solution.py:52
  251.6 53.9 %collective-permute-start.38 = (bf16[1,48,1536]{2,1,0:T(8,128)(2,1)}, bf16[1,48,1536]{2,1,0:T(8,128)(2,1)}, u32[]{:S(2)}, u32[]{:S(2)}) collective-permute-start(bf16[1,48,1536]{2,1,0:T(8,128)(2,1)} %add_convert_fusion.11), channel_id=1, source_target_pairs={{0,8},{1,17},{2,10},{3,19},{4,12},{5,21},{6,14},{7,23},{8,0},{9,25... | collective-permute-start | bytes 442376 | tf_op jit(solution)/shard_map/ppermute | solution.py:52
  265.3 7.3 %collective-permute-start.30 = (bf16[16,48,512]{2,1,0:T(8,128)(2,1)S(1)}, bf16[16,48,512]{2,1,0:T(8,128)(2,1)S(1)}, u32[]{:S(2)}, u32[]{:S(2)}) collective-permute-start(bf16[16,48,512]{2,1,0:T(8,128)(2,1)S(1)} %get-tuple-element.157), channel_id=1, source_target_pairs={{0,1},{1,0},{2,3},{3,2},{4,5},{5,4},{6,7},{7,6},{8,9},{9,8},{10,11... | collective-permute-start | bytes 2359304 | tf_op jit(solution)/shard_map/ppermute | solution.py:56
  265.6 13.1 %collective-permute-start.24 = (bf16[8,48,1152]{2,1,0:T(8,128)(2,1)S(1)}, bf16[8,48,1152]{2,1,0:T(8,128)(2,1)S(1)}, u32[]{:S(2)}, u32[]{:S(2)}) collective-permute-start(bf16[8,48,1152]{2,1,0:T(8,128)(2,1)S(1)} %add_convert_fusion.2), channel_id=1, source_target_pairs={{0,4},{1,3},{2,6},{3,1},{4,0},{5,7},{6,2},{7,5},{8,12},{9,11},{10,... | collective-permute-start | bytes 2654216 | tf_op jit(solution)/shard_map/ppermute | solution.py:52
  272.8 11.8 %collective-permute-start.31 = (bf16[8,48,512]{2,1,0:T(8,128)(2,1)S(1)}, bf16[8,48,512]{2,1,0:T(8,128)(2,1)S(1)}, u32[]{:S(2)}, u32[]{:S(2)}) collective-permute-start(bf16[8,48,512]{2,1,0:T(8,128)(2,1)S(1)} %add_convert_fusion.6), channel_id=1, source_target_pairs={{0,4},{1,3},{2,6},{3,1},{4,0},{5,7},{6,2},{7,5},{8,12},{9,11},{10,... | collective-permute-start | bytes 1179656 | tf_op jit(solution)/shard_map/ppermute | solution.py:52
  278.9 13.0 %collective-permute-start.25 = (bf16[4,48,1152]{2,1,0:T(8,128)(2,1)S(1)}, bf16[4,48,1152]{2,1,0:T(8,128)(2,1)S(1)}, u32[]{:S(2)}, u32[]{:S(2)}) collective-permute-start(bf16[4,48,1152]{2,1,0:T(8,128)(2,1)S(1)} %add_convert_fusion.5), channel_id=1, source_target_pairs={{0,2},{1,5},{2,0},{3,7},{4,6},{5,1},{6,4},{7,3},{8,10},{9,13},{10,... | collective-permute-start | bytes 1327112 | tf_op jit(solution)/shard_map/ppermute | solution.py:52
  284.7 5.7 %collective-permute-start.32 = (bf16[4,48,512]{2,1,0:T(8,128)(2,1)S(1)}, bf16[4,48,512]{2,1,0:T(8,128)(2,1)S(1)}, u32[]{:S(2)}, u32[]{:S(2)}) collective-permute-start(bf16[4,48,512]{2,1,0:T(8,128)(2,1)S(1)} %add_convert_fusion.10), channel_id=1, source_target_pairs={{0,2},{1,5},{2,0},{3,7},{4,6},{5,1},{6,4},{7,3},{8,10},{9,13},{10,... | collective-permute-start | bytes 589832 | tf_op jit(solution)/shard_map/ppermute | solution.py:52
  286.2 19.3 %collective-permute-start.35 = (bf16[1,192,384]{2,1,0:T(8,128)(2,1)S(1)}, bf16[1,192,384]{2,1,0:T(8,128)(2,1)S(1)}, u32[]{:S(2)}, u32[]{:S(2)}) collective-permute-start(bf16[1,192,384]{2,1,0:T(8,128)(2,1)S(1)} %add_convert_fusion.12), channel_id=1, source_target_pairs={{0,8},{1,17},{2,10},{3,19},{4,12},{5,21},{6,14},{7,23},{8,0},{9,25... | collective-permute-start | bytes 442376 | tf_op jit(solution)/shard_map/ppermute | solution.py:52
  290.5 6.0 %collective-permute-start.33 = (bf16[2,48,512]{2,1,0:T(8,128)(2,1)S(1)}, bf16[2,48,512]{2,1,0:T(8,128)(2,1)S(1)}, u32[]{:S(2)}, u32[]{:S(2)}) collective-permute-start(bf16[2,48,512]{2,1,0:T(8,128)(2,1)S(1)} %add_convert_fusion.14), channel_id=1, source_target_pairs={{0,16},{1,9},{2,18},{3,11},{4,20},{5,13},{6,22},{7,15},{8,24},{9,1... | collective-permute-start | bytes 294920 | tf_op jit(solution)/shard_map/ppermute | solution.py:52
  292.0 12.5 %collective-permute-start.26 = (bf16[2,48,1152]{2,1,0:T(8,128)(2,1)S(1)}, bf16[2,48,1152]{2,1,0:T(8,128)(2,1)S(1)}, u32[]{:S(2)}, u32[]{:S(2)}) collective-permute-start(bf16[2,48,1152]{2,1,0:T(8,128)(2,1)S(1)} %add_convert_fusion.9), channel_id=1, source_target_pairs={{0,16},{1,9},{2,18},{3,11},{4,20},{5,13},{6,22},{7,15},{8,24},{9,1... | collective-permute-start | bytes 663560 | tf_op jit(solution)/shard_map/ppermute | solution.py:52
  296.5 11.2 %collective-permute-start.34 = (bf16[1,48,512]{2,1,0:T(8,128)(2,1)S(1)}, bf16[1,48,512]{2,1,0:T(8,128)(2,1)S(1)}, u32[]{:S(2)}, u32[]{:S(2)}) collective-permute-start(bf16[1,48,512]{2,1,0:T(8,128)(2,1)S(1)} %add_convert_fusion.15), channel_id=1, source_target_pairs={{0,8},{1,17},{2,10},{3,19},{4,12},{5,21},{6,14},{7,23},{8,0},{9,25... | collective-permute-start | bytes 147464 | tf_op jit(solution)/shard_map/ppermute | solution.py:52
  304.6 4.8 %collective-permute-start.27 = (bf16[1,48,1152]{2,1,0:T(8,128)(2,1)S(1)}, bf16[1,48,1152]{2,1,0:T(8,128)(2,1)S(1)}, u32[]{:S(2)}, u32[]{:S(2)}) collective-permute-start(bf16[1,48,1152]{2,1,0:T(8,128)(2,1)S(1)} %add_convert_fusion.13), channel_id=1, source_target_pairs={{0,8},{1,17},{2,10},{3,19},{4,12},{5,21},{6,14},{7,23},{8,0},{9,25... | collective-permute-start | bytes 331784 | tf_op jit(solution)/shard_map/ppermute | solution.py:52
  311.2 1.2 collective-permute-start.39
  312.3 3.6 %collective-permute-start.40 = (f32[8,128]{1,0:T(8,128)S(1)}, f32[8,128]{1,0:T(8,128)S(1)}, u32[]{:S(2)}, u32[]{:S(2)}) collective-permute-start(f32[8,128]{1,0:T(8,128)S(1)} %add.357), channel_id=1, source_target_pairs={{0,2},{1,3},{2,0},{3,1},{4,6},{5,7},{6,4},{7,5},{8,10},{9,11},{10,... | collective-permute-start | bytes 12296 | tf_op jit(solution)/shard_map/ppermute | solution.py:52
  315.9 3.6 %collective-permute-start.41 = (f32[8,128]{1,0:T(8,128)S(1)}, f32[8,128]{1,0:T(8,128)S(1)}, u32[]{:S(2)}, u32[]{:S(2)}) collective-permute-start(f32[8,128]{1,0:T(8,128)S(1)} %add.358), channel_id=1, source_target_pairs={{0,4},{1,5},{2,6},{3,7},{4,0},{5,1},{6,2},{7,3},{8,12},{9,13},{10,... | collective-permute-start | bytes 12296 | tf_op jit(solution)/shard_map/ppermute | solution.py:52
  319.5 3.6 %collective-permute-start.42 = (f32[8,128]{1,0:T(8,128)S(1)}, f32[8,128]{1,0:T(8,128)S(1)}, u32[]{:S(2)}, u32[]{:S(2)}) collective-permute-start(f32[8,128]{1,0:T(8,128)S(1)} %add.359), channel_id=1, source_target_pairs={{0,8},{1,9},{2,10},{3,11},{4,12},{5,13},{6,14},{7,15},{8,0},{9,1},... | collective-permute-start | bytes 12296 | tf_op jit(solution)/shard_map/ppermute | solution.py:52
  320.4 7.3 %collective-permute-start.44 = (f32[96,384]{1,0:T(8,128)S(1)}, f32[96,384]{1,0:T(8,128)S(1)}, u32[]{:S(2)}, u32[]{:S(2)}) collective-permute-start(f32[96,384]{1,0:T(8,128)S(1)} %get-tuple-element.165), channel_id=1, source_target_pairs={{0,1},{1,0},{2,3},{3,2},{4,5},{5,4},{6,7},{7,6},{8,9},{9,8},{10,11... | collective-permute-start | bytes 442376 | tf_op jit(solution)/shard_map/ppermute | solution.py:56
  320.4 7.3 %collective-permute-start.45 = (f32[24,1536]{1,0:T(8,128)S(1)}, f32[24,1536]{1,0:T(8,128)S(1)}, u32[]{:S(2)}, u32[]{:S(2)}) collective-permute-start(f32[24,1536]{1,0:T(8,128)S(1)} %get-tuple-element.167), channel_id=1, source_target_pairs={{0,1},{1,0},{2,3},{3,2},{4,5},{5,4},{6,7},{7,6},{8,9},{9,8},{10,11... | collective-permute-start | bytes 442376 | tf_op jit(solution)/shard_map/ppermute | solution.py:56
  321.8 5.9 %collective-permute-start.46 = (f32[24,1152]{1,0:T(8,128)S(1)}, f32[24,1152]{1,0:T(8,128)S(1)}, u32[]{:S(2)}, u32[]{:S(2)}) collective-permute-start(f32[24,1152]{1,0:T(8,128)S(1)} %get-tuple-element.169), channel_id=1, source_target_pairs={{0,1},{1,0},{2,3},{3,2},{4,5},{5,4},{6,7},{7,6},{8,9},{9,8},{10,11... | collective-permute-start | bytes 331784 | tf_op jit(solution)/shard_map/ppermute | solution.py:56
  321.8 5.9 %collective-permute-start.47 = (f32[24,512]{1,0:T(8,128)S(1)}, f32[24,512]{1,0:T(8,128)S(1)}, u32[]{:S(2)}, u32[]{:S(2)}) collective-permute-start(f32[24,512]{1,0:T(8,128)S(1)} %get-tuple-element.171), channel_id=1, source_target_pairs={{0,1},{1,0},{2,3},{3,2},{4,5},{5,4},{6,7},{7,6},{8,9},{9,8},{10,11... | collective-permute-start | bytes 147464 | tf_op jit(solution)/shard_map/ppermute | solution.py:56
  323.2 4.5 %collective-permute-start.43 = (f32[8,128]{1,0:T(8,128)S(1)}, f32[8,128]{1,0:T(8,128)S(1)}, u32[]{:S(2)}, u32[]{:S(2)}) collective-permute-start(f32[8,128]{1,0:T(8,128)S(1)} %add.360), channel_id=1, source_target_pairs={{0,16},{1,17},{2,18},{3,19},{4,20},{5,21},{6,22},{7,23},{8,24},{9,... | collective-permute-start | bytes 12296 | tf_op jit(solution)/shard_map/ppermute | solution.py:52
  (105 other events, 1252.2 us)

commit v3 on v2

--- a/solution.py
+++ b/solution.py
@@ -56,10 +56,14 @@
     return lax.ppermute(block, AXES, core_route(lax.axis_size("dp")))
 
 
-def block_order():
+def near_first(chips):
+    steps = flip_steps(chips)
+    return steps[2:] + steps[:2] if len(steps) == 4 else steps
+
+
+def block_order(steps):
     chips = lax.axis_size("dp")
     d, c = lax.axis_index("dp"), lax.axis_index("pair")
-    steps = flip_steps(chips)
     index = jnp.arange(chips, dtype=jnp.int32)
     blocks, places = [], []
     for core in range(2):
@@ -115,8 +119,8 @@
 
 
 class Gather:
-    def __init__(self, block):
-        self.held, self.got, self.left = block[None], None, list(flip_steps(lax.axis_size("dp")))
+    def __init__(self, block, steps):
+        self.held, self.got, self.left = block[None], None, list(steps)
 
     def step(self, *others):
         if self.got is not None:
@@ -127,13 +131,17 @@
     def finish(self, order, rows, *others):
         while self.left:
             self.step()
-        own = tied(jnp.concatenate([self.held, self.got], axis=0), *others)
-        other = core_swapped(own)
+        own = (self.held, self.got)
+        other = tuple(core_swapped(tied(part, *others)) for part in own)
         if rows % 16:
             own, other = (
-                jnp.zeros(ref.shape, BF16).at[order[side]].set(ref).reshape(16, -1, ref.shape[2])
-                for side, ref in enumerate((own, other))
+                jnp.zeros((2 * self.held.shape[0], *self.held.shape[1:]), BF16)
+                .at[order[side]]
+                .set(jnp.concatenate(parts))
+                .reshape(2, 8, -1, self.held.shape[2])
+                for side, parts in enumerate((own, other))
             )
+            own, other = (own[0], own[1]), (other[0], other[1])
         return own, other
 
 
@@ -158,10 +166,20 @@
 
 
 def total_over_devices(value):
-    chips = lax.axis_size("dp")
+    bits = lax.axis_size("dp").bit_length() - 1
     value = value + core_swapped(value)
-    for bit in range(chips.bit_length() - 1):
-        value = value + flipped(value, (bit, bit))
+    for low in range(0, bits, 2):
+        first = flipped(value, (low, low))
+        if low + 1 < bits:
+            second = flipped(value, (low + 1, low + 1))
+            route = [(2 * d + c, 2 * (d ^ (3 << low)) + c) for d in range(1 << bits) for c in range(2)]
+            both = lax.ppermute(value, AXES, route)
+            bit, over = (lax.axis_index("dp") >> low & 1) == 0, (lax.axis_index("dp") >> low & 2) == 0
+            near = jnp.where(bit, value, first) + jnp.where(bit, first, value)
+            far_sum = jnp.where(bit, second, both) + jnp.where(bit, both, second)
+            value = jnp.where(over, near, far_sum) + jnp.where(over, far_sum, near)
+        else:
+            value = value + first
     return value
 
 
@@ -197,7 +215,7 @@
             vmem_limit_bytes=VMEM_LIMIT, dimension_semantics=("arbitrary",) * len(grid)
         ),
         cost_estimate=pl.CostEstimate(
-            flops=micros * 10_000_000_000, bytes_accessed=micros * 10_000_000, transcendentals=0
+            flops=micros * 300_000_000, bytes_accessed=micros * 300_000, transcendentals=0
         ),
     )(*operands)
 
@@ -216,6 +234,14 @@
 
 def struct(shape, dtype):
     return jax.ShapeDtypeStruct(shape, dtype)
+
+
+def streamed(array):
+    return pltpu.with_memory_space_constraint(array, pltpu.HBM)
+
+
+def far(shape, dtype):
+    return pltpu.HBM(shape, dtype)
 
 
 def dot(left, right):
@@ -264,18 +290,24 @@
     return jnp.sum(value, axis=0, keepdims=True)
 
 
-def fetches(order_ref, own_ref, other_ref, target, sems, rows, width, start=0, lane=0):
+def placed(refs, place):
+    count = refs[0].shape[0]
+    return refs[place // count].at[place % count]
+
+
+def fetches(order_ref, own_refs, other_refs, target, sems, rows, width, start=0, lane=0):
     core = order_ref[4, 0]
     copies = []
-    for b in range(sems.shape[0]):
+    for place in range(sems.shape[0]):
         pair = []
-        for side, ref in enumerate((own_ref, other_ref)):
+        for side, refs in enumerate((own_refs, other_refs)):
             half = core if side == 0 else 1 - core
+            row = pl.multiple_of(order_ref[side, place] * rows, rows)
             pair.append(
                 pltpu.make_async_copy(
-                    ref.at[order_ref[2 + side, b], :, pl.ds(lane, width)],
-                    target.at[pl.ds(b * rows, rows), pl.ds(pl.multiple_of(start + half * width, LANES), width)],
-                    sems.at[b, side],
+                    placed(refs, place).at[:, pl.ds(lane, width)],
+                    target.at[pl.ds(row, rows), pl.ds(pl.multiple_of(start + half * width, LANES), width)],
+                    sems.at[place, side],
                 )
             )
         copies.append(pair)
@@ -305,25 +337,27 @@
 def projection_forward(order, tokens, own, other, affine_rows, after=()):
     rows, width = tokens.shape
     half = width // 2
-    chips, block = own.shape[0], own.shape[1]
+    chips, block = 2 * own[0].shape[0], own[0].shape[1]
 
     def kernel(
-        order_ref, tokens_ref, own_ref, other_ref, w_ref, proj_ref, affine_ref, out_ref, columns, sems, column_sems
+        order_ref, tokens_ref, own_a, own_b, other_a, other_b,
+        w_ref, proj_ref, affine_ref, out_ref, columns, sems, column_sems,
     ):
+        own_refs, other_refs = (own_a, own_b), (other_a, other_b)
         step = pl.program_id(0)
         params = [
             pltpu.make_async_copy(
-                own_ref.at[order_ref[2, b], :, pl.ds(4 * half, LANES)],
-                columns.at[pl.ds(b * block, block), :],
-                column_sems.at[b],
+                placed(own_refs, p).at[:, pl.ds(4 * half, LANES)],
+                columns.at[pl.ds(pl.multiple_of(order_ref[0, p] * block, block), block), :],
+                column_sems.at[p],
             )
-            for b in range(chips)
+            for p in range(chips)
         ]
         parts = [
-            fetches(order_ref, own_ref, other_ref, w_ref, sems.at[k], block, half, k * width, k * half)
+            fetches(order_ref, own_refs, other_refs, w_ref, sems.at[k], block, half, k * width, k * half)
             for k in range(3)
         ]
-        parts.append(fetches(order_ref, own_ref, other_ref, proj_ref, sems.at[3], block, half, 0, 3 * half))
+        parts.append(fetches(order_ref, own_refs, other_refs, proj_ref, sems.at[3], block, half, 0, 3 * half))
 
         @pl.when(step == 0)
         def _():
@@ -354,9 +388,9 @@
     return call(
         kernel,
         (3,),
-        [(tokens, whole(tokens.shape)), (own, ANY), (other, ANY)],
-        [
-            (struct((width, 3 * width), BF16), whole((width, 3 * width))),
+        [(tokens, whole(tokens.shape)), *((blocks, ANY) for blocks in (*own, *other))],
+        [
+            (far((width, 3 * width), BF16), whole((width, 3 * width))),
             (struct((width, width), BF16), whole((width, width))),
             (struct((affine_rows, width), F32), whole((affine_rows, width))),
             (struct((rows, 3 * width), BF16), cols_of(rows, width)),
@@ -419,12 +453,12 @@
         ],
         [
             (
-                struct((spans, pairs, 2 * L, L), BF16),
+                far((spans, pairs, 2 * L, L), BF16),
                 pl.BlockSpec((each, pairs, 2 * L, L), lambda i, *_: (i, 0, 0, 0)),
             ),
-            (struct((rows, width), BF16), rows_of(PART, width)),
-            (struct((rows, width), F32), rows_of(PART, width)),
-            (struct((rows, LANES), F32), rows_of(PART, LANES)),
+            (far((rows, width), BF16), rows_of(PART, width)),
+            (far((rows, width), F32), rows_of(PART, width)),
+            (far((rows, LANES), F32), rows_of(PART, LANES)),
             (struct((rows, width), BF16), rows_of(PART, width)),
         ],
         (),
@@ -435,14 +469,16 @@
 
 def inner_forward(order, side, skip_low, blocks, affine, after=()):
     rows, width = skip_low.shape
-    chips, block, half = blocks.shape
-
-    def kernel(order_ref, skip_ref, blocks_ref, affine_ref, w_ref, act_ref, slope_ref, sems):
+    count, block, half = blocks[0].shape
+    chips = 2 * count
+
+    def kernel(order_ref, skip_ref, first_ref, second_ref, affine_ref, w_ref, act_ref, slope_ref, sems):
         step = pl.program_id(0)
 
-        def copies(b):
+        def copies(p):
+            row = pl.multiple_of(order_ref[side, p] * block, block)
             return pltpu.make_async_copy(
-                blocks_ref.at[order_ref[2 + side, b]], w_ref.at[pl.ds(b * block, block), :], sems.at[b]
+                placed((first_ref, second_ref), p), w_ref.at[pl.ds(row, block), :], sems.at[p]
             )
 
         @pl.when(step == 0)
@@ -473,11 +509,11 @@
     return call(
         kernel,
         (half // width,),
-        [(skip_low, whole(skip_low.shape)), (blocks, ANY), (affine, whole(affine.shape))],
-        [
-            (struct((width, half), BF16), whole((width, half))),
+        [(skip_low, whole(skip_low.shape)), (blocks[0], ANY), (blocks[1], ANY), (affine, whole(affine.shape))],
+        [
+            (far((width, half), BF16), whole((width, half))),
             (struct((rows, half), BF16), cols_of(rows, width)),
-            (struct((rows, half), BF16), cols_of(rows, width)),
+            (far((rows, half), BF16), cols_of(rows, width)),
         ],
         [pltpu.SemaphoreType.DMA((chips,))],
         10,
@@ -489,13 +525,13 @@
 def outer_forward(order, act_own, act_other, own, other, normed_one, affine, mlm_grad, live_rows, after=()):
     rows, wide = act_own.shape
     hidden, width = 2 * wide, normed_one.shape[1]
-    chips, block = own.shape[0], own.shape[1]
+    chips, block = 2 * own[0].shape[0], own[0].shape[1]
     spans = rows // L
     many = 2
     tile = many * PART
 
     def kernel(
-        order_ref, act_own_ref, act_other_ref, own_ref, other_ref, normed_one_ref, affine_ref, mlm_ref, live_ref,
+        order_ref, act_own_ref, act_other_ref, own_a, own_b, other_a, other_b, normed_one_ref, affine_ref, mlm_ref, live_ref,
         w_ref, out_ref, grad_ref, low_ref, sums_ref, cls_ref, cls_normed_ref, cls_inv_ref, sems,
     ):
         step = pl.program_id(0)
@@ -530,7 +566,7 @@
                 cls_normed_ref[to, :] = normed[row]
                 cls_inv_ref[to, :] = jnp.broadcast_to(inv[row], (1, LANES))
 
-        copies = fetches(order_ref, own_ref, other_ref, w_ref, sems, block, width // 2)
+        copies = fetches(order_ref, (own_a, own_b), (other_a, other_b), w_ref, sems, block, width // 2)
 
         @pl.when(step == 0)
         def _():
@@ -546,17 +582,16 @@
         [
             (act_own, rows_of(tile, wide)),
             (act_other, rows_of(tile, wide)),
-            (own, ANY),
-            (other, ANY),
-            (normed_one, rows_of(tile, width)),
+            *((blocks, ANY) for blocks in (*own, *other)),
+            (streamed(normed_one), rows_of(tile, width)),
             (affine, whole(affine.shape)),
-            (mlm_grad, rows_of(tile, width)),
+            (streamed(mlm_grad), rows_of(tile, width)),
             (live_rows, SMEM),
         ],
         [
-            (struct((hidden, width), BF16), whole((hidden, width))),
-            (struct((rows, width), BF16), rows_of(tile, width)),
-            (struct((rows, width), F32), rows_of(tile, width)),
+            (far((hidden, width), BF16), whole((hidden, width))),
+            (far((rows, width), BF16), rows_of(tile, width)),
+            (far((rows, width), F32), rows_of(tile, width)),
             (struct((rows, width), BF16), rows_of(tile, width)),
             (struct((8, width), F32), whole((8, width))),
             (struct((spans, width), F32), whole((spans, width))),
@@ -733,8 +768,8 @@
         (steps,),
         [
             (low, whole(low.shape)),
-            (slope, cols_of(rows, width)),
-            (outer_w, pl.BlockSpec((width, width), lambda i, table: (place(i, table), 0))),
+            (streamed(slope), cols_of(rows, width)),
+            (streamed(outer_w), pl.BlockSpec((width, width), lambda i, table: (place(i, table), 0))),
             (skip_low, whole(skip_low.shape)),
         ],
         [
@@ -798,17 +833,17 @@
         [
             (inner_own, rows_of(tile, half)),
             (inner_other, rows_of(tile, half)),
-            (w_own, whole(w_own.shape)),
-            (w_other, whole(w_other.shape)),
-            (grad_two, rows_of(tile, width)),
+            (streamed(w_own), whole(w_own.shape)),
+            (streamed(w_other), whole(w_other.shape)),
+            (streamed(grad_two), rows_of(tile, width)),
             (more, whole(more.shape)),
-            (normed_one, rows_of(tile, width)),
-            (inv_one, rows_of(tile, LANES)),
+            (streamed(normed_one), rows_of(tile, width)),
+            (streamed(inv_one), rows_of(tile, LANES)),
             (affine, whole(affine.shape)),
             (proj_w, whole(proj_w.shape)),
         ],
         [
-            (struct((rows, width), F32), rows_of(tile, width)),
+            (far((rows, width), F32), rows_of(tile, width)),
             (struct((rows, width), BF16), rows_of(tile, width)),
             (struct((8, width), F32), whole((8, width))),
             (struct((rows, width), BF16), rows_of(tile, width)),
@@ -868,8 +903,8 @@
         (spans // each,),
         [
             (context_grad, rows_of(each * L, width)),
-            (projected, rows_of(each * L, 3 * width)),
-            (attention, pl.BlockSpec((each, width // PAIR_LANES, 2 * L, L), lambda i, *_: (i, 0, 0, 0))),
+            (streamed(projected), rows_of(each * L, 3 * width)),
+            (streamed(attention), pl.BlockSpec((each, width // PAIR_LANES, 2 * L, L), lambda i, *_: (i, 0, 0, 0))),
         ],
         [
             (struct((rows, wide), BF16), rows_of(each * L, wide)),
@@ -964,7 +999,7 @@
         kernel,
         (rows // PART,),
         [(low, rows_of(PART, low.shape[1])) for low in qkv_lows]
-        + [(qkv_w, whole(qkv_w.shape)), (grad_one, rows_of(PART, width))],
+        + [(streamed(qkv_w), whole(qkv_w.shape)), (streamed(grad_one), rows_of(PART, width))],
         [(struct((rows, width), F32), rows_of(PART, width))],
         [pltpu.VMEM((PART, 3 * width), BF16)],
         8,
@@ -1065,8 +1100,8 @@
     return call(
         kernel,
         (1,),
-        [(a, whole(a.shape)) for a in (totals, *grads, *olds)],
-        [(struct(s, F32), whole(s)) for s in shapes for _ in range(3)]
+        [(a, whole(a.shape)) for a in (totals, *grads, *map(streamed, olds))],
+        [(far(s, F32), whole(s)) for s in shapes for _ in range(3)]
         + [(struct((8, LANES), F32), whole((8, LANES)))],
         (),
         4,
@@ -1099,7 +1134,9 @@
     rows, width = tokens.shape
     spans = rows // L
     half = width // 2
-    order = block_order()
+    chips = lax.axis_size("dp")
+    order = block_order(flip_steps(chips))
+    order_outer = block_order(near_first(chips))
     hidden = inner_weight.shape[1]
     pairs = width // PAIR_LANES
     affine_rows = affine_params.shape[0]
@@ -1110,7 +1147,7 @@
     block_two = chip_rows(inner_weight.astype(BF16), (hidden // 2,))
     block_three = chip_rows(outer_weight.astype(BF16), (half,))
     rows_chip, rows_outer = block_one.shape[0], block_three.shape[0]
-    table = kernel_order(order, rows_chip)
+    table, table_outer = kernel_order(order, rows_chip), kernel_order(order_outer, rows_chip)
 
     side = lax.axis_index("pair")
     own_ids, other_ids = pick(side, doc_ids[0], doc_ids[1]), pick(side, doc_ids[1], doc_ids[0])
@@ -1125,31 +1162,32 @@
     masks = jnp.stack([match, key_live, anchor_live]).astype(F32)
     live_rows = (own_count * L)[None]
 
-    one, two, three = Gather(block_one), Gather(block_two), Gather(block_three)
+    steps, steps_outer = flip_steps(chips), near_first(chips)
+    one, two, three = Gather(block_one, steps), Gather(block_two, steps), Gather(block_three, steps_outer)
     one.step()
+    three.step()
     first = one.step()
-    one.step()
-    two.step(first)
+    three.step(three.got)
+    first = (first, three.got)
+    one.step(*first)
+    two.step(*first)
     second = (one.got, two.got)
     one.step(*second)
     two.step(*second)
+    third = (one.got, two.got)
     three.step(*second)
-    third = (one.got, two.got, three.got)
     own, other = one.finish(order, rows_chip, *third)
     two.step(*third)
-    three.step(*third)
-    fourth = (two.got, three.got)
-    two.step(*fourth, other)
     qkv_w, proj_w, affine, projected = projection_forward(table, tokens, own, other, affine_rows)
-    three.step(two.got, projected)
+    two.step(two.got, projected)
+    three.step()
     attention, context, normed_one, inv_one, skip_low = attention_forward(tokens, projected, proj_w, affine)
-    own, other = two.finish(order, rows_chip)
-    three.step(skip_low)
+    own, other = two.finish(order, rows_chip, skip_low)
     w_own, act_own, slope_own = inner_forward(table, 0, skip_low, own, affine)
     w_other, act_other, slope_other = inner_forward(table, 1, skip_low, other, affine)
-    own, other = three.finish(order, rows_outer, act_own)
+    own, other = three.finish(order_outer, rows_outer, act_own)
     outer_w, layer_out, grad_two, low, sums_two, cls, cls_normed, cls_inv = outer_forward(
-        table, act_own, act_other, own, other, normed_one, affine, mlm_grad, live_rows
+        table_outer, act_own, act_other, own, other, normed_one, affine, mlm_grad, live_rows
     )
     low, more, sums_two, loss, own, other = outer_backward(
         table, low, sums_two, cls, core_swapped(cls), masks, cls_normed, cls_inv, act_own, act_other, affine
@@ -1157,40 +1195,36 @@
 
     red_outer = Reduce(*in_order(order, own, other, rows_outer))
     inner_other, bias_other, blocks_other = inner_backward(table, 1, low, slope_other, outer_w, skip_low)
-    got = red_outer.last()
-    inner_own, bias_own, blocks_own = inner_backward(table, 0, low, slope_own, outer_w, skip_low, (got,))
-    red_outer.step()
+    core_done = red_outer.last()
+    got = red_outer.step()
+    inner_own, bias_own, blocks_own = inner_backward(table, 0, low, slope_own, outer_w, skip_low, (core_done,))
     red_inner = Reduce(*in_order(order, blocks_own, blocks_other, rows_chip))
     grad_one, grad_one_low, sums_one, context_grad = skip_backward(
         inner_own, inner_other, w_own, w_other, grad_two, more, normed_one, inv_one, affine, proj_w,
-        (red_inner.last(),),
+        (red_inner.last(), got),
     )
     groups = (
         tuple(p for p in range(pairs) if p % (pairs // 2)),
         tuple(p for p in range(pairs) if not p % (pairs // 2)),
     )
     qkv_low, qkv_sums = [None, None], [None, None]
-    qkv_low[0], qkv_sums[0] = attention_backward(
-        groups[0], context_grad, projected, attention, (red_outer.last(),)
-    )
-    red_outer.step()
-    red_inner.step()
+    got_outer, got_inner = red_outer.step(), red_inner.step()
+    qkv_low[0], qkv_sums[0] = attention_backward(groups[0], context_grad, projected, attention)
+    own, other = qkv_backward(table, tokens, qkv_low[0], (context, grad_one_low), None, (got_outer,))
+    red_first = Reduce(*in_order(order, own, other, rows_chip))
+    core_done = red_first.last()
+    qkv_low[1], qkv_sums[1] = attention_backward(groups[1], context_grad, projected, attention, (got_inner,))
+    got_outer, got_inner = red_outer.step(), red_inner.step()
     own, other = qkv_backward(
-        table, tokens, qkv_low[0], (context, grad_one_low), None, (red_outer.last(),)
-    )
-    red_first = Reduce(*in_order(order, own, other, rows_chip))
-    red_outer.step()
-    qkv_low[1], qkv_sums[1] = attention_backward(
-        groups[1], context_grad, projected, attention, (red_inner.last(), red_outer.last(), red_first.last())
-    )
-    red_first.step()
-    red_inner.step()
-    own, other = qkv_backward(
-        table, tokens, qkv_low[1], None, (sums_one, sums_two, qkv_sums[1], qkv_sums[0], bias_own, bias_other)
-    )
+        table, tokens, qkv_low[1], None, (sums_one, sums_two, qkv_sums[1], qkv_sums[0], bias_own, bias_other),
+        (core_done,),
+    )
+    red_first.step(got_inner)
     red_second = Reduce(*in_order(order, own, other, rows_chip))
+    core_done = red_second.last()
     red_second.step()
-    input_grad = tokens_backward(groups, qkv_low, qkv_w, grad_one)
+    input_grad = tokens_backward(groups, qkv_low, qkv_w, grad_one, (core_done,))
+    red_first.step(input_grad)
     red_second.step(input_grad)
     outer_mine, outer_theirs, inner_mine, inner_theirs, squares = summed(
         table, (red_outer.finish(), red_inner.finish())

time: 338 us -> 290 us (0.86)
  local copies, waits for them, and re-layouts: 54.8 us -> 3.18 us
  Pallas kernels: 110 us -> 130 us
  other arithmetic: 16.8 us -> 9.13 us
  starting transfers between devices: 59.9 us -> 55.6 us
    unnamed x219 -> x26, local copies, waits for them, and re-layouts: 50.2 us -> 1.71 us
    pallas_call x17, Pallas kernels: 110 us -> 130 us  [call(): pl.pallas_call(body, grid_spec=pltpu.PrefetchScalarGridSpec(num_scalar_pr...]
    ppermute x32, starting transfers between devices: 56.6 us -> 44.9 us  [flipped(): return lax.ppermute(block, AXES, flip_route(chips, bits))]
    convert_element_type x16, other arithmetic: 9.21 us -> 2.47 us  [step(): sum((p[self.count:2 * self.count].astype(F32) for p in self.parts))]
    ppermute x32, waiting for transfers between devices: 82.6 us -> 76.3 us  [flipped(): return lax.ppermute(block, AXES, flip_route(chips, bits))]
    ppermute x0 -> x2, waiting for transfers between devices: none -> 4.69 us  [total_over_devices(): both = lax.ppermute(value, AXES, route)]
    ppermute x0 -> x2, starting transfers between devices: none -> 4.04 us  [total_over_devices(): both = lax.ppermute(value, AXES, route)]
    ppermute x16 -> x19, starting transfers between devices: 3.29 us -> 6.69 us  [core_swapped(): return lax.ppermute(block, AXES, core_route(lax.axis_size('dp')))]
  transfers between devices with their start and end apart: 48 -> 53, of which waited for: 26 -> 26; matrix products, arithmetic and copies ran while one was open for 6% -> 3% of each run, Pallas kernels for 24% -> 33%
where the time goes in v3:
time: 290 us; the launch traced here: 287 us
  Pallas kernels  130 us (45%)
  waiting for transfers between devices  85.4 us (29%)
  starting transfers between devices  55.6 us (19%)
  other arithmetic  9.13 us (3%)
  between operations  4.05 us (1%)
  local copies, waits for them, and re-layouts  3.18 us (1%)
    pallas_call x17, Pallas kernels, call(): pl.pallas_call(body, grid_spec=pltpu.PrefetchScalarGridSpec(num_scalar_pr...  130 us
    ppermute x32, waiting for transfers between devices, flipped(): return lax.ppermute(block, AXES, flip_route(chips, bits))  76.3 us
    ppermute x32, starting transfers between devices, flipped(): return lax.ppermute(block, AXES, flip_route(chips, bits))  44.9 us
    ppermute x19, starting transfers between devices, core_swapped(): return lax.ppermute(block, AXES, core_route(lax.axis_size('dp')))  6.69 us
  transfers between devices with their start and end apart: 53, of which 26 were waited for; matrix products, arithmetic and copies ran while one was open for 3% of the time, Pallas kernels for 33%

profile of v3, /device:TPU:0, one launch (start us, length us, event | category | flops | bytes accessed | tf_op | source)
XLA Modules:
  0.0 287.2 jit_solution(12394884881826134780)
XLA Ops:
  4.9 3.0 %collective-permute-start.1 = (bf16[1,48,1664]{2,1,0:T(8,128)(2,1)S(1)}, bf16[1,48,1664]{2,1,0:T(8,128)(2,1)S(1)}, u32[]{:S(2)}, u32[]{:S(2)}) collective-permute-start(bf16[1,48,1664]{2,1,0:T(8,128)(2,1)S(1)} %maximum_select_fusion), channel_id=1, source_target_pairs={{0,8},{1,17},{2,10},{3,19},{4,12},{5,21},{6,14},{7,23},{8,0},{9,25... | collective-permute-start | bytes 479240 | tf_op jit(solution)/shard_map/ppermute | solution.py:52
  8.9 3.6 %collective-permute-done.1 = bf16[1,48,1664]{2,1,0:T(8,128)(2,1)S(1)} collective-permute-done((bf16[1,48,1664]{2,1,0:T(8,128)(2,1)S(1)}, bf16[1,48,1664]{2,1,0:T(8,128)(2,1)S(1)}, u32[]{:S(2)}, u32[]{:S(2)}) %collective-permute-start.1) | collective-permute-done | bytes 159776 | tf_op jit(solution)/shard_map/ppermute | solution.py:52
  12.5 2.6 collective-permute-start.2
  16.7 3.7 %collective-permute-done.4 = bf16[1,192,384]{2,1,0:T(8,128)(2,1)S(1)} collective-permute-done((bf16[1,192,384]{2,1,0:T(8,128)(2,1)S(1)}, bf16[1,192,384]{2,1,0:T(8,128)(2,1)S(1)}, u32[]{:S(2)}, u32[]{:S(2)}) %collective-permute-start.4) | collective-permute-done | bytes 147488 | tf_op jit(solution)/shard_map/ppermute | solution.py:52
  22.4 5.0 %collective-permute-done.5 = bf16[2,192,384]{2,1,0:T(8,128)(2,1)S(1)} collective-permute-done((bf16[2,192,384]{2,1,0:T(8,128)(2,1)S(1)}, bf16[2,192,384]{2,1,0:T(8,128)(2,1)S(1)}, u32[]{:S(2)}, u32[]{:S(2)}) %collective-permute-start.5) | collective-permute-done | bytes 294944 | tf_op jit(solution)/shard_map/ppermute | solution.py:52
  30.3 4.4 %collective-permute-start.8 = (bf16[1,48,1536]{2,1,0:T(8,128)(2,1)S(1)}, bf16[1,48,1536]{2,1,0:T(8,128)(2,1)S(1)}, u32[]{:S(2)}, u32[]{:S(2)}) collective-permute-start(bf16[1,48,1536]{2,1,0:T(8,128)(2,1)S(1)} %maximum_select_fusion.2), channel_id=1, source_target_pairs={{0,8},{1,17},{2,10},{3,19},{4,12},{5,21},{6,14},{7,23},{8,0},{9,25... | collective-permute-start | bytes 442376 | tf_op jit(solution)/shard_map/ppermute | solution.py:52
  34.7 3.1 %collective-permute-done.6 = bf16[4,48,1664]{2,1,0:T(8,128)(2,1)S(1)} collective-permute-done((bf16[4,48,1664]{2,1,0:T(8,128)(2,1)S(1)}, bf16[4,48,1664]{2,1,0:T(8,128)(2,1)S(1)}, u32[]{:S(2)}, u32[]{:S(2)}) %collective-permute-start.6) | collective-permute-done | bytes 639008 | tf_op jit(solution)/shard_map/ppermute | solution.py:52
  40.6 6.8 %collective-permute-done.10 = bf16[2,48,1536]{2,1,0:T(8,128)(2,1)S(1)} collective-permute-done((bf16[2,48,1536]{2,1,0:T(8,128)(2,1)S(1)}, bf16[2,48,1536]{2,1,0:T(8,128)(2,1)S(1)}, u32[]{:S(2)}, u32[]{:S(2)}) %collective-permute-start.10) | collective-permute-done | bytes 294944 | tf_op jit(solution)/shard_map/ppermute | solution.py:52
  47.4 7.9 %collective-permute-done.9.refs_3_ = bf16[8,48,1664]{2,1,0:T(8,128)(2,1)S(1)} collective-permute-done((bf16[8,48,1664]{2,1,0:T(8,128)(2,1)S(1)}, bf16[8,48,1664]{2,1,0:T(8,128)(2,1)S(1)}, u32[]{:S(2)}, u32[]{:S(2)}) %collective-permute-start.9) | collective-permute-done | bytes 1277984 | tf_op jit(solution)/shard_map/ppermute | solution.py:52
  56.7 2.2 collective-permute-start.13
  59.1 3.9 %collective-permute-start.17 = (bf16[4,192,384]{2,1,0:T(8,128)(2,1)S(1)}, bf16[4,192,384]{2,1,0:T(8,128)(2,1)S(1)}, u32[]{:S(2)}, u32[]{:S(2)}) collective-permute-start(bf16[4,192,384]{2,1,0:T(8,128)(2,1)S(1)} %pad_maximum_fusion.5), channel_id=1, source_target_pairs={{0,8},{1,17},{2,10},{3,19},{4,12},{5,21},{6,14},{7,23},{8,0},{9,25... | collective-permute-start | bytes 1769480 | tf_op jit(solution)/shard_map/ppermute | solution.py:52
  63.0 4.1 %collective-permute-done.13 = bf16[4,48,1536]{2,1,0:T(8,128)(2,1)} collective-permute-done((bf16[4,48,1536]{2,1,0:T(8,128)(2,1)}, bf16[4,48,1536]{2,1,0:T(8,128)(2,1)}, u32[]{:S(2)}, u32[]{:S(2)}) %collective-permute-start.13) | collective-permute-done | bytes 589856 | tf_op jit(solution)/shard_map/ppermute | solution.py:52
  67.1 2.3 pad_maximum_fusion.1.refs_2_
  69.4 9.8 %shard_map.330 = (bf16[768,2304]{1,0:T(8,128)(2,1)}, bf16[768,768]{1,0:T(8,128)(2,1)S(1)}, f32[12,768]{1,0:T(8,128)S(1)}, bf16[1024,2304]{1,0:T(8,128)(2,1)S(1)}) custom-call(s32[5,16]{1,0:T(8,128)S(1)} %stack.6.refs_0_, bf16[1024,768]{1,0:T(8,128)(2,1)S(1)} %copy-done.3, bf16[8,48,1664]{2,1,0:T(8,128)(2,1)S(1)} %pad_maximum_fusion.refs_2_, ...), custom_call_target="tpu_custom_call" | custom-call | flops 2400000000 | bytes 2400000 | tf_op jit(solution)/shard_map/pallas_call | solution.py:204
  81.8 8.4 %shard_map.331 = (bf16[8,6,256,128]{3,2,1,0:T(8,128)(2,1)}, bf16[1024,768]{1,0:T(8,128)(2,1)}, f32[1024,768]{1,0:T(8,128)}, f32[1024,128]{1,0:T(8,128)}, bf16[1024,768]{1,0:T(8,128)(2,1)S(1)}) custom-call(bf16[1024,768]{1,0:T(8,128)(2,1)S(1)} %copy-done.3, bf16[1024,2304]{1,0:T(8,128)(2,1)S(1)} %get-tuple-element.116.refs_1_, ...), custom_call_target="tpu_custom_call" | custom-call | flops 3600000000 | bytes 3600000 | tf_op jit(solution)/shard_map/pallas_call | solution.py:204
  90.2 2.5 collective-permute-start.15
  92.7 3.1 %collective-permute-done.14.refs_3_ = bf16[8,48,1536]{2,1,0:T(8,128)(2,1)} collective-permute-done((bf16[8,48,1536]{2,1,0:T(8,128)(2,1)}, bf16[8,48,1536]{2,1,0:T(8,128)(2,1)}, u32[]{:S(2)}, u32[]{:S(2)}) %collective-permute-start.14) | collective-permute-done | bytes 1179680 | tf_op jit(solution)/shard_map/ppermute | solution.py:52
  95.8 8.2 %shard_map.332 = (bf16[768,1536]{1,0:T(8,128)(2,1)}, bf16[1024,1536]{1,0:T(8,128)(2,1)S(1)}, bf16[1024,1536]{1,0:T(8,128)(2,1)}) custom-call(s32[5,16]{1,0:T(8,128)S(1)} %stack.6.refs_0_, bf16[1024,768]{1,0:T(8,128)(2,1)S(1)} %get-tuple-element.119.refs_1_.refs_4_, bf16[8,48,1536]{2,1,0:T(8,128)(2,1)} %pad_maximum_fusion.1.refs_2_, ...), custom_call_target="tpu_custom_call" | custom-call | flops 3000000000 | bytes 3000000 | tf_op jit(solution)/shard_map/pallas_call | solution.py:204
  105.7 5.2 %collective-permute-done.18.refs_4_ = bf16[8,192,384]{2,1,0:T(8,128)(2,1)} collective-permute-done((bf16[8,192,384]{2,1,0:T(8,128)(2,1)S(1)}, bf16[8,192,384]{2,1,0:T(8,128)(2,1)}, u32[]{:S(2)}, u32[]{:S(2)}) %collective-permute-start.18) | collective-permute-done | bytes 1179680 | tf_op jit(solution)/shard_map/ppermute | solution.py:52
  114.8 8.5 %shard_map.333 = (bf16[768,1536]{1,0:T(8,128)(2,1)}, bf16[1024,1536]{1,0:T(8,128)(2,1)S(1)}, bf16[1024,1536]{1,0:T(8,128)(2,1)}) custom-call(s32[5,16]{1,0:T(8,128)S(1)} %stack.6.refs_0_, bf16[1024,768]{1,0:T(8,128)(2,1)S(1)} %get-tuple-element.119.refs_1_.refs_4_, bf16[8,48,1536]{2,1,0:T(8,128)(2,1)} %collective-permute-done.15.refs_2_, ...), custom_call_target="tpu_custom_call" | custom-call | flops 3000000000 | bytes 3000000 | tf_op jit(solution)/shard_map/pallas_call | solution.py:204
  123.3 14.7 %shard_map.334 = (bf16[3072,768]{1,0:T(8,128)(2,1)}, bf16[1024,768]{1,0:T(8,128)(2,1)}, f32[1024,768]{1,0:T(8,128)}, bf16[1024,768]{1,0:T(8,128)(2,1)S(1)}, f32[...) custom-call(s32[5,16]{1,0:T(8,128)S(1)} %stack.7.refs_0_, ...), custom_call_target="tpu_custom_call" | custom-call | flops 2400000000 | bytes 2400000 | tf_op jit(solution)/shard_map/pallas_call | solution.py:204
  139.3 14.8 %shard_map.335 = (bf16[1024,768]{1,0:T(8,128)(2,1)S(1)}, f32[8,768]{1,0:T(8,128)S(1)}, f32[8,768]{1,0:T(8,128)S(1)}, f32[8,128]{1,0:T(8,128)S(1)}, bf16[16,192,3...) custom-call(s32[5,16]{1,0:T(8,128)S(1)} %stack.6.refs_0_, bf16[1024,768]{1,0:T(8,128)(2,1)S(1)} %get-tuple-element.130.refs_1_, ...), custom_call_target="tpu_custom_call" | custom-call | flops 2400000000 | bytes 2400000 | tf_op jit(solution)/shard_map/pallas_call | solution.py:204
  154.3 8.3 %shard_map.337 = (bf16[1024,1536]{1,0:T(8,128)(2,1)S(1)}, f32[8,768]{1,0:T(8,128)S(1)}, bf16[16,48,1536]{2,1,0:T(8,128)(2,1)S(1)}) custom-call(s32[5,16]{1,0:T(8,128)S(1)} %stack.6.refs_0_, bf16[1024,768]{1,0:T(8,128)(2,1)S(1)} %get-tuple-element.135.refs_1_, bf16[1024,1536]{1,0:T(8,128)(2,1)} %get-tuple-element.140.refs_2_, ...), custom_call_target="tpu_custom_call" | custom-call | flops 2400000000 | bytes 2400000 | tf_op jit(solution)/shard_map/pallas_call | solution.py:204
  163.9 8.6 %shard_map.336 = (bf16[1024,1536]{1,0:T(8,128)(2,1)S(1)}, f32[8,768]{1,0:T(8,128)S(1)}, bf16[16,48,1536]{2,1,0:T(8,128)(2,1)S(1)}) custom-call(s32[5,16]{1,0:T(8,128)S(1)} %stack.6.refs_0_, bf16[1024,768]{1,0:T(8,128)(2,1)S(1)} %get-tuple-element.135.refs_1_, bf16[1024,1536]{1,0:T(8,128)(2,1)} %get-tuple-element.136.refs_2_, ...), custom_call_target="tpu_custom_call" | custom-call | flops 2400000000 | bytes 2400000 | tf_op jit(solution)/shard_map/pallas_call | solution.py:204
  174.4 5.1 %collective-permute-done.24.refs_11_.refs_3_ = bf16[8,192,384]{2,1,0:T(8,128)(2,1)S(1)} collective-permute-done((bf16[8,192,384]{2,1,0:T(8,128)(2,1)S(1)}, bf16[8,192,384]{2,1,0:T(8,128)(2,1)S(1)}, u32[]{:S(2)}, u32[]{:S(2)}) %collective-permute-start.24) | collective-permute-done | bytes 1179680 | tf_op jit(solution)/shard_map/ppermute | solution.py:52
  179.8 2.1 collective-permute-start.25
  181.9 12.6 %shard_map.338 = (f32[1024,768]{1,0:T(8,128)}, bf16[1024,768]{1,0:T(8,128)(2,1)S(1)}, f32[8,768]{1,0:T(8,128)S(1)}, bf16[1024,768]{1,0:T(8,128)(2,1)S(1)}) custom-call(bf16[1024,1536]{1,0:T(8,128)(2,1)S(1)} %get-tuple-element.139.refs_0_, bf16[1024,1536]{1,0:T(8,128)(2,1)S(1)} %get-tuple-element.141.refs_1_, bf16[768,1536]{1,0:T(8,128)(2,1)} %get-tuple-element.142.refs_2_, ...), custom_call_target="tpu_custom_call" | custom-call | flops 2400000000 | bytes 2400000 | tf_op jit(solution)/shard_map/pallas_call | solution.py:204
  194.5 8.5 %shard_map.339 = (bf16[1024,1536]{1,0:T(8,128)(2,1)S(1)}, f32[1,1536]{1,0:T(1,128)S(1)}) custom-call(bf16[1024,768]{1,0:T(8,128)(2,1)S(1)} %get-tuple-element.149.refs_0_, bf16[1024,2304]{1,0:T(8,128)(2,1)} %copy-done, bf16[8,6,256,128]{3,2,1,0:T(8,128)(2,1)} %get-tuple-element.150.refs_2_), custom_call_target="tpu_custom_call" | custom-call | flops 3600000000 | bytes 3600000 | tf_op jit(solution)/shard_map/pallas_call | solution.py:204
  203.0 4.5 %shard_map.340 = (bf16[16,48,1152]{2,1,0:T(8,128)(2,1)S(1)}, bf16[16,48,1152]{2,1,0:T(8,128)(2,1)S(1)}) custom-call(s32[5,16]{1,0:T(8,128)S(1)} %stack.6.refs_0_, bf16[1024,768]{1,0:T(8,128)(2,1)S(1)} %copy-done.4, bf16[1024,1536]{1,0:T(8,128)(2,1)S(1)} %get-tuple-element.151.refs_2_.refs_0_, bf16[1024,768]{1,0:T(8,128)(2,1)S(1)} %copy-done.5, ...), custom_call_target="tpu_custom_call" | custom-call | flops 1500000000 | bytes 1500000 | tf_op jit(solution)/shard_map/pallas_call | solution.py:204
  208.0 6.0 %shard_map.341 = (bf16[1024,768]{1,0:T(8,128)(2,1)S(1)}, f32[1,768]{1,0:T(1,128)S(1)}) custom-call(bf16[1024,768]{1,0:T(8,128)(2,1)S(1)} %get-tuple-element.149.refs_0_, bf16[1024,2304]{1,0:T(8,128)(2,1)} %copy-done, bf16[8,6,256,128]{3,2,1,0:T(8,128)(2,1)} %get-tuple-element.150.refs_2_, bf16[8,48,1536]{2,1,0:T(8,128)(2,1)S(1)} %collective-permute-done.27.refs_3_.refs_9_), custom_call_target="tpu_custom_call" | custom-call | flops 1800000000 | bytes 1800000 | tf_op jit(solution)/shard_map/pallas_call | solution.py:204
  214.0 3.8 %collective-permute-done.28.refs_10_ = bf16[4,48,1536]{2,1,0:T(8,128)(2,1)S(1)} collective-permute-done((bf16[4,48,1536]{2,1,0:T(8,128)(2,1)S(1)}, bf16[4,48,1536]{2,1,0:T(8,128)(2,1)S(1)}, u32[]{:S(2)}, u32[]{:S(2)}) %collective-permute-start.28) | collective-permute-done | bytes 589856 | tf_op jit(solution)/shard_map/ppermute | solution.py:52
  218.2 3.0 %collective-permute-start.38 = (bf16[2,192,384]{2,1,0:T(8,128)(2,1)S(1)}, bf16[2,192,384]{2,1,0:T(8,128)(2,1)S(1)}, u32[]{:S(2)}, u32[]{:S(2)}) collective-permute-start(bf16[2,192,384]{2,1,0:T(8,128)(2,1)S(1)} %add_convert_fusion.8), channel_id=1, source_target_pairs={{0,16},{1,9},{2,18},{3,11},{4,20},{5,13},{6,22},{7,15},{8,24},{9,1... | collective-permute-start | bytes 884744 | tf_op jit(solution)/shard_map/ppermute | solution.py:52
  221.2 2.1 shard_map.342
  224.2 5.2 %collective-permute-done.40.refs_11_ = bf16[2,48,1536]{2,1,0:T(8,128)(2,1)S(1)} collective-permute-done((bf16[2,48,1536]{2,1,0:T(8,128)(2,1)S(1)}, bf16[2,48,1536]{2,1,0:T(8,128)(2,1)S(1)}, u32[]{:S(2)}, u32[]{:S(2)}) %collective-permute-start.40) | collective-permute-done | bytes 294944 | tf_op jit(solution)/shard_map/ppermute | solution.py:52
  230.2 8.2 %shard_map.343 = f32[1024,768]{1,0:T(8,128)} custom-call(bf16[1024,1536]{1,0:T(8,128)(2,1)S(1)} %get-tuple-element.151.refs_2_.refs_0_, bf16[1024,768]{1,0:T(8,128)(2,1)S(1)} %get-tuple-element.158.refs_2_.refs_1_, bf16[768,2304]{1,0:T(8,128)(2,1)} %get-tuple-element.159.refs_2_, f32[1024,768]{1,0:T(8,128)} %get-tuple-element.160.refs_3_, ...), custom_call_target="tpu_custom_call" | custom-call | flops 2400000000 | bytes 2400000 | tf_op jit(solution)/shard_map/pallas_call | solution.py:204
  238.9 2.1 collective-permute-start.39
  243.0 4.0 %collective-permute-done.31.refs_4_ = bf16[4,48,1152]{2,1,0:T(8,128)(2,1)S(1)} collective-permute-done((bf16[4,48,1152]{2,1,0:T(8,128)(2,1)S(1)}, bf16[4,48,1152]{2,1,0:T(8,128)(2,1)S(1)}, u32[]{:S(2)}, u32[]{:S(2)}) %collective-permute-start.31) | collective-permute-done | bytes 442400 | tf_op jit(solution)/shard_map/ppermute | solution.py:52
  247.1 1.9 collective-permute-start.32
  249.1 2.0 collective-permute-start.36
  251.1 8.9 %collective-permute-done.32.refs_5_ = bf16[2,48,1152]{2,1,0:T(8,128)(2,1)S(1)} collective-permute-done((bf16[2,48,1152]{2,1,0:T(8,128)(2,1)S(1)}, bf16[2,48,1152]{2,1,0:T(8,128)(2,1)S(1)}, u32[]{:S(2)}, u32[]{:S(2)}) %collective-permute-start.32) | collective-permute-done | bytes 221216 | tf_op jit(solution)/shard_map/ppermute | solution.py:52
  260.1 1.8 collective-permute-done.36.refs_11_
  263.4 2.7 collective-permute-done.37.refs_12_
  269.8 2.0 collective-permute-start.45
  272.5 1.9 collective-permute-done.45
  274.5 2.1 collective-permute-start.47
  276.7 2.1 collective-permute-start.48
  279.3 2.8 collective-permute-done.48
  282.1 4.4 %shard_map.346 = (f32[24,2304]{1,0:T(8,128)}, f32[24,2304]{1,0:T(8,128)}, f32[24,2304]{1,0:T(8,128)}, f32[24,768]{1,0:T(8,128)}, f32[24,768]{1,0:T(8,128)}, /*in...) custom-call(s32[5,16]{1,0:T(8,128)S(1)} %stack.6.refs_0_, ...), custom_call_target="tpu_custom_call" | custom-call | flops 1200000000 | bytes 1200000 | tf_op jit(solution)/shard_map/pallas_call | solution.py:204
  (160 shorter events, 38.7 us)
Async XLA Ops:
  4.9 7.5 %collective-permute-start.1 = (bf16[1,48,1664]{2,1,0:T(8,128)(2,1)S(1)}, bf16[1,48,1664]{2,1,0:T(8,128)(2,1)S(1)}, u32[]{:S(2)}, u32[]{:S(2)}) collective-permute-start(bf16[1,48,1664]{2,1,0:T(8,128)(2,1)S(1)} %maximum_select_fusion), channel_id=1, source_target_pairs={{0,8},{1,17},{2,10},{3,19},{4,12},{5,21},{6,14},{7,23},{8,0},{9,25... | collective-permute-start | bytes 479240 | tf_op jit(solution)/shard_map/ppermute | solution.py:52
  7.9 7.2 %collective-permute-start.3 = (bf16[96,384]{1,0:T(8,128)(2,1)S(1)}, bf16[96,384]{1,0:T(8,128)(2,1)S(1)}, u32[]{:S(2)}, u32[]{:S(2)}) collective-permute-start(bf16[96,384]{1,0:T(8,128)(2,1)S(1)} %get-tuple-element.202), channel_id=1, source_target_pairs={{0,1},{1,0},{2,3},{3,2},{4,5},{5,4},{6,7},{7,6},{8,9},{9,8},{10,11... | collective-permute-start | bytes 221192 | tf_op jit(solution)/shard_map/ppermute | solution.py:56
  12.5 9.8 %collective-permute-start.2 = (bf16[2,48,1664]{2,1,0:T(8,128)(2,1)S(1)}, bf16[2,48,1664]{2,1,0:T(8,128)(2,1)S(1)}, u32[]{:S(2)}, u32[]{:S(2)}) collective-permute-start(bf16[2,48,1664]{2,1,0:T(8,128)(2,1)S(1)} %pad_maximum_fusion.6), channel_id=1, source_target_pairs={{0,16},{1,9},{2,18},{3,11},{4,20},{5,13},{6,22},{7,15},{8,24},{9,1... | collective-permute-start | bytes 958472 | tf_op jit(solution)/shard_map/ppermute | solution.py:52
  15.1 5.2 %collective-permute-start.4 = (bf16[1,192,384]{2,1,0:T(8,128)(2,1)S(1)}, bf16[1,192,384]{2,1,0:T(8,128)(2,1)S(1)}, u32[]{:S(2)}, u32[]{:S(2)}) collective-permute-start(bf16[1,192,384]{2,1,0:T(8,128)(2,1)S(1)} %maximum_select_fusion.1), channel_id=1, source_target_pairs={{0,2},{1,5},{2,0},{3,7},{4,6},{5,1},{6,4},{7,3},{8,10},{9,13},{10,... | collective-permute-start | bytes 442376 | tf_op jit(solution)/shard_map/ppermute | solution.py:52
  20.4 7.0 %collective-permute-start.5 = (bf16[2,192,384]{2,1,0:T(8,128)(2,1)S(1)}, bf16[2,192,384]{2,1,0:T(8,128)(2,1)S(1)}, u32[]{:S(2)}, u32[]{:S(2)}) collective-permute-start(bf16[2,192,384]{2,1,0:T(8,128)(2,1)S(1)} %pad_maximum_fusion.7), channel_id=1, source_target_pairs={{0,4},{1,3},{2,6},{3,1},{4,0},{5,7},{6,2},{7,5},{8,12},{9,11},{10,... | collective-permute-start | bytes 884744 | tf_op jit(solution)/shard_map/ppermute | solution.py:52
  27.4 10.4 %collective-permute-start.6 = (bf16[4,48,1664]{2,1,0:T(8,128)(2,1)S(1)}, bf16[4,48,1664]{2,1,0:T(8,128)(2,1)S(1)}, u32[]{:S(2)}, u32[]{:S(2)}) collective-permute-start(bf16[4,48,1664]{2,1,0:T(8,128)(2,1)S(1)} %pad_maximum_fusion.3), channel_id=1, source_target_pairs={{0,2},{1,5},{2,0},{3,7},{4,6},{5,1},{6,4},{7,3},{8,10},{9,13},{10,... | collective-permute-start | bytes 1916936 | tf_op jit(solution)/shard_map/ppermute | solution.py:52
  30.3 7.7 %collective-permute-start.8 = (bf16[1,48,1536]{2,1,0:T(8,128)(2,1)S(1)}, bf16[1,48,1536]{2,1,0:T(8,128)(2,1)S(1)}, u32[]{:S(2)}, u32[]{:S(2)}) collective-permute-start(bf16[1,48,1536]{2,1,0:T(8,128)(2,1)S(1)} %maximum_select_fusion.2), channel_id=1, source_target_pairs={{0,8},{1,17},{2,10},{3,19},{4,12},{5,21},{6,14},{7,23},{8,0},{9,25... | collective-permute-start | bytes 442376 | tf_op jit(solution)/shard_map/ppermute | solution.py:52
  38.0 17.3 %collective-permute-start.9 = (bf16[8,48,1664]{2,1,0:T(8,128)(2,1)S(1)}, bf16[8,48,1664]{2,1,0:T(8,128)(2,1)S(1)}, u32[]{:S(2)}, u32[]{:S(2)}) collective-permute-start(bf16[8,48,1664]{2,1,0:T(8,128)(2,1)S(1)} %pad_maximum_fusion.refs_2_), channel_id=1, source_target_pairs={{0,4},{1,3},{2,6},{3,1},{4,0},{5,7},{6,2},{7,5},{8,12},{9,11},{10,... | collective-permute-start | bytes 3833864 | tf_op jit(solution)/shard_map/ppermute | solution.py:52
  39.6 7.8 %collective-permute-start.10 = (bf16[2,48,1536]{2,1,0:T(8,128)(2,1)S(1)}, bf16[2,48,1536]{2,1,0:T(8,128)(2,1)S(1)}, u32[]{:S(2)}, u32[]{:S(2)}) collective-permute-start(bf16[2,48,1536]{2,1,0:T(8,128)(2,1)S(1)} %pad_maximum_fusion.8), channel_id=1, source_target_pairs={{0,16},{1,9},{2,18},{3,11},{4,20},{5,13},{6,22},{7,15},{8,24},{9,1... | collective-permute-start | bytes 884744 | tf_op jit(solution)/shard_map/ppermute | solution.py:52
  55.3 14.0 %collective-permute-start.12 = (bf16[8,48,1664]{2,1,0:T(8,128)(2,1)S(1)}, bf16[8,48,1664]{2,1,0:T(8,128)(2,1)}, u32[]{:S(2)}, u32[]{:S(2)}) collective-permute-start(bf16[8,48,1664]{2,1,0:T(8,128)(2,1)S(1)} %collective-permute-done.9.refs_3_), channel_id=1, source_target_pairs={{0,1},{1,0},{2,3},{3,2},{4,5},{5,4},{6,7},{7,6},{8,9},{9,8},{10,11... | collective-permute-start | bytes 3833864 | tf_op jit(solution)/shard_map/ppermute | solution.py:56
  55.3 14.0 %collective-permute-start.11 = (bf16[8,48,1664]{2,1,0:T(8,128)(2,1)S(1)}, bf16[8,48,1664]{2,1,0:T(8,128)(2,1)}, u32[]{:S(2)}, u32[]{:S(2)}) collective-permute-start(bf16[8,48,1664]{2,1,0:T(8,128)(2,1)S(1)} %pad_maximum_fusion.refs_2_), channel_id=1, source_target_pairs={{0,1},{1,0},{2,3},{3,2},{4,5},{5,4},{6,7},{7,6},{8,9},{9,8},{10,11... | collective-permute-start | bytes 3833864 | tf_op jit(solution)/shard_map/ppermute | solution.py:56
  56.7 10.4 %collective-permute-start.13 = (bf16[4,48,1536]{2,1,0:T(8,128)(2,1)}, bf16[4,48,1536]{2,1,0:T(8,128)(2,1)}, u32[]{:S(2)}, u32[]{:S(2)}) collective-permute-start(bf16[4,48,1536]{2,1,0:T(8,128)(2,1)} %pad_maximum_fusion.4), channel_id=1, source_target_pairs={{0,2},{1,5},{2,0},{3,7},{4,6},{5,1},{6,4},{7,3},{8,10},{9,13},{10,... | collective-permute-start | bytes 1769480 | tf_op jit(solution)/shard_map/ppermute | solution.py:52
  59.1 21.8 %collective-permute-start.17 = (bf16[4,192,384]{2,1,0:T(8,128)(2,1)S(1)}, bf16[4,192,384]{2,1,0:T(8,128)(2,1)S(1)}, u32[]{:S(2)}, u32[]{:S(2)}) collective-permute-start(bf16[4,192,384]{2,1,0:T(8,128)(2,1)S(1)} %pad_maximum_fusion.5), channel_id=1, source_target_pairs={{0,8},{1,17},{2,10},{3,19},{4,12},{5,21},{6,14},{7,23},{8,0},{9,25... | collective-permute-start | bytes 1769480 | tf_op jit(solution)/shard_map/ppermute | solution.py:52
  79.2 16.6 %collective-permute-start.14 = (bf16[8,48,1536]{2,1,0:T(8,128)(2,1)}, bf16[8,48,1536]{2,1,0:T(8,128)(2,1)}, u32[]{:S(2)}, u32[]{:S(2)}) collective-permute-start(bf16[8,48,1536]{2,1,0:T(8,128)(2,1)} %pad_maximum_fusion.1.refs_2_), channel_id=1, source_target_pairs={{0,4},{1,3},{2,6},{3,1},{4,0},{5,7},{6,2},{7,5},{8,12},{9,11},{10,... | collective-permute-start | bytes 3538952 | tf_op jit(solution)/shard_map/ppermute | solution.py:52
  81.0 30.0 %collective-permute-start.18 = (bf16[8,192,384]{2,1,0:T(8,128)(2,1)S(1)}, bf16[8,192,384]{2,1,0:T(8,128)(2,1)}, u32[]{:S(2)}, u32[]{:S(2)}) collective-permute-start(bf16[8,192,384]{2,1,0:T(8,128)(2,1)S(1)} %pad_maximum_fusion.2.refs_3_), channel_id=1, source_target_pairs={{0,16},{1,9},{2,18},{3,11},{4,20},{5,13},{6,22},{7,15},{8,24},{9,1... | collective-permute-start | bytes 3538952 | tf_op jit(solution)/shard_map/ppermute | solution.py:52
  90.2 24.6 %collective-permute-start.15 = (bf16[8,48,1536]{2,1,0:T(8,128)(2,1)}, bf16[8,48,1536]{2,1,0:T(8,128)(2,1)}, u32[]{:S(2)}, u32[]{:S(2)}) collective-permute-start(bf16[8,48,1536]{2,1,0:T(8,128)(2,1)} %pad_maximum_fusion.1.refs_2_), channel_id=1, source_target_pairs={{0,1},{1,0},{2,3},{3,2},{4,5},{5,4},{6,7},{7,6},{8,9},{9,8},{10,11... | collective-permute-start | bytes 3538952 | tf_op jit(solution)/shard_map/ppermute | solution.py:56
  95.8 19.0 %collective-permute-start.16 = (bf16[8,48,1536]{2,1,0:T(8,128)(2,1)}, bf16[8,48,1536]{2,1,0:T(8,128)(2,1)}, u32[]{:S(2)}, u32[]{:S(2)}) collective-permute-start(bf16[8,48,1536]{2,1,0:T(8,128)(2,1)} %collective-permute-done.14.refs_3_), channel_id=1, source_target_pairs={{0,1},{1,0},{2,3},{3,2},{4,5},{5,4},{6,7},{7,6},{8,9},{9,8},{10,11... | collective-permute-start | bytes 3538952 | tf_op jit(solution)/shard_map/ppermute | solution.py:56
  110.9 12.3 %collective-permute-start.20 = (bf16[8,192,384]{2,1,0:T(8,128)(2,1)}, bf16[8,192,384]{2,1,0:T(8,128)(2,1)}, u32[]{:S(2)}, u32[]{:S(2)}) collective-permute-start(bf16[8,192,384]{2,1,0:T(8,128)(2,1)} %collective-permute-done.18.refs_4_), channel_id=1, source_target_pairs={{0,1},{1,0},{2,3},{3,2},{4,5},{5,4},{6,7},{7,6},{8,9},{9,8},{10,11... | collective-permute-start | bytes 3538952 | tf_op jit(solution)/shard_map/ppermute | solution.py:56
  110.9 12.4 %collective-permute-start.19 = (bf16[8,192,384]{2,1,0:T(8,128)(2,1)S(1)}, bf16[8,192,384]{2,1,0:T(8,128)(2,1)}, u32[]{:S(2)}, u32[]{:S(2)}) collective-permute-start(bf16[8,192,384]{2,1,0:T(8,128)(2,1)S(1)} %pad_maximum_fusion.2.refs_3_), channel_id=1, source_target_pairs={{0,1},{1,0},{2,3},{3,2},{4,5},{5,4},{6,7},{7,6},{8,9},{9,8},{10,11... | collective-permute-start | bytes 3538952 | tf_op jit(solution)/shard_map/ppermute | solution.py:56
  154.1 8.9 %collective-permute-start.22 = (bf16[16,192,384]{2,1,0:T(8,128)(2,1)S(1)}, bf16[16,192,384]{2,1,0:T(8,128)(2,1)S(1)}, u32[]{:S(2)}, u32[]{:S(2)}) collective-permute-start(bf16[16,192,384]{2,1,0:T(8,128)(2,1)S(1)} %get-tuple-element.138), channel_id=1, source_target_pairs={{0,1},{1,0},{2,3},{3,2},{4,5},{5,4},{6,7},{7,6},{8,9},{9,8},{10,11... | collective-permute-start | bytes 7077896 | tf_op jit(solution)/shard_map/ppermute | solution.py:56
  162.6 9.9 %collective-permute-start.23 = (bf16[16,48,1536]{2,1,0:T(8,128)(2,1)S(1)}, bf16[16,48,1536]{2,1,0:T(8,128)(2,1)S(1)}, u32[]{:S(2)}, u32[]{:S(2)}) collective-permute-start(bf16[16,48,1536]{2,1,0:T(8,128)(2,1)S(1)} %get-tuple-element.147), channel_id=1, source_target_pairs={{0,1},{1,0},{2,3},{3,2},{4,5},{5,4},{6,7},{7,6},{8,9},{9,8},{10,11... | collective-permute-start | bytes 7077896 | tf_op jit(solution)/shard_map/ppermute | solution.py:56
  163.3 16.3 %collective-permute-start.24 = (bf16[8,192,384]{2,1,0:T(8,128)(2,1)S(1)}, bf16[8,192,384]{2,1,0:T(8,128)(2,1)S(1)}, u32[]{:S(2)}, u32[]{:S(2)}) collective-permute-start(bf16[8,192,384]{2,1,0:T(8,128)(2,1)S(1)} %add_convert_fusion.1), channel_id=1, source_target_pairs={{0,4},{1,3},{2,6},{3,1},{4,0},{5,7},{6,2},{7,5},{8,12},{9,11},{10,... | collective-permute-start | bytes 3538952 | tf_op jit(solution)/shard_map/ppermute | solution.py:52
  172.8 34.8 %collective-permute-start.27 = (bf16[8,48,1536]{2,1,0:T(8,128)(2,1)S(1)}, bf16[8,48,1536]{2,1,0:T(8,128)(2,1)S(1)}, u32[]{:S(2)}, u32[]{:S(2)}) collective-permute-start(bf16[8,48,1536]{2,1,0:T(8,128)(2,1)S(1)} %add_convert_fusion), channel_id=1, source_target_pairs={{0,4},{1,3},{2,6},{3,1},{4,0},{5,7},{6,2},{7,5},{8,12},{9,11},{10,... | collective-permute-start | bytes 3538952 | tf_op jit(solution)/shard_map/ppermute | solution.py:52
  179.8 23.2 %collective-permute-start.25 = (bf16[4,192,384]{2,1,0:T(8,128)(2,1)S(1)}, bf16[4,192,384]{2,1,0:T(8,128)(2,1)S(1)}, u32[]{:S(2)}, u32[]{:S(2)}) collective-permute-start(bf16[4,192,384]{2,1,0:T(8,128)(2,1)S(1)} %add_convert_fusion.4), channel_id=1, source_target_pairs={{0,2},{1,5},{2,0},{3,7},{4,6},{5,1},{6,4},{7,3},{8,10},{9,13},{10,... | collective-permute-start | bytes 1769480 | tf_op jit(solution)/shard_map/ppermute | solution.py:52
  207.5 13.6 %collective-permute-start.26 = (bf16[16,48,1152]{2,1,0:T(8,128)(2,1)S(1)}, bf16[16,48,1152]{2,1,0:T(8,128)(2,1)S(1)}, u32[]{:S(2)}, u32[]{:S(2)}) collective-permute-start(bf16[16,48,1152]{2,1,0:T(8,128)(2,1)S(1)} %get-tuple-element.155), channel_id=1, source_target_pairs={{0,1},{1,0},{2,3},{3,2},{4,5},{5,4},{6,7},{7,6},{8,9},{9,8},{10,11... | collective-permute-start | bytes 5308424 | tf_op jit(solution)/shard_map/ppermute | solution.py:56
  207.9 9.9 %collective-permute-start.28 = (bf16[4,48,1536]{2,1,0:T(8,128)(2,1)S(1)}, bf16[4,48,1536]{2,1,0:T(8,128)(2,1)S(1)}, u32[]{:S(2)}, u32[]{:S(2)}) collective-permute-start(bf16[4,48,1536]{2,1,0:T(8,128)(2,1)S(1)} %add_convert_fusion.3), channel_id=1, source_target_pairs={{0,2},{1,5},{2,0},{3,7},{4,6},{5,1},{6,4},{7,3},{8,10},{9,13},{10,... | collective-permute-start | bytes 1769480 | tf_op jit(solution)/shard_map/ppermute | solution.py:52
  218.0 11.4 %collective-permute-start.40 = (bf16[2,48,1536]{2,1,0:T(8,128)(2,1)S(1)}, bf16[2,48,1536]{2,1,0:T(8,128)(2,1)S(1)}, u32[]{:S(2)}, u32[]{:S(2)}) collective-permute-start(bf16[2,48,1536]{2,1,0:T(8,128)(2,1)S(1)} %add_convert_fusion.7), channel_id=1, source_target_pairs={{0,16},{1,9},{2,18},{3,11},{4,20},{5,13},{6,22},{7,15},{8,24},{9,1... | collective-permute-start | bytes 884744 | tf_op jit(solution)/shard_map/ppermute | solution.py:52
  218.2 20.6 %collective-permute-start.38 = (bf16[2,192,384]{2,1,0:T(8,128)(2,1)S(1)}, bf16[2,192,384]{2,1,0:T(8,128)(2,1)S(1)}, u32[]{:S(2)}, u32[]{:S(2)}) collective-permute-start(bf16[2,192,384]{2,1,0:T(8,128)(2,1)S(1)} %add_convert_fusion.8), channel_id=1, source_target_pairs={{0,16},{1,9},{2,18},{3,11},{4,20},{5,13},{6,22},{7,15},{8,24},{9,1... | collective-permute-start | bytes 884744 | tf_op jit(solution)/shard_map/ppermute | solution.py:52
  223.3 6.2 %collective-permute-start.30 = (bf16[16,48,512]{2,1,0:T(8,128)(2,1)S(1)}, bf16[16,48,512]{2,1,0:T(8,128)(2,1)S(1)}, u32[]{:S(2)}, u32[]{:S(2)}) collective-permute-start(bf16[16,48,512]{2,1,0:T(8,128)(2,1)S(1)} %get-tuple-element.167), channel_id=1, source_target_pairs={{0,1},{1,0},{2,3},{3,2},{4,5},{5,4},{6,7},{7,6},{8,9},{9,8},{10,11... | collective-permute-start | bytes 2359304 | tf_op jit(solution)/shard_map/ppermute | solution.py:56
  223.6 14.8 %collective-permute-start.29 = (bf16[8,48,1152]{2,1,0:T(8,128)(2,1)S(1)}, bf16[8,48,1152]{2,1,0:T(8,128)(2,1)S(1)}, u32[]{:S(2)}, u32[]{:S(2)}) collective-permute-start(bf16[8,48,1152]{2,1,0:T(8,128)(2,1)S(1)} %add_convert_fusion.2), channel_id=1, source_target_pairs={{0,4},{1,3},{2,6},{3,1},{4,0},{5,7},{6,2},{7,5},{8,12},{9,11},{10,... | collective-permute-start | bytes 2654216 | tf_op jit(solution)/shard_map/ppermute | solution.py:52
  229.5 32.8 %collective-permute-start.41 = (bf16[1,48,1536]{2,1,0:T(8,128)(2,1)S(1)}, bf16[1,48,1536]{2,1,0:T(8,128)(2,1)S(1)}, u32[]{:S(2)}, u32[]{:S(2)}) collective-permute-start(bf16[1,48,1536]{2,1,0:T(8,128)(2,1)S(1)} %add_convert_fusion.11), channel_id=1, source_target_pairs={{0,8},{1,17},{2,10},{3,19},{4,12},{5,21},{6,14},{7,23},{8,0},{9,25... | collective-permute-start | bytes 442376 | tf_op jit(solution)/shard_map/ppermute | solution.py:52
  229.7 12.9 %collective-permute-start.34 = (bf16[8,48,512]{2,1,0:T(8,128)(2,1)S(1)}, bf16[8,48,512]{2,1,0:T(8,128)(2,1)S(1)}, u32[]{:S(2)}, u32[]{:S(2)}) collective-permute-start(bf16[8,48,512]{2,1,0:T(8,128)(2,1)S(1)} %add_convert_fusion.6), channel_id=1, source_target_pairs={{0,4},{1,3},{2,6},{3,1},{4,0},{5,7},{6,2},{7,5},{8,12},{9,11},{10,... | collective-permute-start | bytes 1179656 | tf_op jit(solution)/shard_map/ppermute | solution.py:52
  238.6 8.4 %collective-permute-start.31 = (bf16[4,48,1152]{2,1,0:T(8,128)(2,1)S(1)}, bf16[4,48,1152]{2,1,0:T(8,128)(2,1)S(1)}, u32[]{:S(2)}, u32[]{:S(2)}) collective-permute-start(bf16[4,48,1152]{2,1,0:T(8,128)(2,1)S(1)} %add_convert_fusion.5), channel_id=1, source_target_pairs={{0,2},{1,5},{2,0},{3,7},{4,6},{5,1},{6,4},{7,3},{8,10},{9,13},{10,... | collective-permute-start | bytes 1327112 | tf_op jit(solution)/shard_map/ppermute | solution.py:52
  238.9 23.4 %collective-permute-start.39 = (bf16[1,192,384]{2,1,0:T(8,128)(2,1)S(1)}, bf16[1,192,384]{2,1,0:T(8,128)(2,1)S(1)}, u32[]{:S(2)}, u32[]{:S(2)}) collective-permute-start(bf16[1,192,384]{2,1,0:T(8,128)(2,1)S(1)} %add_convert_fusion.12), channel_id=1, source_target_pairs={{0,8},{1,17},{2,10},{3,19},{4,12},{5,21},{6,14},{7,23},{8,0},{9,25... | collective-permute-start | bytes 442376 | tf_op jit(solution)/shard_map/ppermute | solution.py:52
  242.7 6.4 %collective-permute-start.35 = (bf16[4,48,512]{2,1,0:T(8,128)(2,1)S(1)}, bf16[4,48,512]{2,1,0:T(8,128)(2,1)S(1)}, u32[]{:S(2)}, u32[]{:S(2)}) collective-permute-start(bf16[4,48,512]{2,1,0:T(8,128)(2,1)S(1)} %add_convert_fusion.10), channel_id=1, source_target_pairs={{0,2},{1,5},{2,0},{3,7},{4,6},{5,1},{6,4},{7,3},{8,10},{9,13},{10,... | collective-permute-start | bytes 589832 | tf_op jit(solution)/shard_map/ppermute | solution.py:52
  247.1 12.9 %collective-permute-start.32 = (bf16[2,48,1152]{2,1,0:T(8,128)(2,1)S(1)}, bf16[2,48,1152]{2,1,0:T(8,128)(2,1)S(1)}, u32[]{:S(2)}, u32[]{:S(2)}) collective-permute-start(bf16[2,48,1152]{2,1,0:T(8,128)(2,1)S(1)} %add_convert_fusion.9), channel_id=1, source_target_pairs={{0,16},{1,9},{2,18},{3,11},{4,20},{5,13},{6,22},{7,15},{8,24},{9,1... | collective-permute-start | bytes 663560 | tf_op jit(solution)/shard_map/ppermute | solution.py:52
  249.1 12.8 %collective-permute-start.36 = (bf16[2,48,512]{2,1,0:T(8,128)(2,1)S(1)}, bf16[2,48,512]{2,1,0:T(8,128)(2,1)S(1)}, u32[]{:S(2)}, u32[]{:S(2)}) collective-permute-start(bf16[2,48,512]{2,1,0:T(8,128)(2,1)S(1)} %add_convert_fusion.14), channel_id=1, source_target_pairs={{0,16},{1,9},{2,18},{3,11},{4,20},{5,13},{6,22},{7,15},{8,24},{9,1... | collective-permute-start | bytes 294920 | tf_op jit(solution)/shard_map/ppermute | solution.py:52
  260.1 6.1 %collective-permute-start.33 = (bf16[1,48,1152]{2,1,0:T(8,128)(2,1)S(1)}, bf16[1,48,1152]{2,1,0:T(8,128)(2,1)S(1)}, u32[]{:S(2)}, u32[]{:S(2)}) collective-permute-start(bf16[1,48,1152]{2,1,0:T(8,128)(2,1)S(1)} %add_convert_fusion.13), channel_id=1, source_target_pairs={{0,8},{1,17},{2,10},{3,19},{4,12},{5,21},{6,14},{7,23},{8,0},{9,25... | collective-permute-start | bytes 331784 | tf_op jit(solution)/shard_map/ppermute | solution.py:52
  262.0 4.2 %collective-permute-start.37 = (bf16[1,48,512]{2,1,0:T(8,128)(2,1)S(1)}, bf16[1,48,512]{2,1,0:T(8,128)(2,1)S(1)}, u32[]{:S(2)}, u32[]{:S(2)}) collective-permute-start(bf16[1,48,512]{2,1,0:T(8,128)(2,1)S(1)} %add_convert_fusion.15), channel_id=1, source_target_pairs={{0,8},{1,17},{2,10},{3,19},{4,12},{5,21},{6,14},{7,23},{8,0},{9,25... | collective-permute-start | bytes 147464 | tf_op jit(solution)/shard_map/ppermute | solution.py:52
  268.3 4.1 %collective-permute-start.43 = (f32[8,128]{1,0:T(8,128)S(1)}, f32[8,128]{1,0:T(8,128)S(1)}, u32[]{:S(2)}, u32[]{:S(2)}) collective-permute-start(f32[8,128]{1,0:T(8,128)S(1)} %add.543), channel_id=1, source_target_pairs={{0,2},{1,3},{2,0},{3,1},{4,6},{5,7},{6,4},{7,5},{8,10},{9,11},{10,... | collective-permute-start | bytes 12296 | tf_op jit(solution)/shard_map/ppermute | solution.py:52
  268.4 4.0 %collective-permute-start.44 = (f32[8,128]{1,0:T(8,128)S(1)}, f32[8,128]{1,0:T(8,128)S(1)}, u32[]{:S(2)}, u32[]{:S(2)}) collective-permute-start(f32[8,128]{1,0:T(8,128)S(1)} %add.543), channel_id=1, source_target_pairs={{0,4},{1,5},{2,6},{3,7},{4,0},{5,1},{6,2},{7,3},{8,12},{9,13},{10,... | collective-permute-start | bytes 12296 | tf_op jit(solution)/shard_map/ppermute | solution.py:52
  269.8 4.5 %collective-permute-start.45 = (f32[8,128]{1,0:T(8,128)S(1)}, f32[8,128]{1,0:T(8,128)S(1)}, u32[]{:S(2)}, u32[]{:S(2)}) collective-permute-start(f32[8,128]{1,0:T(8,128)S(1)} %add.543), channel_id=1, source_target_pairs={{0,6},{1,7},{2,4},{3,5},{4,2},{5,3},{6,0},{7,1},{8,14},{9,15},{10,... | collective-permute-start | bytes 12296 | tf_op jit(solution)/shard_map/ppermute | solution.py:176
  271.8 10.3 %collective-permute-start.49 = (f32[96,384]{1,0:T(8,128)S(1)}, f32[96,384]{1,0:T(8,128)S(1)}, u32[]{:S(2)}, u32[]{:S(2)}) collective-permute-start(f32[96,384]{1,0:T(8,128)S(1)} %get-tuple-element.175), channel_id=1, source_target_pairs={{0,1},{1,0},{2,3},{3,2},{4,5},{5,4},{6,7},{7,6},{8,9},{9,8},{10,11... | collective-permute-start | bytes 442376 | tf_op jit(solution)/shard_map/ppermute | solution.py:56
  271.8 10.3 %collective-permute-start.50 = (f32[24,1536]{1,0:T(8,128)S(1)}, f32[24,1536]{1,0:T(8,128)S(1)}, u32[]{:S(2)}, u32[]{:S(2)}) collective-permute-start(f32[24,1536]{1,0:T(8,128)S(1)} %get-tuple-element.177), channel_id=1, source_target_pairs={{0,1},{1,0},{2,3},{3,2},{4,5},{5,4},{6,7},{7,6},{8,9},{9,8},{10,11... | collective-permute-start | bytes 442376 | tf_op jit(solution)/shard_map/ppermute | solution.py:56
  274.4 4.4 %collective-permute-start.46 = (f32[8,128]{1,0:T(8,128)S(1)}, f32[8,128]{1,0:T(8,128)S(1)}, u32[]{:S(2)}, u32[]{:S(2)}) collective-permute-start(f32[8,128]{1,0:T(8,128)S(1)} %select_add_fusion.1), channel_id=1, source_target_pairs={{0,8},{1,9},{2,10},{3,11},{4,12},{5,13},{6,14},{7,15},{8,0},{9,1},... | collective-permute-start | bytes 12296 | tf_op jit(solution)/shard_map/ppermute | solution.py:52
  274.5 4.5 %collective-permute-start.47 = (f32[8,128]{1,0:T(8,128)S(1)}, f32[8,128]{1,0:T(8,128)S(1)}, u32[]{:S(2)}, u32[]{:S(2)}) collective-permute-start(f32[8,128]{1,0:T(8,128)S(1)} %select_add_fusion.1), channel_id=1, source_target_pairs={{0,16},{1,17},{2,18},{3,19},{4,20},{5,21},{6,22},{7,23},{8,24},{9,... | collective-permute-start | bytes 12296 | tf_op jit(solution)/shard_map/ppermute | solution.py:52
  276.7 5.4 %collective-permute-start.48 = (f32[8,128]{1,0:T(8,128)S(1)}, f32[8,128]{1,0:T(8,128)S(1)}, u32[]{:S(2)}, u32[]{:S(2)}) collective-permute-start(f32[8,128]{1,0:T(8,128)S(1)} %select_add_fusion.1), channel_id=1, source_target_pairs={{0,24},{1,25},{2,26},{3,27},{4,28},{5,29},{6,30},{7,31},{8,16},{9,... | collective-permute-start | bytes 12296 | tf_op jit(solution)/shard_map/ppermute | solution.py:176
  278.7 3.3 %collective-permute-start.51 = (f32[24,1152]{1,0:T(8,128)S(1)}, f32[24,1152]{1,0:T(8,128)S(1)}, u32[]{:S(2)}, u32[]{:S(2)}) collective-permute-start(f32[24,1152]{1,0:T(8,128)S(1)} %get-tuple-element.179), channel_id=1, source_target_pairs={{0,1},{1,0},{2,3},{3,2},{4,5},{5,4},{6,7},{7,6},{8,9},{9,8},{10,11... | collective-permute-start | bytes 331784 | tf_op jit(solution)/shard_map/ppermute | solution.py:56
  (18 other events, 153.0 us)

commit v4 on v3

--- a/solution.py
+++ b/solution.py
@@ -438,7 +438,7 @@
         in_turn(each * pairs, scored, weighed)
         total = dot(context_ref[...], proj_ref[...]) + affine_ref[6:7, :]
         normed, inv = normalize(tokens_ref[...].astype(F32) + total)
-        normed_ref[...] = normed
+        normed_ref[...] = normed.astype(BF16)
         inv_ref[...] = jnp.broadcast_to(inv, (PART, LANES))
         skip_ref[...] = (normed * affine_ref[0:1, :] + affine_ref[1:2, :]).astype(BF16)
 
@@ -457,7 +457,7 @@
                 pl.BlockSpec((each, pairs, 2 * L, L), lambda i, *_: (i, 0, 0, 0)),
             ),
             (far((rows, width), BF16), rows_of(PART, width)),
-            (far((rows, width), F32), rows_of(PART, width)),
+            (far((rows, width), BF16), rows_of(PART, width)),
             (far((rows, LANES), F32), rows_of(PART, LANES)),
             (struct((rows, width), BF16), rows_of(PART, width)),
         ],
@@ -522,17 +522,17 @@
     )
 
 
-def outer_forward(order, act_own, act_other, own, other, normed_one, affine, mlm_grad, live_rows, after=()):
+def outer_forward(order, act_own, act_other, own, other, skip_low, affine, mlm_grad, live_rows, after=()):
     rows, wide = act_own.shape
-    hidden, width = 2 * wide, normed_one.shape[1]
+    hidden, width = 2 * wide, skip_low.shape[1]
     chips, block = 2 * own[0].shape[0], own[0].shape[1]
     spans = rows // L
     many = 2
     tile = many * PART
 
     def kernel(
-        order_ref, act_own_ref, act_other_ref, own_a, own_b, other_a, other_b, normed_one_ref, affine_ref, mlm_ref, live_ref,
-        w_ref, out_ref, grad_ref, low_ref, sums_ref, cls_ref, cls_normed_ref, cls_inv_ref, sems,
+        order_ref, act_own_ref, act_other_ref, own_a, own_b, other_a, other_b, skip_ref, affine_ref, mlm_ref, live_ref,
+        w_ref, out_ref, low_ref, sums_ref, cls_ref, cls_normed_ref, cls_inv_ref, sems,
     ):
         step = pl.program_id(0)
 
@@ -548,15 +548,13 @@
 
         def ended(n, total):
             at = slice(n * PART, (n + 1) * PART)
-            skip = normed_one_ref[at, :] * affine_ref[0:1, :] + affine_ref[1:2, :]
-            normed, inv = normalize(skip + (total + affine_ref[7:8, :]))
+            normed, inv = normalize(skip_ref[at, :].astype(F32) + (total + affine_ref[7:8, :]))
             out = (normed * affine_ref[2:3, :] + affine_ref[3:4, :]).astype(BF16)
             out_ref[at, :] = out
             line = lax.broadcasted_iota(jnp.int32, (PART, 1), 0)
             live = line < live_ref[0] - (step * many + n) * PART
             upstream = jnp.where(live, mlm_ref[at, :].astype(F32), 0.0)
             grad = normalize_back(upstream, normed, inv, affine_ref[2:3, :])
-            grad_ref[at, :] = grad
             low_ref[at, :] = grad.astype(BF16)
             for k, value in enumerate((upstream * normed, upstream, grad)):
                 sums_ref[k : k + 1, :] += column_sum(value)
@@ -583,7 +581,7 @@
             (act_own, rows_of(tile, wide)),
             (act_other, rows_of(tile, wide)),
             *((blocks, ANY) for blocks in (*own, *other)),
-            (streamed(normed_one), rows_of(tile, width)),
+            (skip_low, rows_of(tile, width)),
             (affine, whole(affine.shape)),
             (streamed(mlm_grad), rows_of(tile, width)),
             (live_rows, SMEM),
@@ -591,7 +589,6 @@
         [
             (far((hidden, width), BF16), whole((hidden, width))),
             (far((rows, width), BF16), rows_of(tile, width)),
-            (far((rows, width), F32), rows_of(tile, width)),
             (struct((rows, width), BF16), rows_of(tile, width)),
             (struct((8, width), F32), whole((8, width))),
             (struct((spans, width), F32), whole((spans, width))),
@@ -638,7 +635,7 @@
 
     def kernel(
         order_ref, low_in_ref, sums_in_ref, cls_ref, cls_other_ref, masks_ref, normed_ref, inv_ref, act_own_ref, act_other_ref, affine_ref,
-        low_ref, more_ref, sums_ref, loss_ref, own_ref, other_ref, own_held, other_held, sems,
+        low_ref, sums_ref, loss_ref, own_ref, other_ref, own_held, other_held, sems,
     ):
         step = pl.program_id(0)
 
@@ -649,7 +646,6 @@
             )
             normed = normed_ref[...]
             more = normalize_back(up, normed, inv_ref[:, :1], affine_ref[2:3, :])
-            more_ref[...] = more
             loss_ref[...] = jnp.broadcast_to(loss, loss_ref.shape)
             for k, value in enumerate((up * normed, up, more)):
                 sums_ref[k : k + 1, :] = sums_in_ref[k : k + 1, :] + column_sum(value)
@@ -715,11 +711,10 @@
         ],
         [
             (struct((rows, width), BF16), whole((rows, width))),
-            (struct((spans, width), F32), whole((spans, width))),
             (struct((8, width), F32), whole((8, width))),
             (struct((8, LANES), F32), whole((8, LANES))),
-            (struct(shape, BF16), ANY),
-            (struct(shape, BF16), ANY),
+            (far(shape, BF16), ANY),
+            (far(shape, BF16), ANY),
         ],
         [
             pltpu.VMEM(shape, BF16),
@@ -787,15 +782,15 @@
     )
 
 
-def skip_backward(inner_own, inner_other, w_own, w_other, grad_two, more, normed_one, inv_one, affine, proj_w, after=()):
-    rows, width = grad_two.shape
+def skip_backward(inner_own, inner_other, w_own, w_other, grad_two_low, normed_one, inv_one, affine, proj_w, after=()):
+    rows, width = grad_two_low.shape
     half = w_own.shape[1]
     many = 2
     tile = many * PART
 
     def kernel(
-        own_ref, other_ref, w_own_ref, w_other_ref, grad_two_ref, more_ref, normed_ref, inv_ref, affine_ref, proj_ref,
-        grad_ref, low_ref, sums_ref, context_ref,
+        own_ref, other_ref, w_own_ref, w_other_ref, grad_two_ref, normed_ref, inv_ref, affine_ref, proj_ref,
+        low_ref, sums_ref, context_ref,
     ):
         step = pl.program_id(0)
 
@@ -805,20 +800,15 @@
 
         def entered(n):
             at = slice(n * PART, (n + 1) * PART)
-            up = grad_two_ref[at, :]
+            up = grad_two_ref[at, :].astype(F32)
             for ref, weight in ((own_ref, w_own_ref), (other_ref, w_other_ref)):
                 up = up + contract_cols(ref[at, :], weight[...])
             return up
 
         def ended(n, up):
             at = slice(n * PART, (n + 1) * PART)
-            line = lax.broadcasted_iota(jnp.int32, (PART, 1), 0)
-            for s in range(PART // L):
-                row = pl.ds((step * many + n) * (PART // L) + s, 1)
-                up = up + jnp.where(line == s * L, more_ref[row, :], 0.0)
-            normed = normed_ref[at, :]
+            normed = normed_ref[at, :].astype(F32)
             grad = normalize_back(up, normed, inv_ref[at, :1], affine_ref[0:1, :])
-            grad_ref[at, :] = grad
             low = grad.astype(BF16)
             low_ref[at, :] = low
             for k, value in enumerate((up * normed, up, grad)):
@@ -835,15 +825,13 @@
             (inner_other, rows_of(tile, half)),
             (streamed(w_own), whole(w_own.shape)),
             (streamed(w_other), whole(w_other.shape)),
-            (streamed(grad_two), rows_of(tile, width)),
-            (more, whole(more.shape)),
+            (grad_two_low, rows_of(tile, width)),
             (streamed(normed_one), rows_of(tile, width)),
             (streamed(inv_one), rows_of(tile, LANES)),
             (affine, whole(affine.shape)),
             (proj_w, whole(proj_w.shape)),
         ],
         [
-            (far((rows, width), F32), rows_of(tile, width)),
             (struct((rows, width), BF16), rows_of(tile, width)),
             (struct((8, width), F32), whole((8, width))),
             (struct((rows, width), BF16), rows_of(tile, width)),
@@ -993,13 +981,13 @@
                     held[:, part * width + p * PAIR_LANES : part * width + (p + 1) * PAIR_LANES] = ref[
                         :, (part * len(pairs) + n) * PAIR_LANES : (part * len(pairs) + n + 1) * PAIR_LANES
                     ]
-        out_ref[...] = contract_cols(held[...], w_ref[...]) + grad_ref[...]
+        out_ref[...] = contract_cols(held[...], w_ref[...]) + grad_ref[...].astype(F32)
 
     return call(
         kernel,
         (rows // PART,),
         [(low, rows_of(PART, low.shape[1])) for low in qkv_lows]
-        + [(streamed(qkv_w), whole(qkv_w.shape)), (streamed(grad_one), rows_of(PART, width))],
+        + [(streamed(qkv_w), whole(qkv_w.shape)), (grad_one, rows_of(PART, width))],
         [(struct((rows, width), F32), rows_of(PART, width))],
         [pltpu.VMEM((PART, 3 * width), BF16)],
         8,
@@ -1186,10 +1174,10 @@
     w_own, act_own, slope_own = inner_forward(table, 0, skip_low, own, affine)
     w_other, act_other, slope_other = inner_forward(table, 1, skip_low, other, affine)
     own, other = three.finish(order_outer, rows_outer, act_own)
-    outer_w, layer_out, grad_two, low, sums_two, cls, cls_normed, cls_inv = outer_forward(
-        table_outer, act_own, act_other, own, other, normed_one, affine, mlm_grad, live_rows
-    )
-    low, more, sums_two, loss, own, other = outer_backward(
+    outer_w, layer_out, low, sums_two, cls, cls_normed, cls_inv = outer_forward(
+        table_outer, act_own, act_other, own, other, skip_low, affine, mlm_grad, live_rows
+    )
+    low, sums_two, loss, own, other = outer_backward(
         table, low, sums_two, cls, core_swapped(cls), masks, cls_normed, cls_inv, act_own, act_other, affine
     )
 
@@ -1199,8 +1187,8 @@
     got = red_outer.step()
     inner_own, bias_own, blocks_own = inner_backward(table, 0, low, slope_own, outer_w, skip_low, (core_done,))
     red_inner = Reduce(*in_order(order, blocks_own, blocks_other, rows_chip))
-    grad_one, grad_one_low, sums_one, context_grad = skip_backward(
-        inner_own, inner_other, w_own, w_other, grad_two, more, normed_one, inv_one, affine, proj_w,
+    grad_one_low, sums_one, context_grad = skip_backward(
+        inner_own, inner_other, w_own, w_other, low, normed_one, inv_one, affine, proj_w,
         (red_inner.last(), got),
     )
     groups = (
@@ -1223,7 +1211,7 @@
     red_second = Reduce(*in_order(order, own, other, rows_chip))
     core_done = red_second.last()
     red_second.step()
-    input_grad = tokens_backward(groups, qkv_low, qkv_w, grad_one, (core_done,))
+    input_grad = tokens_backward(groups, qkv_low, qkv_w, grad_one_low, (core_done,))
     red_first.step(input_grad)
     red_second.step(input_grad)
     outer_mine, outer_theirs, inner_mine, inner_theirs, squares = summed(

time: 290 us -> 281 us (0.969)
  Pallas kernels: 130 us -> 120 us
    pallas_call x17, Pallas kernels: 130 us -> 120 us  [call(): pl.pallas_call(body, grid_spec=pltpu.PrefetchScalarGridSpec(num_scalar_pr...]
where the time goes in v4:
time: 281 us; the launch traced here: 277 us
  Pallas kernels  120 us (43%)
  waiting for transfers between devices  85 us (30%)
  starting transfers between devices  55.1 us (20%)
  other arithmetic  10.1 us (4%)
  between operations  4.1 us (1%)
  local copies, waits for them, and re-layouts  3.22 us (1%)
    pallas_call x17, Pallas kernels, call(): pl.pallas_call(body, grid_spec=pltpu.PrefetchScalarGridSpec(num_scalar_pr...  120 us
    ppermute x32, waiting for transfers between devices, flipped(): return lax.ppermute(block, AXES, flip_route(chips, bits))  75.9 us
    ppermute x32, starting transfers between devices, flipped(): return lax.ppermute(block, AXES, flip_route(chips, bits))  44.3 us
    ppermute x19, starting transfers between devices, core_swapped(): return lax.ppermute(block, AXES, core_route(lax.axis_size('dp')))  6.71 us
  transfers between devices with their start and end apart: 53, of which 26 were waited for; matrix products, arithmetic and copies ran while one was open for 3% of the time, Pallas kernels for 33%

profile of v4, /device:TPU:0, one launch (start us, length us, event | category | flops | bytes accessed | tf_op | source)
XLA Modules:
  0.0 277.4 jit_solution(5352704695411563472)
XLA Ops:
  4.9 3.0 %collective-permute-start.1 = (bf16[1,48,1664]{2,1,0:T(8,128)(2,1)S(1)}, bf16[1,48,1664]{2,1,0:T(8,128)(2,1)S(1)}, u32[]{:S(2)}, u32[]{:S(2)}) collective-permute-start(bf16[1,48,1664]{2,1,0:T(8,128)(2,1)S(1)} %maximum_select_fusion), channel_id=1, source_target_pairs={{0,8},{1,17},{2,10},{3,19},{4,12},{5,21},{6,14},{7,23},{8,0},{9,25... | collective-permute-start | bytes 479240 | tf_op jit(solution)/shard_map/ppermute | solution.py:52
  8.9 3.6 %collective-permute-done.1 = bf16[1,48,1664]{2,1,0:T(8,128)(2,1)S(1)} collective-permute-done((bf16[1,48,1664]{2,1,0:T(8,128)(2,1)S(1)}, bf16[1,48,1664]{2,1,0:T(8,128)(2,1)S(1)}, u32[]{:S(2)}, u32[]{:S(2)}) %collective-permute-start.1) | collective-permute-done | bytes 159776 | tf_op jit(solution)/shard_map/ppermute | solution.py:52
  12.5 2.6 collective-permute-start.2
  16.7 3.7 %collective-permute-done.4 = bf16[1,192,384]{2,1,0:T(8,128)(2,1)S(1)} collective-permute-done((bf16[1,192,384]{2,1,0:T(8,128)(2,1)S(1)}, bf16[1,192,384]{2,1,0:T(8,128)(2,1)S(1)}, u32[]{:S(2)}, u32[]{:S(2)}) %collective-permute-start.4) | collective-permute-done | bytes 147488 | tf_op jit(solution)/shard_map/ppermute | solution.py:52
  22.4 5.0 %collective-permute-done.5 = bf16[2,192,384]{2,1,0:T(8,128)(2,1)S(1)} collective-permute-done((bf16[2,192,384]{2,1,0:T(8,128)(2,1)S(1)}, bf16[2,192,384]{2,1,0:T(8,128)(2,1)S(1)}, u32[]{:S(2)}, u32[]{:S(2)}) %collective-permute-start.5) | collective-permute-done | bytes 294944 | tf_op jit(solution)/shard_map/ppermute | solution.py:52
  30.3 4.4 %collective-permute-start.8 = (bf16[1,48,1536]{2,1,0:T(8,128)(2,1)S(1)}, bf16[1,48,1536]{2,1,0:T(8,128)(2,1)S(1)}, u32[]{:S(2)}, u32[]{:S(2)}) collective-permute-start(bf16[1,48,1536]{2,1,0:T(8,128)(2,1)S(1)} %maximum_select_fusion.2), channel_id=1, source_target_pairs={{0,8},{1,17},{2,10},{3,19},{4,12},{5,21},{6,14},{7,23},{8,0},{9,25... | collective-permute-start | bytes 442376 | tf_op jit(solution)/shard_map/ppermute | solution.py:52
  34.7 3.1 %collective-permute-done.6 = bf16[4,48,1664]{2,1,0:T(8,128)(2,1)S(1)} collective-permute-done((bf16[4,48,1664]{2,1,0:T(8,128)(2,1)S(1)}, bf16[4,48,1664]{2,1,0:T(8,128)(2,1)S(1)}, u32[]{:S(2)}, u32[]{:S(2)}) %collective-permute-start.6) | collective-permute-done | bytes 639008 | tf_op jit(solution)/shard_map/ppermute | solution.py:52
  40.6 6.8 %collective-permute-done.10 = bf16[2,48,1536]{2,1,0:T(8,128)(2,1)S(1)} collective-permute-done((bf16[2,48,1536]{2,1,0:T(8,128)(2,1)S(1)}, bf16[2,48,1536]{2,1,0:T(8,128)(2,1)S(1)}, u32[]{:S(2)}, u32[]{:S(2)}) %collective-permute-start.10) | collective-permute-done | bytes 294944 | tf_op jit(solution)/shard_map/ppermute | solution.py:52
  47.4 7.9 %collective-permute-done.9.refs_3_ = bf16[8,48,1664]{2,1,0:T(8,128)(2,1)S(1)} collective-permute-done((bf16[8,48,1664]{2,1,0:T(8,128)(2,1)S(1)}, bf16[8,48,1664]{2,1,0:T(8,128)(2,1)S(1)}, u32[]{:S(2)}, u32[]{:S(2)}) %collective-permute-start.9) | collective-permute-done | bytes 1277984 | tf_op jit(solution)/shard_map/ppermute | solution.py:52
  56.7 2.2 collective-permute-start.13
  59.1 3.9 %collective-permute-start.17 = (bf16[4,192,384]{2,1,0:T(8,128)(2,1)S(1)}, bf16[4,192,384]{2,1,0:T(8,128)(2,1)S(1)}, u32[]{:S(2)}, u32[]{:S(2)}) collective-permute-start(bf16[4,192,384]{2,1,0:T(8,128)(2,1)S(1)} %pad_maximum_fusion.5), channel_id=1, source_target_pairs={{0,8},{1,17},{2,10},{3,19},{4,12},{5,21},{6,14},{7,23},{8,0},{9,25... | collective-permute-start | bytes 1769480 | tf_op jit(solution)/shard_map/ppermute | solution.py:52
  63.0 4.1 %collective-permute-done.13 = bf16[4,48,1536]{2,1,0:T(8,128)(2,1)} collective-permute-done((bf16[4,48,1536]{2,1,0:T(8,128)(2,1)}, bf16[4,48,1536]{2,1,0:T(8,128)(2,1)}, u32[]{:S(2)}, u32[]{:S(2)}) %collective-permute-start.13) | collective-permute-done | bytes 589856 | tf_op jit(solution)/shard_map/ppermute | solution.py:52
  67.1 2.3 pad_maximum_fusion.1.refs_2_
  69.4 9.8 %shard_map.330 = (bf16[768,2304]{1,0:T(8,128)(2,1)}, bf16[768,768]{1,0:T(8,128)(2,1)S(1)}, f32[12,768]{1,0:T(8,128)S(1)}, bf16[1024,2304]{1,0:T(8,128)(2,1)S(1)}) custom-call(s32[5,16]{1,0:T(8,128)S(1)} %stack.6.refs_0_, bf16[1024,768]{1,0:T(8,128)(2,1)S(1)} %copy-done.4, bf16[8,48,1664]{2,1,0:T(8,128)(2,1)S(1)} %pad_maximum_fusion.refs_2_, ...), custom_call_target="tpu_custom_call" | custom-call | flops 2400000000 | bytes 2400000 | tf_op jit(solution)/shard_map/pallas_call | solution.py:204
  81.8 8.3 %shard_map.331 = (bf16[8,6,256,128]{3,2,1,0:T(8,128)(2,1)}, bf16[1024,768]{1,0:T(8,128)(2,1)}, bf16[1024,768]{1,0:T(8,128)(2,1)}, f32[1024,128]{1,0:T(8,128)}, bf16[1024,768]{1,0:T(8,128)(2,1)S(1)}) custom-call(bf16[1024,768]{1,0:T(8,128)(2,1)S(1)} %copy-done.4, bf16[1024,2304]{1,0:T(8,128)(2,1)S(1)} %get-tuple-element.113.refs_1_, ...), custom_call_target="tpu_custom_call" | custom-call | flops 3600000000 | bytes 3600000 | tf_op jit(solution)/shard_map/pallas_call | solution.py:204
  90.2 2.5 collective-permute-start.15
  92.7 3.2 %collective-permute-done.14.refs_3_ = bf16[8,48,1536]{2,1,0:T(8,128)(2,1)} collective-permute-done((bf16[8,48,1536]{2,1,0:T(8,128)(2,1)}, bf16[8,48,1536]{2,1,0:T(8,128)(2,1)}, u32[]{:S(2)}, u32[]{:S(2)}) %collective-permute-start.14) | collective-permute-done | bytes 1179680 | tf_op jit(solution)/shard_map/ppermute | solution.py:52
  95.8 8.2 %shard_map.332 = (bf16[768,1536]{1,0:T(8,128)(2,1)}, bf16[1024,1536]{1,0:T(8,128)(2,1)S(1)}, bf16[1024,1536]{1,0:T(8,128)(2,1)}) custom-call(s32[5,16]{1,0:T(8,128)S(1)} %stack.6.refs_0_, bf16[1024,768]{1,0:T(8,128)(2,1)S(1)} %get-tuple-element.116.refs_1_.refs_7_.refs_4_, bf16[8,48,1536]{2,1,0:T(8,128)(2,1)} %pad_maximum_fusion.1.refs_2_, ...), custom_call_target="tpu_custom_call" | custom-call | flops 3000000000 | bytes 3000000 | tf_op jit(solution)/shard_map/pallas_call | solution.py:204
  105.8 5.2 %collective-permute-done.18.refs_4_ = bf16[8,192,384]{2,1,0:T(8,128)(2,1)} collective-permute-done((bf16[8,192,384]{2,1,0:T(8,128)(2,1)S(1)}, bf16[8,192,384]{2,1,0:T(8,128)(2,1)}, u32[]{:S(2)}, u32[]{:S(2)}) %collective-permute-start.18) | collective-permute-done | bytes 1179680 | tf_op jit(solution)/shard_map/ppermute | solution.py:52
  114.8 8.4 %shard_map.333 = (bf16[768,1536]{1,0:T(8,128)(2,1)}, bf16[1024,1536]{1,0:T(8,128)(2,1)S(1)}, bf16[1024,1536]{1,0:T(8,128)(2,1)}) custom-call(s32[5,16]{1,0:T(8,128)S(1)} %stack.6.refs_0_, bf16[1024,768]{1,0:T(8,128)(2,1)S(1)} %get-tuple-element.116.refs_1_.refs_7_.refs_4_, bf16[8,48,1536]{2,1,0:T(8,128)(2,1)} %collective-permute-done.15.refs_2_, ...), custom_call_target="tpu_custom_call" | custom-call | flops 3000000000 | bytes 3000000 | tf_op jit(solution)/shard_map/pallas_call | solution.py:204
  123.3 13.7 %shard_map.334 = (bf16[3072,768]{1,0:T(8,128)(2,1)}, bf16[1024,768]{1,0:T(8,128)(2,1)}, bf16[1024,768]{1,0:T(8,128)(2,1)S(1)}, f32[8,768]{1,0:T(8,128)S(1)}, f32...) custom-call(s32[5,16]{1,0:T(8,128)S(1)} %stack.7.refs_0_, bf16[1024,1536]{1,0:T(8,128)(2,1)S(1)} %copy-done.3, ...), custom_call_target="tpu_custom_call" | custom-call | flops 2400000000 | bytes 2400000 | tf_op jit(solution)/shard_map/pallas_call | solution.py:204
  138.3 8.8 %shard_map.335 = (bf16[1024,768]{1,0:T(8,128)(2,1)S(1)}, f32[8,768]{1,0:T(8,128)S(1)}, f32[8,128]{1,0:T(8,128)S(1)}, bf16[16,192,384]{2,1,0:T(8,128)(2,1)}, bf16[16,192,384]{2,1,0:T(8,128)(2,1)}) custom-call(s32[5,16]{1,0:T(8,128)S(1)} %stack.6.refs_0_, bf16[1024,768]{1,0:T(8,128)(2,1)S(1)} %get-tuple-element.126.refs_1_, ...), custom_call_target="tpu_custom_call" | custom-call | flops 2400000000 | bytes 2400000 | tf_op jit(solution)/shard_map/pallas_call | solution.py:204
  147.3 8.4 %shard_map.337 = (bf16[1024,1536]{1,0:T(8,128)(2,1)S(1)}, f32[8,768]{1,0:T(8,128)S(1)}, bf16[16,48,1536]{2,1,0:T(8,128)(2,1)S(1)}) custom-call(s32[5,16]{1,0:T(8,128)S(1)} %stack.6.refs_0_, bf16[1024,768]{1,0:T(8,128)(2,1)S(1)} %get-tuple-element.131.refs_1_.refs_4_, bf16[1024,1536]{1,0:T(8,128)(2,1)} %get-tuple-element.136.refs_2_, ...), custom_call_target="tpu_custom_call" | custom-call | flops 2400000000 | bytes 2400000 | tf_op jit(solution)/shard_map/pallas_call | solution.py:204
  156.9 8.7 %shard_map.336 = (bf16[1024,1536]{1,0:T(8,128)(2,1)S(1)}, f32[8,768]{1,0:T(8,128)S(1)}, bf16[16,48,1536]{2,1,0:T(8,128)(2,1)S(1)}) custom-call(s32[5,16]{1,0:T(8,128)S(1)} %stack.6.refs_0_, bf16[1024,768]{1,0:T(8,128)(2,1)S(1)} %get-tuple-element.131.refs_1_.refs_4_, bf16[1024,1536]{1,0:T(8,128)(2,1)} %get-tuple-element.132.refs_2_, ...), custom_call_target="tpu_custom_call" | custom-call | flops 2400000000 | bytes 2400000 | tf_op jit(solution)/shard_map/pallas_call | solution.py:204
  168.5 4.2 %collective-permute-done.24.refs_10_.refs_3_ = bf16[8,192,384]{2,1,0:T(8,128)(2,1)S(1)} collective-permute-done((bf16[8,192,384]{2,1,0:T(8,128)(2,1)S(1)}, bf16[8,192,384]{2,1,0:T(8,128)(2,1)S(1)}, u32[]{:S(2)}, u32[]{:S(2)}) %collective-permute-start.24) | collective-permute-done | bytes 1179680 | tf_op jit(solution)/shard_map/ppermute | solution.py:52
  172.9 2.1 collective-permute-start.25
  175.0 10.1 %shard_map.338 = (bf16[1024,768]{1,0:T(8,128)(2,1)S(1)}, f32[8,768]{1,0:T(8,128)S(1)}, bf16[1024,768]{1,0:T(8,128)(2,1)S(1)}) custom-call(bf16[1024,1536]{1,0:T(8,128)(2,1)S(1)} %get-tuple-element.135.refs_0_, bf16[1024,1536]{1,0:T(8,128)(2,1)S(1)} %get-tuple-element.137.refs_1_, bf16[768,1536]{1,0:T(8,128)(2,1)} %get-tuple-element.138.refs_2_, ...), custom_call_target="tpu_custom_call" | custom-call | flops 2400000000 | bytes 2400000 | tf_op jit(solution)/shard_map/pallas_call | solution.py:204
  185.1 8.5 %shard_map.339 = (bf16[1024,1536]{1,0:T(8,128)(2,1)S(1)}, f32[1,1536]{1,0:T(1,128)S(1)}) custom-call(bf16[1024,768]{1,0:T(8,128)(2,1)S(1)} %get-tuple-element.144.refs_0_, bf16[1024,2304]{1,0:T(8,128)(2,1)} %copy-done.1, bf16[8,6,256,128]{3,2,1,0:T(8,128)(2,1)} %get-tuple-element.145.refs_2_), custom_call_target="tpu_custom_call" | custom-call | flops 3600000000 | bytes 3600000 | tf_op jit(solution)/shard_map/pallas_call | solution.py:204
  193.6 4.5 %shard_map.340 = (bf16[16,48,1152]{2,1,0:T(8,128)(2,1)S(1)}, bf16[16,48,1152]{2,1,0:T(8,128)(2,1)S(1)}) custom-call(s32[5,16]{1,0:T(8,128)S(1)} %stack.6.refs_0_, bf16[1024,768]{1,0:T(8,128)(2,1)S(1)} %copy-done.5, bf16[1024,1536]{1,0:T(8,128)(2,1)S(1)} %get-tuple-element.146.refs_2_.refs_0_, bf16[1024,768]{1,0:T(8,128)(2,1)S(1)} %copy-done.6, ...), custom_call_target="tpu_custom_call" | custom-call | flops 1500000000 | bytes 1500000 | tf_op jit(solution)/shard_map/pallas_call | solution.py:204
  198.6 6.0 %shard_map.341 = (bf16[1024,768]{1,0:T(8,128)(2,1)S(1)}, f32[1,768]{1,0:T(1,128)S(1)}) custom-call(bf16[1024,768]{1,0:T(8,128)(2,1)S(1)} %get-tuple-element.144.refs_0_, bf16[1024,2304]{1,0:T(8,128)(2,1)} %copy-done.1, bf16[8,6,256,128]{3,2,1,0:T(8,128)(2,1)} %get-tuple-element.145.refs_2_, bf16[8,48,1536]{2,1,0:T(8,128)(2,1)S(1)} %collective-permute-done.27.refs_3_.refs_9_), custom_call_target="tpu_custom_call" | custom-call | flops 1800000000 | bytes 1800000 | tf_op jit(solution)/shard_map/pallas_call | solution.py:204
  204.6 3.8 %collective-permute-done.28.refs_10_ = bf16[4,48,1536]{2,1,0:T(8,128)(2,1)S(1)} collective-permute-done((bf16[4,48,1536]{2,1,0:T(8,128)(2,1)S(1)}, bf16[4,48,1536]{2,1,0:T(8,128)(2,1)S(1)}, u32[]{:S(2)}, u32[]{:S(2)}) %collective-permute-start.28) | collective-permute-done | bytes 589856 | tf_op jit(solution)/shard_map/ppermute | solution.py:52
  208.8 3.0 %collective-permute-start.38 = (bf16[2,192,384]{2,1,0:T(8,128)(2,1)S(1)}, bf16[2,192,384]{2,1,0:T(8,128)(2,1)S(1)}, u32[]{:S(2)}, u32[]{:S(2)}) collective-permute-start(bf16[2,192,384]{2,1,0:T(8,128)(2,1)S(1)} %add_convert_fusion.8), channel_id=1, source_target_pairs={{0,16},{1,9},{2,18},{3,11},{4,20},{5,13},{6,22},{7,15},{8,24},{9,1... | collective-permute-start | bytes 884744 | tf_op jit(solution)/shard_map/ppermute | solution.py:52
  211.8 2.1 shard_map.342
  214.9 5.1 %collective-permute-done.40.refs_11_ = bf16[2,48,1536]{2,1,0:T(8,128)(2,1)S(1)} collective-permute-done((bf16[2,48,1536]{2,1,0:T(8,128)(2,1)S(1)}, bf16[2,48,1536]{2,1,0:T(8,128)(2,1)S(1)}, u32[]{:S(2)}, u32[]{:S(2)}) %collective-permute-start.40) | collective-permute-done | bytes 294944 | tf_op jit(solution)/shard_map/ppermute | solution.py:52
  220.9 7.8 %shard_map.343 = f32[1024,768]{1,0:T(8,128)} custom-call(bf16[1024,1536]{1,0:T(8,128)(2,1)S(1)} %get-tuple-element.146.refs_2_.refs_0_, bf16[1024,768]{1,0:T(8,128)(2,1)S(1)} %get-tuple-element.153.refs_2_.refs_1_, bf16[768,2304]{1,0:T(8,128)(2,1)} %get-tuple-element.154.refs_2_, bf16[1024,768]{1,0:T(8,128)(2,1)S(1)} %get-tuple-element.148.refs_4_.refs_3_, ...), custom_call_target="tpu_custom_call" | custom-call | flops 2400000000 | bytes 2400000 | tf_op jit(solution)/shard_map/pallas_call | solution.py:204
  229.1 2.1 collective-permute-start.39
  231.2 2.1 collective-permute-done.34.refs_9_
  233.4 3.8 %collective-permute-done.31.refs_4_ = bf16[4,48,1152]{2,1,0:T(8,128)(2,1)S(1)} collective-permute-done((bf16[4,48,1152]{2,1,0:T(8,128)(2,1)S(1)}, bf16[4,48,1152]{2,1,0:T(8,128)(2,1)S(1)}, u32[]{:S(2)}, u32[]{:S(2)}) %collective-permute-start.31) | collective-permute-done | bytes 442400 | tf_op jit(solution)/shard_map/ppermute | solution.py:52
  237.4 1.8 collective-permute-start.32
  239.4 1.8 collective-permute-start.36
  241.2 9.0 %collective-permute-done.32.refs_5_ = bf16[2,48,1152]{2,1,0:T(8,128)(2,1)S(1)} collective-permute-done((bf16[2,48,1152]{2,1,0:T(8,128)(2,1)S(1)}, bf16[2,48,1152]{2,1,0:T(8,128)(2,1)S(1)}, u32[]{:S(2)}, u32[]{:S(2)}) %collective-permute-start.32) | collective-permute-done | bytes 221216 | tf_op jit(solution)/shard_map/ppermute | solution.py:52
  253.7 2.7 collective-permute-done.37.refs_12_
  260.1 2.0 collective-permute-start.45
  262.7 1.9 collective-permute-done.45
  264.8 2.1 collective-permute-start.47
  266.9 2.1 collective-permute-start.48
  269.5 2.8 collective-permute-done.48
  272.3 4.4 %shard_map.346 = (f32[24,2304]{1,0:T(8,128)}, f32[24,2304]{1,0:T(8,128)}, f32[24,2304]{1,0:T(8,128)}, f32[24,768]{1,0:T(8,128)}, f32[24,768]{1,0:T(8,128)}, /*in...) custom-call(s32[5,16]{1,0:T(8,128)S(1)} %stack.6.refs_0_, ...), custom_call_target="tpu_custom_call" | custom-call | flops 1200000000 | bytes 1200000 | tf_op jit(solution)/shard_map/pallas_call | solution.py:204
  (162 shorter events, 39.7 us)
Async XLA Ops:
  4.9 7.5 %collective-permute-start.1 = (bf16[1,48,1664]{2,1,0:T(8,128)(2,1)S(1)}, bf16[1,48,1664]{2,1,0:T(8,128)(2,1)S(1)}, u32[]{:S(2)}, u32[]{:S(2)}) collective-permute-start(bf16[1,48,1664]{2,1,0:T(8,128)(2,1)S(1)} %maximum_select_fusion), channel_id=1, source_target_pairs={{0,8},{1,17},{2,10},{3,19},{4,12},{5,21},{6,14},{7,23},{8,0},{9,25... | collective-permute-start | bytes 479240 | tf_op jit(solution)/shard_map/ppermute | solution.py:52
  7.9 7.2 %collective-permute-start.3 = (bf16[96,384]{1,0:T(8,128)(2,1)S(1)}, bf16[96,384]{1,0:T(8,128)(2,1)S(1)}, u32[]{:S(2)}, u32[]{:S(2)}) collective-permute-start(bf16[96,384]{1,0:T(8,128)(2,1)S(1)} %get-tuple-element.196), channel_id=1, source_target_pairs={{0,1},{1,0},{2,3},{3,2},{4,5},{5,4},{6,7},{7,6},{8,9},{9,8},{10,11... | collective-permute-start | bytes 221192 | tf_op jit(solution)/shard_map/ppermute | solution.py:56
  12.5 9.8 %collective-permute-start.2 = (bf16[2,48,1664]{2,1,0:T(8,128)(2,1)S(1)}, bf16[2,48,1664]{2,1,0:T(8,128)(2,1)S(1)}, u32[]{:S(2)}, u32[]{:S(2)}) collective-permute-start(bf16[2,48,1664]{2,1,0:T(8,128)(2,1)S(1)} %pad_maximum_fusion.6), channel_id=1, source_target_pairs={{0,16},{1,9},{2,18},{3,11},{4,20},{5,13},{6,22},{7,15},{8,24},{9,1... | collective-permute-start | bytes 958472 | tf_op jit(solution)/shard_map/ppermute | solution.py:52
  15.1 5.2 %collective-permute-start.4 = (bf16[1,192,384]{2,1,0:T(8,128)(2,1)S(1)}, bf16[1,192,384]{2,1,0:T(8,128)(2,1)S(1)}, u32[]{:S(2)}, u32[]{:S(2)}) collective-permute-start(bf16[1,192,384]{2,1,0:T(8,128)(2,1)S(1)} %maximum_select_fusion.1), channel_id=1, source_target_pairs={{0,2},{1,5},{2,0},{3,7},{4,6},{5,1},{6,4},{7,3},{8,10},{9,13},{10,... | collective-permute-start | bytes 442376 | tf_op jit(solution)/shard_map/ppermute | solution.py:52
  20.4 7.0 %collective-permute-start.5 = (bf16[2,192,384]{2,1,0:T(8,128)(2,1)S(1)}, bf16[2,192,384]{2,1,0:T(8,128)(2,1)S(1)}, u32[]{:S(2)}, u32[]{:S(2)}) collective-permute-start(bf16[2,192,384]{2,1,0:T(8,128)(2,1)S(1)} %pad_maximum_fusion.7), channel_id=1, source_target_pairs={{0,4},{1,3},{2,6},{3,1},{4,0},{5,7},{6,2},{7,5},{8,12},{9,11},{10,... | collective-permute-start | bytes 884744 | tf_op jit(solution)/shard_map/ppermute | solution.py:52
  27.4 10.4 %collective-permute-start.6 = (bf16[4,48,1664]{2,1,0:T(8,128)(2,1)S(1)}, bf16[4,48,1664]{2,1,0:T(8,128)(2,1)S(1)}, u32[]{:S(2)}, u32[]{:S(2)}) collective-permute-start(bf16[4,48,1664]{2,1,0:T(8,128)(2,1)S(1)} %pad_maximum_fusion.3), channel_id=1, source_target_pairs={{0,2},{1,5},{2,0},{3,7},{4,6},{5,1},{6,4},{7,3},{8,10},{9,13},{10,... | collective-permute-start | bytes 1916936 | tf_op jit(solution)/shard_map/ppermute | solution.py:52
  30.3 7.7 %collective-permute-start.8 = (bf16[1,48,1536]{2,1,0:T(8,128)(2,1)S(1)}, bf16[1,48,1536]{2,1,0:T(8,128)(2,1)S(1)}, u32[]{:S(2)}, u32[]{:S(2)}) collective-permute-start(bf16[1,48,1536]{2,1,0:T(8,128)(2,1)S(1)} %maximum_select_fusion.2), channel_id=1, source_target_pairs={{0,8},{1,17},{2,10},{3,19},{4,12},{5,21},{6,14},{7,23},{8,0},{9,25... | collective-permute-start | bytes 442376 | tf_op jit(solution)/shard_map/ppermute | solution.py:52
  38.0 17.3 %collective-permute-start.9 = (bf16[8,48,1664]{2,1,0:T(8,128)(2,1)S(1)}, bf16[8,48,1664]{2,1,0:T(8,128)(2,1)S(1)}, u32[]{:S(2)}, u32[]{:S(2)}) collective-permute-start(bf16[8,48,1664]{2,1,0:T(8,128)(2,1)S(1)} %pad_maximum_fusion.refs_2_), channel_id=1, source_target_pairs={{0,4},{1,3},{2,6},{3,1},{4,0},{5,7},{6,2},{7,5},{8,12},{9,11},{10,... | collective-permute-start | bytes 3833864 | tf_op jit(solution)/shard_map/ppermute | solution.py:52
  39.6 7.8 %collective-permute-start.10 = (bf16[2,48,1536]{2,1,0:T(8,128)(2,1)S(1)}, bf16[2,48,1536]{2,1,0:T(8,128)(2,1)S(1)}, u32[]{:S(2)}, u32[]{:S(2)}) collective-permute-start(bf16[2,48,1536]{2,1,0:T(8,128)(2,1)S(1)} %pad_maximum_fusion.8), channel_id=1, source_target_pairs={{0,16},{1,9},{2,18},{3,11},{4,20},{5,13},{6,22},{7,15},{8,24},{9,1... | collective-permute-start | bytes 884744 | tf_op jit(solution)/shard_map/ppermute | solution.py:52
  55.3 14.0 %collective-permute-start.12 = (bf16[8,48,1664]{2,1,0:T(8,128)(2,1)S(1)}, bf16[8,48,1664]{2,1,0:T(8,128)(2,1)}, u32[]{:S(2)}, u32[]{:S(2)}) collective-permute-start(bf16[8,48,1664]{2,1,0:T(8,128)(2,1)S(1)} %collective-permute-done.9.refs_3_), channel_id=1, source_target_pairs={{0,1},{1,0},{2,3},{3,2},{4,5},{5,4},{6,7},{7,6},{8,9},{9,8},{10,11... | collective-permute-start | bytes 3833864 | tf_op jit(solution)/shard_map/ppermute | solution.py:56
  55.3 14.0 %collective-permute-start.11 = (bf16[8,48,1664]{2,1,0:T(8,128)(2,1)S(1)}, bf16[8,48,1664]{2,1,0:T(8,128)(2,1)}, u32[]{:S(2)}, u32[]{:S(2)}) collective-permute-start(bf16[8,48,1664]{2,1,0:T(8,128)(2,1)S(1)} %pad_maximum_fusion.refs_2_), channel_id=1, source_target_pairs={{0,1},{1,0},{2,3},{3,2},{4,5},{5,4},{6,7},{7,6},{8,9},{9,8},{10,11... | collective-permute-start | bytes 3833864 | tf_op jit(solution)/shard_map/ppermute | solution.py:56
  56.7 10.4 %collective-permute-start.13 = (bf16[4,48,1536]{2,1,0:T(8,128)(2,1)}, bf16[4,48,1536]{2,1,0:T(8,128)(2,1)}, u32[]{:S(2)}, u32[]{:S(2)}) collective-permute-start(bf16[4,48,1536]{2,1,0:T(8,128)(2,1)} %pad_maximum_fusion.4), channel_id=1, source_target_pairs={{0,2},{1,5},{2,0},{3,7},{4,6},{5,1},{6,4},{7,3},{8,10},{9,13},{10,... | collective-permute-start | bytes 1769480 | tf_op jit(solution)/shard_map/ppermute | solution.py:52
  59.1 21.8 %collective-permute-start.17 = (bf16[4,192,384]{2,1,0:T(8,128)(2,1)S(1)}, bf16[4,192,384]{2,1,0:T(8,128)(2,1)S(1)}, u32[]{:S(2)}, u32[]{:S(2)}) collective-permute-start(bf16[4,192,384]{2,1,0:T(8,128)(2,1)S(1)} %pad_maximum_fusion.5), channel_id=1, source_target_pairs={{0,8},{1,17},{2,10},{3,19},{4,12},{5,21},{6,14},{7,23},{8,0},{9,25... | collective-permute-start | bytes 1769480 | tf_op jit(solution)/shard_map/ppermute | solution.py:52
  79.2 16.6 %collective-permute-start.14 = (bf16[8,48,1536]{2,1,0:T(8,128)(2,1)}, bf16[8,48,1536]{2,1,0:T(8,128)(2,1)}, u32[]{:S(2)}, u32[]{:S(2)}) collective-permute-start(bf16[8,48,1536]{2,1,0:T(8,128)(2,1)} %pad_maximum_fusion.1.refs_2_), channel_id=1, source_target_pairs={{0,4},{1,3},{2,6},{3,1},{4,0},{5,7},{6,2},{7,5},{8,12},{9,11},{10,... | collective-permute-start | bytes 3538952 | tf_op jit(solution)/shard_map/ppermute | solution.py:52
  81.0 30.0 %collective-permute-start.18 = (bf16[8,192,384]{2,1,0:T(8,128)(2,1)S(1)}, bf16[8,192,384]{2,1,0:T(8,128)(2,1)}, u32[]{:S(2)}, u32[]{:S(2)}) collective-permute-start(bf16[8,192,384]{2,1,0:T(8,128)(2,1)S(1)} %pad_maximum_fusion.2.refs_3_), channel_id=1, source_target_pairs={{0,16},{1,9},{2,18},{3,11},{4,20},{5,13},{6,22},{7,15},{8,24},{9,1... | collective-permute-start | bytes 3538952 | tf_op jit(solution)/shard_map/ppermute | solution.py:52
  90.2 24.7 %collective-permute-start.15 = (bf16[8,48,1536]{2,1,0:T(8,128)(2,1)}, bf16[8,48,1536]{2,1,0:T(8,128)(2,1)}, u32[]{:S(2)}, u32[]{:S(2)}) collective-permute-start(bf16[8,48,1536]{2,1,0:T(8,128)(2,1)} %pad_maximum_fusion.1.refs_2_), channel_id=1, source_target_pairs={{0,1},{1,0},{2,3},{3,2},{4,5},{5,4},{6,7},{7,6},{8,9},{9,8},{10,11... | collective-permute-start | bytes 3538952 | tf_op jit(solution)/shard_map/ppermute | solution.py:56
  95.8 19.0 %collective-permute-start.16 = (bf16[8,48,1536]{2,1,0:T(8,128)(2,1)}, bf16[8,48,1536]{2,1,0:T(8,128)(2,1)}, u32[]{:S(2)}, u32[]{:S(2)}) collective-permute-start(bf16[8,48,1536]{2,1,0:T(8,128)(2,1)} %collective-permute-done.14.refs_3_), channel_id=1, source_target_pairs={{0,1},{1,0},{2,3},{3,2},{4,5},{5,4},{6,7},{7,6},{8,9},{9,8},{10,11... | collective-permute-start | bytes 3538952 | tf_op jit(solution)/shard_map/ppermute | solution.py:56
  111.0 12.3 %collective-permute-start.20 = (bf16[8,192,384]{2,1,0:T(8,128)(2,1)}, bf16[8,192,384]{2,1,0:T(8,128)(2,1)}, u32[]{:S(2)}, u32[]{:S(2)}) collective-permute-start(bf16[8,192,384]{2,1,0:T(8,128)(2,1)} %collective-permute-done.18.refs_4_), channel_id=1, source_target_pairs={{0,1},{1,0},{2,3},{3,2},{4,5},{5,4},{6,7},{7,6},{8,9},{9,8},{10,11... | collective-permute-start | bytes 3538952 | tf_op jit(solution)/shard_map/ppermute | solution.py:56
  111.0 12.3 %collective-permute-start.19 = (bf16[8,192,384]{2,1,0:T(8,128)(2,1)S(1)}, bf16[8,192,384]{2,1,0:T(8,128)(2,1)}, u32[]{:S(2)}, u32[]{:S(2)}) collective-permute-start(bf16[8,192,384]{2,1,0:T(8,128)(2,1)S(1)} %pad_maximum_fusion.2.refs_3_), channel_id=1, source_target_pairs={{0,1},{1,0},{2,3},{3,2},{4,5},{5,4},{6,7},{7,6},{8,9},{9,8},{10,11... | collective-permute-start | bytes 3538952 | tf_op jit(solution)/shard_map/ppermute | solution.py:56
  147.1 9.0 %collective-permute-start.22 = (bf16[16,192,384]{2,1,0:T(8,128)(2,1)}, bf16[16,192,384]{2,1,0:T(8,128)(2,1)S(1)}, u32[]{:S(2)}, u32[]{:S(2)}) collective-permute-start(bf16[16,192,384]{2,1,0:T(8,128)(2,1)} %get-tuple-element.134), channel_id=1, source_target_pairs={{0,1},{1,0},{2,3},{3,2},{4,5},{5,4},{6,7},{7,6},{8,9},{9,8},{10,11... | collective-permute-start | bytes 7077896 | tf_op jit(solution)/shard_map/ppermute | solution.py:56
  155.7 9.9 %collective-permute-start.23 = (bf16[16,48,1536]{2,1,0:T(8,128)(2,1)S(1)}, bf16[16,48,1536]{2,1,0:T(8,128)(2,1)S(1)}, u32[]{:S(2)}, u32[]{:S(2)}) collective-permute-start(bf16[16,48,1536]{2,1,0:T(8,128)(2,1)S(1)} %get-tuple-element.142), channel_id=1, source_target_pairs={{0,1},{1,0},{2,3},{3,2},{4,5},{5,4},{6,7},{7,6},{8,9},{9,8},{10,11... | collective-permute-start | bytes 7077896 | tf_op jit(solution)/shard_map/ppermute | solution.py:56
  156.4 16.3 %collective-permute-start.24 = (bf16[8,192,384]{2,1,0:T(8,128)(2,1)S(1)}, bf16[8,192,384]{2,1,0:T(8,128)(2,1)S(1)}, u32[]{:S(2)}, u32[]{:S(2)}) collective-permute-start(bf16[8,192,384]{2,1,0:T(8,128)(2,1)S(1)} %add_convert_fusion.1), channel_id=1, source_target_pairs={{0,4},{1,3},{2,6},{3,1},{4,0},{5,7},{6,2},{7,5},{8,12},{9,11},{10,... | collective-permute-start | bytes 3538952 | tf_op jit(solution)/shard_map/ppermute | solution.py:52
  167.0 31.3 %collective-permute-start.27 = (bf16[8,48,1536]{2,1,0:T(8,128)(2,1)}, bf16[8,48,1536]{2,1,0:T(8,128)(2,1)S(1)}, u32[]{:S(2)}, u32[]{:S(2)}) collective-permute-start(bf16[8,48,1536]{2,1,0:T(8,128)(2,1)} %add_convert_fusion), channel_id=1, source_target_pairs={{0,4},{1,3},{2,6},{3,1},{4,0},{5,7},{6,2},{7,5},{8,12},{9,11},{10,... | collective-permute-start | bytes 3538952 | tf_op jit(solution)/shard_map/ppermute | solution.py:52
  172.9 20.7 %collective-permute-start.25 = (bf16[4,192,384]{2,1,0:T(8,128)(2,1)S(1)}, bf16[4,192,384]{2,1,0:T(8,128)(2,1)S(1)}, u32[]{:S(2)}, u32[]{:S(2)}) collective-permute-start(bf16[4,192,384]{2,1,0:T(8,128)(2,1)S(1)} %add_convert_fusion.4), channel_id=1, source_target_pairs={{0,2},{1,5},{2,0},{3,7},{4,6},{5,1},{6,4},{7,3},{8,10},{9,13},{10,... | collective-permute-start | bytes 1769480 | tf_op jit(solution)/shard_map/ppermute | solution.py:52
  198.2 13.6 %collective-permute-start.26 = (bf16[16,48,1152]{2,1,0:T(8,128)(2,1)S(1)}, bf16[16,48,1152]{2,1,0:T(8,128)(2,1)S(1)}, u32[]{:S(2)}, u32[]{:S(2)}) collective-permute-start(bf16[16,48,1152]{2,1,0:T(8,128)(2,1)S(1)} %get-tuple-element.150), channel_id=1, source_target_pairs={{0,1},{1,0},{2,3},{3,2},{4,5},{5,4},{6,7},{7,6},{8,9},{9,8},{10,11... | collective-permute-start | bytes 5308424 | tf_op jit(solution)/shard_map/ppermute | solution.py:56
  198.5 9.9 %collective-permute-start.28 = (bf16[4,48,1536]{2,1,0:T(8,128)(2,1)S(1)}, bf16[4,48,1536]{2,1,0:T(8,128)(2,1)S(1)}, u32[]{:S(2)}, u32[]{:S(2)}) collective-permute-start(bf16[4,48,1536]{2,1,0:T(8,128)(2,1)S(1)} %add_convert_fusion.3), channel_id=1, source_target_pairs={{0,2},{1,5},{2,0},{3,7},{4,6},{5,1},{6,4},{7,3},{8,10},{9,13},{10,... | collective-permute-start | bytes 1769480 | tf_op jit(solution)/shard_map/ppermute | solution.py:52
  208.6 11.4 %collective-permute-start.40 = (bf16[2,48,1536]{2,1,0:T(8,128)(2,1)S(1)}, bf16[2,48,1536]{2,1,0:T(8,128)(2,1)S(1)}, u32[]{:S(2)}, u32[]{:S(2)}) collective-permute-start(bf16[2,48,1536]{2,1,0:T(8,128)(2,1)S(1)} %add_convert_fusion.7), channel_id=1, source_target_pairs={{0,16},{1,9},{2,18},{3,11},{4,20},{5,13},{6,22},{7,15},{8,24},{9,1... | collective-permute-start | bytes 884744 | tf_op jit(solution)/shard_map/ppermute | solution.py:52
  208.8 20.1 %collective-permute-start.38 = (bf16[2,192,384]{2,1,0:T(8,128)(2,1)S(1)}, bf16[2,192,384]{2,1,0:T(8,128)(2,1)S(1)}, u32[]{:S(2)}, u32[]{:S(2)}) collective-permute-start(bf16[2,192,384]{2,1,0:T(8,128)(2,1)S(1)} %add_convert_fusion.8), channel_id=1, source_target_pairs={{0,16},{1,9},{2,18},{3,11},{4,20},{5,13},{6,22},{7,15},{8,24},{9,1... | collective-permute-start | bytes 884744 | tf_op jit(solution)/shard_map/ppermute | solution.py:52
  214.0 6.2 %collective-permute-start.30 = (bf16[16,48,512]{2,1,0:T(8,128)(2,1)S(1)}, bf16[16,48,512]{2,1,0:T(8,128)(2,1)S(1)}, u32[]{:S(2)}, u32[]{:S(2)}) collective-permute-start(bf16[16,48,512]{2,1,0:T(8,128)(2,1)S(1)} %get-tuple-element.161), channel_id=1, source_target_pairs={{0,1},{1,0},{2,3},{3,2},{4,5},{5,4},{6,7},{7,6},{8,9},{9,8},{10,11... | collective-permute-start | bytes 2359304 | tf_op jit(solution)/shard_map/ppermute | solution.py:56
  214.3 14.5 %collective-permute-start.29 = (bf16[8,48,1152]{2,1,0:T(8,128)(2,1)S(1)}, bf16[8,48,1152]{2,1,0:T(8,128)(2,1)S(1)}, u32[]{:S(2)}, u32[]{:S(2)}) collective-permute-start(bf16[8,48,1152]{2,1,0:T(8,128)(2,1)S(1)} %add_convert_fusion.2), channel_id=1, source_target_pairs={{0,4},{1,3},{2,6},{3,1},{4,0},{5,7},{6,2},{7,5},{8,12},{9,11},{10,... | collective-permute-start | bytes 2654216 | tf_op jit(solution)/shard_map/ppermute | solution.py:52
  220.1 32.4 %collective-permute-start.41 = (bf16[1,48,1536]{2,1,0:T(8,128)(2,1)S(1)}, bf16[1,48,1536]{2,1,0:T(8,128)(2,1)S(1)}, u32[]{:S(2)}, u32[]{:S(2)}) collective-permute-start(bf16[1,48,1536]{2,1,0:T(8,128)(2,1)S(1)} %add_convert_fusion.11), channel_id=1, source_target_pairs={{0,8},{1,17},{2,10},{3,19},{4,12},{5,21},{6,14},{7,23},{8,0},{9,25... | collective-permute-start | bytes 442376 | tf_op jit(solution)/shard_map/ppermute | solution.py:52
  220.3 13.0 %collective-permute-start.34 = (bf16[8,48,512]{2,1,0:T(8,128)(2,1)S(1)}, bf16[8,48,512]{2,1,0:T(8,128)(2,1)S(1)}, u32[]{:S(2)}, u32[]{:S(2)}) collective-permute-start(bf16[8,48,512]{2,1,0:T(8,128)(2,1)S(1)} %add_convert_fusion.6), channel_id=1, source_target_pairs={{0,4},{1,3},{2,6},{3,1},{4,0},{5,7},{6,2},{7,5},{8,12},{9,11},{10,... | collective-permute-start | bytes 1179656 | tf_op jit(solution)/shard_map/ppermute | solution.py:52
  228.9 8.4 %collective-permute-start.31 = (bf16[4,48,1152]{2,1,0:T(8,128)(2,1)S(1)}, bf16[4,48,1152]{2,1,0:T(8,128)(2,1)S(1)}, u32[]{:S(2)}, u32[]{:S(2)}) collective-permute-start(bf16[4,48,1152]{2,1,0:T(8,128)(2,1)S(1)} %add_convert_fusion.5), channel_id=1, source_target_pairs={{0,2},{1,5},{2,0},{3,7},{4,6},{5,1},{6,4},{7,3},{8,10},{9,13},{10,... | collective-permute-start | bytes 1327112 | tf_op jit(solution)/shard_map/ppermute | solution.py:52
  229.1 23.5 %collective-permute-start.39 = (bf16[1,192,384]{2,1,0:T(8,128)(2,1)S(1)}, bf16[1,192,384]{2,1,0:T(8,128)(2,1)S(1)}, u32[]{:S(2)}, u32[]{:S(2)}) collective-permute-start(bf16[1,192,384]{2,1,0:T(8,128)(2,1)S(1)} %add_convert_fusion.12), channel_id=1, source_target_pairs={{0,8},{1,17},{2,10},{3,19},{4,12},{5,21},{6,14},{7,23},{8,0},{9,25... | collective-permute-start | bytes 442376 | tf_op jit(solution)/shard_map/ppermute | solution.py:52
  233.3 6.0 %collective-permute-start.35 = (bf16[4,48,512]{2,1,0:T(8,128)(2,1)S(1)}, bf16[4,48,512]{2,1,0:T(8,128)(2,1)S(1)}, u32[]{:S(2)}, u32[]{:S(2)}) collective-permute-start(bf16[4,48,512]{2,1,0:T(8,128)(2,1)S(1)} %add_convert_fusion.10), channel_id=1, source_target_pairs={{0,2},{1,5},{2,0},{3,7},{4,6},{5,1},{6,4},{7,3},{8,10},{9,13},{10,... | collective-permute-start | bytes 589832 | tf_op jit(solution)/shard_map/ppermute | solution.py:52
  237.4 12.9 %collective-permute-start.32 = (bf16[2,48,1152]{2,1,0:T(8,128)(2,1)S(1)}, bf16[2,48,1152]{2,1,0:T(8,128)(2,1)S(1)}, u32[]{:S(2)}, u32[]{:S(2)}) collective-permute-start(bf16[2,48,1152]{2,1,0:T(8,128)(2,1)S(1)} %add_convert_fusion.9), channel_id=1, source_target_pairs={{0,16},{1,9},{2,18},{3,11},{4,20},{5,13},{6,22},{7,15},{8,24},{9,1... | collective-permute-start | bytes 663560 | tf_op jit(solution)/shard_map/ppermute | solution.py:52
  239.4 12.8 %collective-permute-start.36 = (bf16[2,48,512]{2,1,0:T(8,128)(2,1)S(1)}, bf16[2,48,512]{2,1,0:T(8,128)(2,1)S(1)}, u32[]{:S(2)}, u32[]{:S(2)}) collective-permute-start(bf16[2,48,512]{2,1,0:T(8,128)(2,1)S(1)} %add_convert_fusion.14), channel_id=1, source_target_pairs={{0,16},{1,9},{2,18},{3,11},{4,20},{5,13},{6,22},{7,15},{8,24},{9,1... | collective-permute-start | bytes 294920 | tf_op jit(solution)/shard_map/ppermute | solution.py:52
  250.3 6.1 %collective-permute-start.33 = (bf16[1,48,1152]{2,1,0:T(8,128)(2,1)S(1)}, bf16[1,48,1152]{2,1,0:T(8,128)(2,1)S(1)}, u32[]{:S(2)}, u32[]{:S(2)}) collective-permute-start(bf16[1,48,1152]{2,1,0:T(8,128)(2,1)S(1)} %add_convert_fusion.13), channel_id=1, source_target_pairs={{0,8},{1,17},{2,10},{3,19},{4,12},{5,21},{6,14},{7,23},{8,0},{9,25... | collective-permute-start | bytes 331784 | tf_op jit(solution)/shard_map/ppermute | solution.py:52
  252.3 4.2 %collective-permute-start.37 = (bf16[1,48,512]{2,1,0:T(8,128)(2,1)S(1)}, bf16[1,48,512]{2,1,0:T(8,128)(2,1)S(1)}, u32[]{:S(2)}, u32[]{:S(2)}) collective-permute-start(bf16[1,48,512]{2,1,0:T(8,128)(2,1)S(1)} %add_convert_fusion.15), channel_id=1, source_target_pairs={{0,8},{1,17},{2,10},{3,19},{4,12},{5,21},{6,14},{7,23},{8,0},{9,25... | collective-permute-start | bytes 147464 | tf_op jit(solution)/shard_map/ppermute | solution.py:52
  258.6 4.1 %collective-permute-start.43 = (f32[8,128]{1,0:T(8,128)S(1)}, f32[8,128]{1,0:T(8,128)S(1)}, u32[]{:S(2)}, u32[]{:S(2)}) collective-permute-start(f32[8,128]{1,0:T(8,128)S(1)} %add.543), channel_id=1, source_target_pairs={{0,2},{1,3},{2,0},{3,1},{4,6},{5,7},{6,4},{7,5},{8,10},{9,11},{10,... | collective-permute-start | bytes 12296 | tf_op jit(solution)/shard_map/ppermute | solution.py:52
  258.6 4.1 %collective-permute-start.44 = (f32[8,128]{1,0:T(8,128)S(1)}, f32[8,128]{1,0:T(8,128)S(1)}, u32[]{:S(2)}, u32[]{:S(2)}) collective-permute-start(f32[8,128]{1,0:T(8,128)S(1)} %add.543), channel_id=1, source_target_pairs={{0,4},{1,5},{2,6},{3,7},{4,0},{5,1},{6,2},{7,3},{8,12},{9,13},{10,... | collective-permute-start | bytes 12296 | tf_op jit(solution)/shard_map/ppermute | solution.py:52
  260.1 4.5 %collective-permute-start.45 = (f32[8,128]{1,0:T(8,128)S(1)}, f32[8,128]{1,0:T(8,128)S(1)}, u32[]{:S(2)}, u32[]{:S(2)}) collective-permute-start(f32[8,128]{1,0:T(8,128)S(1)} %add.543), channel_id=1, source_target_pairs={{0,6},{1,7},{2,4},{3,5},{4,2},{5,3},{6,0},{7,1},{8,14},{9,15},{10,... | collective-permute-start | bytes 12296 | tf_op jit(solution)/shard_map/ppermute | solution.py:176
  262.1 10.2 %collective-permute-start.49 = (f32[96,384]{1,0:T(8,128)S(1)}, f32[96,384]{1,0:T(8,128)S(1)}, u32[]{:S(2)}, u32[]{:S(2)}) collective-permute-start(f32[96,384]{1,0:T(8,128)S(1)} %get-tuple-element.169), channel_id=1, source_target_pairs={{0,1},{1,0},{2,3},{3,2},{4,5},{5,4},{6,7},{7,6},{8,9},{9,8},{10,11... | collective-permute-start | bytes 442376 | tf_op jit(solution)/shard_map/ppermute | solution.py:56
  262.1 10.2 %collective-permute-start.50 = (f32[24,1536]{1,0:T(8,128)S(1)}, f32[24,1536]{1,0:T(8,128)S(1)}, u32[]{:S(2)}, u32[]{:S(2)}) collective-permute-start(f32[24,1536]{1,0:T(8,128)S(1)} %get-tuple-element.171), channel_id=1, source_target_pairs={{0,1},{1,0},{2,3},{3,2},{4,5},{5,4},{6,7},{7,6},{8,9},{9,8},{10,11... | collective-permute-start | bytes 442376 | tf_op jit(solution)/shard_map/ppermute | solution.py:56
  264.6 4.4 %collective-permute-start.46 = (f32[8,128]{1,0:T(8,128)S(1)}, f32[8,128]{1,0:T(8,128)S(1)}, u32[]{:S(2)}, u32[]{:S(2)}) collective-permute-start(f32[8,128]{1,0:T(8,128)S(1)} %select_add_fusion.1), channel_id=1, source_target_pairs={{0,8},{1,9},{2,10},{3,11},{4,12},{5,13},{6,14},{7,15},{8,0},{9,1},... | collective-permute-start | bytes 12296 | tf_op jit(solution)/shard_map/ppermute | solution.py:52
  264.8 4.5 %collective-permute-start.47 = (f32[8,128]{1,0:T(8,128)S(1)}, f32[8,128]{1,0:T(8,128)S(1)}, u32[]{:S(2)}, u32[]{:S(2)}) collective-permute-start(f32[8,128]{1,0:T(8,128)S(1)} %select_add_fusion.1), channel_id=1, source_target_pairs={{0,16},{1,17},{2,18},{3,19},{4,20},{5,21},{6,22},{7,23},{8,24},{9,... | collective-permute-start | bytes 12296 | tf_op jit(solution)/shard_map/ppermute | solution.py:52
  266.9 5.4 %collective-permute-start.48 = (f32[8,128]{1,0:T(8,128)S(1)}, f32[8,128]{1,0:T(8,128)S(1)}, u32[]{:S(2)}, u32[]{:S(2)}) collective-permute-start(f32[8,128]{1,0:T(8,128)S(1)} %select_add_fusion.1), channel_id=1, source_target_pairs={{0,24},{1,25},{2,26},{3,27},{4,28},{5,29},{6,30},{7,31},{8,16},{9,... | collective-permute-start | bytes 12296 | tf_op jit(solution)/shard_map/ppermute | solution.py:176
  269.0 3.3 %collective-permute-start.51 = (f32[24,1152]{1,0:T(8,128)S(1)}, f32[24,1152]{1,0:T(8,128)S(1)}, u32[]{:S(2)}, u32[]{:S(2)}) collective-permute-start(f32[24,1152]{1,0:T(8,128)S(1)} %get-tuple-element.173), channel_id=1, source_target_pairs={{0,1},{1,0},{2,3},{3,2},{4,5},{5,4},{6,7},{7,6},{8,9},{9,8},{10,11... | collective-permute-start | bytes 331784 | tf_op jit(solution)/shard_map/ppermute | solution.py:56
  (19 other events, 160.7 us)

commit v5 on v4

--- a/solution.py
+++ b/solution.py
@@ -1207,7 +1207,7 @@
         table, tokens, qkv_low[1], None, (sums_one, sums_two, qkv_sums[1], qkv_sums[0], bias_own, bias_other),
         (core_done,),
     )
-    red_first.step(got_inner)
+    red_first.step()
     red_second = Reduce(*in_order(order, own, other, rows_chip))
     core_done = red_second.last()
     red_second.step()

time: 281 us -> 281 us (level)
  no operation moved by 1% of the time
where the time goes in v5:
time: 281 us; the launch traced here: 277 us
  Pallas kernels  120 us (43%)
  waiting for transfers between devices  85 us (30%)
  starting transfers between devices  55.1 us (20%)
  other arithmetic  10.1 us (4%)
  between operations  4.1 us (1%)
  local copies, waits for them, and re-layouts  3.22 us (1%)
    pallas_call x17, Pallas kernels, call(): pl.pallas_call(body, grid_spec=pltpu.PrefetchScalarGridSpec(num_scalar_pr...  120 us
    ppermute x32, waiting for transfers between devices, flipped(): return lax.ppermute(block, AXES, flip_route(chips, bits))  75.9 us
    ppermute x32, starting transfers between devices, flipped(): return lax.ppermute(block, AXES, flip_route(chips, bits))  44.3 us
    ppermute x19, starting transfers between devices, core_swapped(): return lax.ppermute(block, AXES, core_route(lax.axis_size('dp')))  6.71 us
  transfers between devices with their start and end apart: 53, of which 26 were waited for; matrix products, arithmetic and copies ran while one was open for 3% of the time, Pallas kernels for 33%

profile of v5, /device:TPU:0, one launch (start us, length us, event | category | flops | bytes accessed | tf_op | source)
XLA Modules:
  0.0 277.4 jit_solution(5352704695411563472)
XLA Ops:
  4.9 3.0 %collective-permute-start.1 = (bf16[1,48,1664]{2,1,0:T(8,128)(2,1)S(1)}, bf16[1,48,1664]{2,1,0:T(8,128)(2,1)S(1)}, u32[]{:S(2)}, u32[]{:S(2)}) collective-permute-start(bf16[1,48,1664]{2,1,0:T(8,128)(2,1)S(1)} %maximum_select_fusion), channel_id=1, source_target_pairs={{0,8},{1,17},{2,10},{3,19},{4,12},{5,21},{6,14},{7,23},{8,0},{9,25... | collective-permute-start | bytes 479240 | tf_op jit(solution)/shard_map/ppermute | solution.py:52
  8.9 3.6 %collective-permute-done.1 = bf16[1,48,1664]{2,1,0:T(8,128)(2,1)S(1)} collective-permute-done((bf16[1,48,1664]{2,1,0:T(8,128)(2,1)S(1)}, bf16[1,48,1664]{2,1,0:T(8,128)(2,1)S(1)}, u32[]{:S(2)}, u32[]{:S(2)}) %collective-permute-start.1) | collective-permute-done | bytes 159776 | tf_op jit(solution)/shard_map/ppermute | solution.py:52
  12.5 2.6 collective-permute-start.2
  16.7 3.7 %collective-permute-done.4 = bf16[1,192,384]{2,1,0:T(8,128)(2,1)S(1)} collective-permute-done((bf16[1,192,384]{2,1,0:T(8,128)(2,1)S(1)}, bf16[1,192,384]{2,1,0:T(8,128)(2,1)S(1)}, u32[]{:S(2)}, u32[]{:S(2)}) %collective-permute-start.4) | collective-permute-done | bytes 147488 | tf_op jit(solution)/shard_map/ppermute | solution.py:52
  22.4 5.0 %collective-permute-done.5 = bf16[2,192,384]{2,1,0:T(8,128)(2,1)S(1)} collective-permute-done((bf16[2,192,384]{2,1,0:T(8,128)(2,1)S(1)}, bf16[2,192,384]{2,1,0:T(8,128)(2,1)S(1)}, u32[]{:S(2)}, u32[]{:S(2)}) %collective-permute-start.5) | collective-permute-done | bytes 294944 | tf_op jit(solution)/shard_map/ppermute | solution.py:52
  30.3 4.4 %collective-permute-start.8 = (bf16[1,48,1536]{2,1,0:T(8,128)(2,1)S(1)}, bf16[1,48,1536]{2,1,0:T(8,128)(2,1)S(1)}, u32[]{:S(2)}, u32[]{:S(2)}) collective-permute-start(bf16[1,48,1536]{2,1,0:T(8,128)(2,1)S(1)} %maximum_select_fusion.2), channel_id=1, source_target_pairs={{0,8},{1,17},{2,10},{3,19},{4,12},{5,21},{6,14},{7,23},{8,0},{9,25... | collective-permute-start | bytes 442376 | tf_op jit(solution)/shard_map/ppermute | solution.py:52
  34.7 3.1 %collective-permute-done.6 = bf16[4,48,1664]{2,1,0:T(8,128)(2,1)S(1)} collective-permute-done((bf16[4,48,1664]{2,1,0:T(8,128)(2,1)S(1)}, bf16[4,48,1664]{2,1,0:T(8,128)(2,1)S(1)}, u32[]{:S(2)}, u32[]{:S(2)}) %collective-permute-start.6) | collective-permute-done | bytes 639008 | tf_op jit(solution)/shard_map/ppermute | solution.py:52
  40.6 6.8 %collective-permute-done.10 = bf16[2,48,1536]{2,1,0:T(8,128)(2,1)S(1)} collective-permute-done((bf16[2,48,1536]{2,1,0:T(8,128)(2,1)S(1)}, bf16[2,48,1536]{2,1,0:T(8,128)(2,1)S(1)}, u32[]{:S(2)}, u32[]{:S(2)}) %collective-permute-start.10) | collective-permute-done | bytes 294944 | tf_op jit(solution)/shard_map/ppermute | solution.py:52
  47.4 7.9 %collective-permute-done.9.refs_3_ = bf16[8,48,1664]{2,1,0:T(8,128)(2,1)S(1)} collective-permute-done((bf16[8,48,1664]{2,1,0:T(8,128)(2,1)S(1)}, bf16[8,48,1664]{2,1,0:T(8,128)(2,1)S(1)}, u32[]{:S(2)}, u32[]{:S(2)}) %collective-permute-start.9) | collective-permute-done | bytes 1277984 | tf_op jit(solution)/shard_map/ppermute | solution.py:52
  56.7 2.2 collective-permute-start.13
  59.1 3.9 %collective-permute-start.17 = (bf16[4,192,384]{2,1,0:T(8,128)(2,1)S(1)}, bf16[4,192,384]{2,1,0:T(8,128)(2,1)S(1)}, u32[]{:S(2)}, u32[]{:S(2)}) collective-permute-start(bf16[4,192,384]{2,1,0:T(8,128)(2,1)S(1)} %pad_maximum_fusion.5), channel_id=1, source_target_pairs={{0,8},{1,17},{2,10},{3,19},{4,12},{5,21},{6,14},{7,23},{8,0},{9,25... | collective-permute-start | bytes 1769480 | tf_op jit(solution)/shard_map/ppermute | solution.py:52
  63.0 4.1 %collective-permute-done.13 = bf16[4,48,1536]{2,1,0:T(8,128)(2,1)} collective-permute-done((bf16[4,48,1536]{2,1,0:T(8,128)(2,1)}, bf16[4,48,1536]{2,1,0:T(8,128)(2,1)}, u32[]{:S(2)}, u32[]{:S(2)}) %collective-permute-start.13) | collective-permute-done | bytes 589856 | tf_op jit(solution)/shard_map/ppermute | solution.py:52
  67.1 2.3 pad_maximum_fusion.1.refs_2_
  69.4 9.8 %shard_map.330 = (bf16[768,2304]{1,0:T(8,128)(2,1)}, bf16[768,768]{1,0:T(8,128)(2,1)S(1)}, f32[12,768]{1,0:T(8,128)S(1)}, bf16[1024,2304]{1,0:T(8,128)(2,1)S(1)}) custom-call(s32[5,16]{1,0:T(8,128)S(1)} %stack.6.refs_0_, bf16[1024,768]{1,0:T(8,128)(2,1)S(1)} %copy-done.4, bf16[8,48,1664]{2,1,0:T(8,128)(2,1)S(1)} %pad_maximum_fusion.refs_2_, ...), custom_call_target="tpu_custom_call" | custom-call | flops 2400000000 | bytes 2400000 | tf_op jit(solution)/shard_map/pallas_call | solution.py:204
  81.8 8.3 %shard_map.331 = (bf16[8,6,256,128]{3,2,1,0:T(8,128)(2,1)}, bf16[1024,768]{1,0:T(8,128)(2,1)}, bf16[1024,768]{1,0:T(8,128)(2,1)}, f32[1024,128]{1,0:T(8,128)}, bf16[1024,768]{1,0:T(8,128)(2,1)S(1)}) custom-call(bf16[1024,768]{1,0:T(8,128)(2,1)S(1)} %copy-done.4, bf16[1024,2304]{1,0:T(8,128)(2,1)S(1)} %get-tuple-element.112.refs_1_, ...), custom_call_target="tpu_custom_call" | custom-call | flops 3600000000 | bytes 3600000 | tf_op jit(solution)/shard_map/pallas_call | solution.py:204
  90.2 2.5 collective-permute-start.15
  92.7 3.2 %collective-permute-done.14.refs_3_ = bf16[8,48,1536]{2,1,0:T(8,128)(2,1)} collective-permute-done((bf16[8,48,1536]{2,1,0:T(8,128)(2,1)}, bf16[8,48,1536]{2,1,0:T(8,128)(2,1)}, u32[]{:S(2)}, u32[]{:S(2)}) %collective-permute-start.14) | collective-permute-done | bytes 1179680 | tf_op jit(solution)/shard_map/ppermute | solution.py:52
  95.8 8.2 %shard_map.332 = (bf16[768,1536]{1,0:T(8,128)(2,1)}, bf16[1024,1536]{1,0:T(8,128)(2,1)S(1)}, bf16[1024,1536]{1,0:T(8,128)(2,1)}) custom-call(s32[5,16]{1,0:T(8,128)S(1)} %stack.6.refs_0_, bf16[1024,768]{1,0:T(8,128)(2,1)S(1)} %get-tuple-element.115.refs_1_.refs_7_.refs_4_, bf16[8,48,1536]{2,1,0:T(8,128)(2,1)} %pad_maximum_fusion.1.refs_2_, ...), custom_call_target="tpu_custom_call" | custom-call | flops 3000000000 | bytes 3000000 | tf_op jit(solution)/shard_map/pallas_call | solution.py:204
  105.8 5.2 %collective-permute-done.18.refs_4_ = bf16[8,192,384]{2,1,0:T(8,128)(2,1)} collective-permute-done((bf16[8,192,384]{2,1,0:T(8,128)(2,1)S(1)}, bf16[8,192,384]{2,1,0:T(8,128)(2,1)}, u32[]{:S(2)}, u32[]{:S(2)}) %collective-permute-start.18) | collective-permute-done | bytes 1179680 | tf_op jit(solution)/shard_map/ppermute | solution.py:52
  114.8 8.4 %shard_map.333 = (bf16[768,1536]{1,0:T(8,128)(2,1)}, bf16[1024,1536]{1,0:T(8,128)(2,1)S(1)}, bf16[1024,1536]{1,0:T(8,128)(2,1)}) custom-call(s32[5,16]{1,0:T(8,128)S(1)} %stack.6.refs_0_, bf16[1024,768]{1,0:T(8,128)(2,1)S(1)} %get-tuple-element.115.refs_1_.refs_7_.refs_4_, bf16[8,48,1536]{2,1,0:T(8,128)(2,1)} %collective-permute-done.15.refs_2_, ...), custom_call_target="tpu_custom_call" | custom-call | flops 3000000000 | bytes 3000000 | tf_op jit(solution)/shard_map/pallas_call | solution.py:204
  123.3 13.7 %shard_map.334 = (bf16[3072,768]{1,0:T(8,128)(2,1)}, bf16[1024,768]{1,0:T(8,128)(2,1)}, bf16[1024,768]{1,0:T(8,128)(2,1)S(1)}, f32[8,768]{1,0:T(8,128)S(1)}, f32...) custom-call(s32[5,16]{1,0:T(8,128)S(1)} %stack.7.refs_0_, bf16[1024,1536]{1,0:T(8,128)(2,1)S(1)} %copy-done.3, ...), custom_call_target="tpu_custom_call" | custom-call | flops 2400000000 | bytes 2400000 | tf_op jit(solution)/shard_map/pallas_call | solution.py:204
  138.3 8.8 %shard_map.335 = (bf16[1024,768]{1,0:T(8,128)(2,1)S(1)}, f32[8,768]{1,0:T(8,128)S(1)}, f32[8,128]{1,0:T(8,128)S(1)}, bf16[16,192,384]{2,1,0:T(8,128)(2,1)}, bf16[16,192,384]{2,1,0:T(8,128)(2,1)}) custom-call(s32[5,16]{1,0:T(8,128)S(1)} %stack.6.refs_0_, bf16[1024,768]{1,0:T(8,128)(2,1)S(1)} %get-tuple-element.125.refs_1_, ...), custom_call_target="tpu_custom_call" | custom-call | flops 2400000000 | bytes 2400000 | tf_op jit(solution)/shard_map/pallas_call | solution.py:204
  147.3 8.4 %shard_map.337 = (bf16[1024,1536]{1,0:T(8,128)(2,1)S(1)}, f32[8,768]{1,0:T(8,128)S(1)}, bf16[16,48,1536]{2,1,0:T(8,128)(2,1)S(1)}) custom-call(s32[5,16]{1,0:T(8,128)S(1)} %stack.6.refs_0_, bf16[1024,768]{1,0:T(8,128)(2,1)S(1)} %get-tuple-element.130.refs_1_.refs_4_, bf16[1024,1536]{1,0:T(8,128)(2,1)} %get-tuple-element.135.refs_2_, ...), custom_call_target="tpu_custom_call" | custom-call | flops 2400000000 | bytes 2400000 | tf_op jit(solution)/shard_map/pallas_call | solution.py:204
  156.9 8.7 %shard_map.336 = (bf16[1024,1536]{1,0:T(8,128)(2,1)S(1)}, f32[8,768]{1,0:T(8,128)S(1)}, bf16[16,48,1536]{2,1,0:T(8,128)(2,1)S(1)}) custom-call(s32[5,16]{1,0:T(8,128)S(1)} %stack.6.refs_0_, bf16[1024,768]{1,0:T(8,128)(2,1)S(1)} %get-tuple-element.130.refs_1_.refs_4_, bf16[1024,1536]{1,0:T(8,128)(2,1)} %get-tuple-element.131.refs_2_, ...), custom_call_target="tpu_custom_call" | custom-call | flops 2400000000 | bytes 2400000 | tf_op jit(solution)/shard_map/pallas_call | solution.py:204
  168.5 4.2 %collective-permute-done.24.refs_10_.refs_3_ = bf16[8,192,384]{2,1,0:T(8,128)(2,1)S(1)} collective-permute-done((bf16[8,192,384]{2,1,0:T(8,128)(2,1)S(1)}, bf16[8,192,384]{2,1,0:T(8,128)(2,1)S(1)}, u32[]{:S(2)}, u32[]{:S(2)}) %collective-permute-start.24) | collective-permute-done | bytes 1179680 | tf_op jit(solution)/shard_map/ppermute | solution.py:52
  172.9 2.1 collective-permute-start.25
  175.0 10.1 %shard_map.338 = (bf16[1024,768]{1,0:T(8,128)(2,1)S(1)}, f32[8,768]{1,0:T(8,128)S(1)}, bf16[1024,768]{1,0:T(8,128)(2,1)S(1)}) custom-call(bf16[1024,1536]{1,0:T(8,128)(2,1)S(1)} %get-tuple-element.134.refs_0_, bf16[1024,1536]{1,0:T(8,128)(2,1)S(1)} %get-tuple-element.136.refs_1_, bf16[768,1536]{1,0:T(8,128)(2,1)} %get-tuple-element.137.refs_2_, ...), custom_call_target="tpu_custom_call" | custom-call | flops 2400000000 | bytes 2400000 | tf_op jit(solution)/shard_map/pallas_call | solution.py:204
  185.1 8.5 %shard_map.339 = (bf16[1024,1536]{1,0:T(8,128)(2,1)S(1)}, f32[1,1536]{1,0:T(1,128)S(1)}) custom-call(bf16[1024,768]{1,0:T(8,128)(2,1)S(1)} %get-tuple-element.143.refs_0_, bf16[1024,2304]{1,0:T(8,128)(2,1)} %copy-done.1, bf16[8,6,256,128]{3,2,1,0:T(8,128)(2,1)} %get-tuple-element.144.refs_2_), custom_call_target="tpu_custom_call" | custom-call | flops 3600000000 | bytes 3600000 | tf_op jit(solution)/shard_map/pallas_call | solution.py:204
  193.6 4.5 %shard_map.340 = (bf16[16,48,1152]{2,1,0:T(8,128)(2,1)S(1)}, bf16[16,48,1152]{2,1,0:T(8,128)(2,1)S(1)}) custom-call(s32[5,16]{1,0:T(8,128)S(1)} %stack.6.refs_0_, bf16[1024,768]{1,0:T(8,128)(2,1)S(1)} %copy-done.5, bf16[1024,1536]{1,0:T(8,128)(2,1)S(1)} %get-tuple-element.145.refs_2_.refs_0_, bf16[1024,768]{1,0:T(8,128)(2,1)S(1)} %copy-done.6, ...), custom_call_target="tpu_custom_call" | custom-call | flops 1500000000 | bytes 1500000 | tf_op jit(solution)/shard_map/pallas_call | solution.py:204
  198.6 6.0 %shard_map.341 = (bf16[1024,768]{1,0:T(8,128)(2,1)S(1)}, f32[1,768]{1,0:T(1,128)S(1)}) custom-call(bf16[1024,768]{1,0:T(8,128)(2,1)S(1)} %get-tuple-element.143.refs_0_, bf16[1024,2304]{1,0:T(8,128)(2,1)} %copy-done.1, bf16[8,6,256,128]{3,2,1,0:T(8,128)(2,1)} %get-tuple-element.144.refs_2_, bf16[8,48,1536]{2,1,0:T(8,128)(2,1)S(1)} %collective-permute-done.28.refs_3_.refs_9_), custom_call_target="tpu_custom_call" | custom-call | flops 1800000000 | bytes 1800000 | tf_op jit(solution)/shard_map/pallas_call | solution.py:204
  204.6 3.8 %collective-permute-done.39.refs_10_ = bf16[4,48,1536]{2,1,0:T(8,128)(2,1)S(1)} collective-permute-done((bf16[4,48,1536]{2,1,0:T(8,128)(2,1)S(1)}, bf16[4,48,1536]{2,1,0:T(8,128)(2,1)S(1)}, u32[]{:S(2)}, u32[]{:S(2)}) %collective-permute-start.39) | collective-permute-done | bytes 589856 | tf_op jit(solution)/shard_map/ppermute | solution.py:52
  208.8 3.0 %collective-permute-start.37 = (bf16[2,192,384]{2,1,0:T(8,128)(2,1)S(1)}, bf16[2,192,384]{2,1,0:T(8,128)(2,1)S(1)}, u32[]{:S(2)}, u32[]{:S(2)}) collective-permute-start(bf16[2,192,384]{2,1,0:T(8,128)(2,1)S(1)} %add_convert_fusion.8), channel_id=1, source_target_pairs={{0,16},{1,9},{2,18},{3,11},{4,20},{5,13},{6,22},{7,15},{8,24},{9,1... | collective-permute-start | bytes 884744 | tf_op jit(solution)/shard_map/ppermute | solution.py:52
  211.8 2.1 shard_map.342
  214.9 5.1 %collective-permute-done.40.refs_11_ = bf16[2,48,1536]{2,1,0:T(8,128)(2,1)S(1)} collective-permute-done((bf16[2,48,1536]{2,1,0:T(8,128)(2,1)S(1)}, bf16[2,48,1536]{2,1,0:T(8,128)(2,1)S(1)}, u32[]{:S(2)}, u32[]{:S(2)}) %collective-permute-start.40) | collective-permute-done | bytes 294944 | tf_op jit(solution)/shard_map/ppermute | solution.py:52
  220.9 7.8 %shard_map.343 = f32[1024,768]{1,0:T(8,128)} custom-call(bf16[1024,1536]{1,0:T(8,128)(2,1)S(1)} %get-tuple-element.145.refs_2_.refs_0_, bf16[1024,768]{1,0:T(8,128)(2,1)S(1)} %get-tuple-element.151.refs_2_.refs_1_, bf16[768,2304]{1,0:T(8,128)(2,1)} %get-tuple-element.152.refs_2_, bf16[1024,768]{1,0:T(8,128)(2,1)S(1)} %get-tuple-element.147.refs_4_.refs_3_, ...), custom_call_target="tpu_custom_call" | custom-call | flops 2400000000 | bytes 2400000 | tf_op jit(solution)/shard_map/pallas_call | solution.py:204
  229.1 2.1 collective-permute-start.38
  231.2 2.1 collective-permute-done.33.refs_9_
  233.4 3.8 %collective-permute-done.30.refs_4_ = bf16[4,48,1152]{2,1,0:T(8,128)(2,1)S(1)} collective-permute-done((bf16[4,48,1152]{2,1,0:T(8,128)(2,1)S(1)}, bf16[4,48,1152]{2,1,0:T(8,128)(2,1)S(1)}, u32[]{:S(2)}, u32[]{:S(2)}) %collective-permute-start.30) | collective-permute-done | bytes 442400 | tf_op jit(solution)/shard_map/ppermute | solution.py:52
  237.4 1.8 collective-permute-start.31
  239.4 1.8 collective-permute-start.35
  241.2 9.0 %collective-permute-done.31.refs_5_ = bf16[2,48,1152]{2,1,0:T(8,128)(2,1)S(1)} collective-permute-done((bf16[2,48,1152]{2,1,0:T(8,128)(2,1)S(1)}, bf16[2,48,1152]{2,1,0:T(8,128)(2,1)S(1)}, u32[]{:S(2)}, u32[]{:S(2)}) %collective-permute-start.31) | collective-permute-done | bytes 221216 | tf_op jit(solution)/shard_map/ppermute | solution.py:52
  253.7 2.7 collective-permute-done.36.refs_12_
  260.1 2.0 collective-permute-start.45
  262.7 1.9 collective-permute-done.45
  264.8 2.1 collective-permute-start.47
  266.9 2.1 collective-permute-start.48
  269.5 2.8 collective-permute-done.48
  272.3 4.4 %shard_map.346 = (f32[24,2304]{1,0:T(8,128)}, f32[24,2304]{1,0:T(8,128)}, f32[24,2304]{1,0:T(8,128)}, f32[24,768]{1,0:T(8,128)}, f32[24,768]{1,0:T(8,128)}, /*in...) custom-call(s32[5,16]{1,0:T(8,128)S(1)} %stack.6.refs_0_, ...), custom_call_target="tpu_custom_call" | custom-call | flops 1200000000 | bytes 1200000 | tf_op jit(solution)/shard_map/pallas_call | solution.py:204
  (162 shorter events, 39.7 us)
Async XLA Ops:
  4.9 7.5 %collective-permute-start.1 = (bf16[1,48,1664]{2,1,0:T(8,128)(2,1)S(1)}, bf16[1,48,1664]{2,1,0:T(8,128)(2,1)S(1)}, u32[]{:S(2)}, u32[]{:S(2)}) collective-permute-start(bf16[1,48,1664]{2,1,0:T(8,128)(2,1)S(1)} %maximum_select_fusion), channel_id=1, source_target_pairs={{0,8},{1,17},{2,10},{3,19},{4,12},{5,21},{6,14},{7,23},{8,0},{9,25... | collective-permute-start | bytes 479240 | tf_op jit(solution)/shard_map/ppermute | solution.py:52
  7.9 7.2 %collective-permute-start.3 = (bf16[96,384]{1,0:T(8,128)(2,1)S(1)}, bf16[96,384]{1,0:T(8,128)(2,1)S(1)}, u32[]{:S(2)}, u32[]{:S(2)}) collective-permute-start(bf16[96,384]{1,0:T(8,128)(2,1)S(1)} %get-tuple-element.194), channel_id=1, source_target_pairs={{0,1},{1,0},{2,3},{3,2},{4,5},{5,4},{6,7},{7,6},{8,9},{9,8},{10,11... | collective-permute-start | bytes 221192 | tf_op jit(solution)/shard_map/ppermute | solution.py:56
  12.5 9.8 %collective-permute-start.2 = (bf16[2,48,1664]{2,1,0:T(8,128)(2,1)S(1)}, bf16[2,48,1664]{2,1,0:T(8,128)(2,1)S(1)}, u32[]{:S(2)}, u32[]{:S(2)}) collective-permute-start(bf16[2,48,1664]{2,1,0:T(8,128)(2,1)S(1)} %pad_maximum_fusion.6), channel_id=1, source_target_pairs={{0,16},{1,9},{2,18},{3,11},{4,20},{5,13},{6,22},{7,15},{8,24},{9,1... | collective-permute-start | bytes 958472 | tf_op jit(solution)/shard_map/ppermute | solution.py:52
  15.1 5.2 %collective-permute-start.4 = (bf16[1,192,384]{2,1,0:T(8,128)(2,1)S(1)}, bf16[1,192,384]{2,1,0:T(8,128)(2,1)S(1)}, u32[]{:S(2)}, u32[]{:S(2)}) collective-permute-start(bf16[1,192,384]{2,1,0:T(8,128)(2,1)S(1)} %maximum_select_fusion.1), channel_id=1, source_target_pairs={{0,2},{1,5},{2,0},{3,7},{4,6},{5,1},{6,4},{7,3},{8,10},{9,13},{10,... | collective-permute-start | bytes 442376 | tf_op jit(solution)/shard_map/ppermute | solution.py:52
  20.4 7.0 %collective-permute-start.5 = (bf16[2,192,384]{2,1,0:T(8,128)(2,1)S(1)}, bf16[2,192,384]{2,1,0:T(8,128)(2,1)S(1)}, u32[]{:S(2)}, u32[]{:S(2)}) collective-permute-start(bf16[2,192,384]{2,1,0:T(8,128)(2,1)S(1)} %pad_maximum_fusion.7), channel_id=1, source_target_pairs={{0,4},{1,3},{2,6},{3,1},{4,0},{5,7},{6,2},{7,5},{8,12},{9,11},{10,... | collective-permute-start | bytes 884744 | tf_op jit(solution)/shard_map/ppermute | solution.py:52
  27.4 10.4 %collective-permute-start.6 = (bf16[4,48,1664]{2,1,0:T(8,128)(2,1)S(1)}, bf16[4,48,1664]{2,1,0:T(8,128)(2,1)S(1)}, u32[]{:S(2)}, u32[]{:S(2)}) collective-permute-start(bf16[4,48,1664]{2,1,0:T(8,128)(2,1)S(1)} %pad_maximum_fusion.3), channel_id=1, source_target_pairs={{0,2},{1,5},{2,0},{3,7},{4,6},{5,1},{6,4},{7,3},{8,10},{9,13},{10,... | collective-permute-start | bytes 1916936 | tf_op jit(solution)/shard_map/ppermute | solution.py:52
  30.3 7.7 %collective-permute-start.8 = (bf16[1,48,1536]{2,1,0:T(8,128)(2,1)S(1)}, bf16[1,48,1536]{2,1,0:T(8,128)(2,1)S(1)}, u32[]{:S(2)}, u32[]{:S(2)}) collective-permute-start(bf16[1,48,1536]{2,1,0:T(8,128)(2,1)S(1)} %maximum_select_fusion.2), channel_id=1, source_target_pairs={{0,8},{1,17},{2,10},{3,19},{4,12},{5,21},{6,14},{7,23},{8,0},{9,25... | collective-permute-start | bytes 442376 | tf_op jit(solution)/shard_map/ppermute | solution.py:52
  38.0 17.3 %collective-permute-start.9 = (bf16[8,48,1664]{2,1,0:T(8,128)(2,1)S(1)}, bf16[8,48,1664]{2,1,0:T(8,128)(2,1)S(1)}, u32[]{:S(2)}, u32[]{:S(2)}) collective-permute-start(bf16[8,48,1664]{2,1,0:T(8,128)(2,1)S(1)} %pad_maximum_fusion.refs_2_), channel_id=1, source_target_pairs={{0,4},{1,3},{2,6},{3,1},{4,0},{5,7},{6,2},{7,5},{8,12},{9,11},{10,... | collective-permute-start | bytes 3833864 | tf_op jit(solution)/shard_map/ppermute | solution.py:52
  39.6 7.8 %collective-permute-start.10 = (bf16[2,48,1536]{2,1,0:T(8,128)(2,1)S(1)}, bf16[2,48,1536]{2,1,0:T(8,128)(2,1)S(1)}, u32[]{:S(2)}, u32[]{:S(2)}) collective-permute-start(bf16[2,48,1536]{2,1,0:T(8,128)(2,1)S(1)} %pad_maximum_fusion.8), channel_id=1, source_target_pairs={{0,16},{1,9},{2,18},{3,11},{4,20},{5,13},{6,22},{7,15},{8,24},{9,1... | collective-permute-start | bytes 884744 | tf_op jit(solution)/shard_map/ppermute | solution.py:52
  55.3 14.0 %collective-permute-start.12 = (bf16[8,48,1664]{2,1,0:T(8,128)(2,1)S(1)}, bf16[8,48,1664]{2,1,0:T(8,128)(2,1)}, u32[]{:S(2)}, u32[]{:S(2)}) collective-permute-start(bf16[8,48,1664]{2,1,0:T(8,128)(2,1)S(1)} %collective-permute-done.9.refs_3_), channel_id=1, source_target_pairs={{0,1},{1,0},{2,3},{3,2},{4,5},{5,4},{6,7},{7,6},{8,9},{9,8},{10,11... | collective-permute-start | bytes 3833864 | tf_op jit(solution)/shard_map/ppermute | solution.py:56
  55.3 14.0 %collective-permute-start.11 = (bf16[8,48,1664]{2,1,0:T(8,128)(2,1)S(1)}, bf16[8,48,1664]{2,1,0:T(8,128)(2,1)}, u32[]{:S(2)}, u32[]{:S(2)}) collective-permute-start(bf16[8,48,1664]{2,1,0:T(8,128)(2,1)S(1)} %pad_maximum_fusion.refs_2_), channel_id=1, source_target_pairs={{0,1},{1,0},{2,3},{3,2},{4,5},{5,4},{6,7},{7,6},{8,9},{9,8},{10,11... | collective-permute-start | bytes 3833864 | tf_op jit(solution)/shard_map/ppermute | solution.py:56
  56.7 10.4 %collective-permute-start.13 = (bf16[4,48,1536]{2,1,0:T(8,128)(2,1)}, bf16[4,48,1536]{2,1,0:T(8,128)(2,1)}, u32[]{:S(2)}, u32[]{:S(2)}) collective-permute-start(bf16[4,48,1536]{2,1,0:T(8,128)(2,1)} %pad_maximum_fusion.4), channel_id=1, source_target_pairs={{0,2},{1,5},{2,0},{3,7},{4,6},{5,1},{6,4},{7,3},{8,10},{9,13},{10,... | collective-permute-start | bytes 1769480 | tf_op jit(solution)/shard_map/ppermute | solution.py:52
  59.1 21.8 %collective-permute-start.17 = (bf16[4,192,384]{2,1,0:T(8,128)(2,1)S(1)}, bf16[4,192,384]{2,1,0:T(8,128)(2,1)S(1)}, u32[]{:S(2)}, u32[]{:S(2)}) collective-permute-start(bf16[4,192,384]{2,1,0:T(8,128)(2,1)S(1)} %pad_maximum_fusion.5), channel_id=1, source_target_pairs={{0,8},{1,17},{2,10},{3,19},{4,12},{5,21},{6,14},{7,23},{8,0},{9,25... | collective-permute-start | bytes 1769480 | tf_op jit(solution)/shard_map/ppermute | solution.py:52
  79.2 16.6 %collective-permute-start.14 = (bf16[8,48,1536]{2,1,0:T(8,128)(2,1)}, bf16[8,48,1536]{2,1,0:T(8,128)(2,1)}, u32[]{:S(2)}, u32[]{:S(2)}) collective-permute-start(bf16[8,48,1536]{2,1,0:T(8,128)(2,1)} %pad_maximum_fusion.1.refs_2_), channel_id=1, source_target_pairs={{0,4},{1,3},{2,6},{3,1},{4,0},{5,7},{6,2},{7,5},{8,12},{9,11},{10,... | collective-permute-start | bytes 3538952 | tf_op jit(solution)/shard_map/ppermute | solution.py:52
  81.0 30.0 %collective-permute-start.18 = (bf16[8,192,384]{2,1,0:T(8,128)(2,1)S(1)}, bf16[8,192,384]{2,1,0:T(8,128)(2,1)}, u32[]{:S(2)}, u32[]{:S(2)}) collective-permute-start(bf16[8,192,384]{2,1,0:T(8,128)(2,1)S(1)} %pad_maximum_fusion.2.refs_3_), channel_id=1, source_target_pairs={{0,16},{1,9},{2,18},{3,11},{4,20},{5,13},{6,22},{7,15},{8,24},{9,1... | collective-permute-start | bytes 3538952 | tf_op jit(solution)/shard_map/ppermute | solution.py:52
  90.2 24.7 %collective-permute-start.15 = (bf16[8,48,1536]{2,1,0:T(8,128)(2,1)}, bf16[8,48,1536]{2,1,0:T(8,128)(2,1)}, u32[]{:S(2)}, u32[]{:S(2)}) collective-permute-start(bf16[8,48,1536]{2,1,0:T(8,128)(2,1)} %pad_maximum_fusion.1.refs_2_), channel_id=1, source_target_pairs={{0,1},{1,0},{2,3},{3,2},{4,5},{5,4},{6,7},{7,6},{8,9},{9,8},{10,11... | collective-permute-start | bytes 3538952 | tf_op jit(solution)/shard_map/ppermute | solution.py:56
  95.8 19.0 %collective-permute-start.16 = (bf16[8,48,1536]{2,1,0:T(8,128)(2,1)}, bf16[8,48,1536]{2,1,0:T(8,128)(2,1)}, u32[]{:S(2)}, u32[]{:S(2)}) collective-permute-start(bf16[8,48,1536]{2,1,0:T(8,128)(2,1)} %collective-permute-done.14.refs_3_), channel_id=1, source_target_pairs={{0,1},{1,0},{2,3},{3,2},{4,5},{5,4},{6,7},{7,6},{8,9},{9,8},{10,11... | collective-permute-start | bytes 3538952 | tf_op jit(solution)/shard_map/ppermute | solution.py:56
  111.0 12.3 %collective-permute-start.20 = (bf16[8,192,384]{2,1,0:T(8,128)(2,1)}, bf16[8,192,384]{2,1,0:T(8,128)(2,1)}, u32[]{:S(2)}, u32[]{:S(2)}) collective-permute-start(bf16[8,192,384]{2,1,0:T(8,128)(2,1)} %collective-permute-done.18.refs_4_), channel_id=1, source_target_pairs={{0,1},{1,0},{2,3},{3,2},{4,5},{5,4},{6,7},{7,6},{8,9},{9,8},{10,11... | collective-permute-start | bytes 3538952 | tf_op jit(solution)/shard_map/ppermute | solution.py:56
  111.0 12.3 %collective-permute-start.19 = (bf16[8,192,384]{2,1,0:T(8,128)(2,1)S(1)}, bf16[8,192,384]{2,1,0:T(8,128)(2,1)}, u32[]{:S(2)}, u32[]{:S(2)}) collective-permute-start(bf16[8,192,384]{2,1,0:T(8,128)(2,1)S(1)} %pad_maximum_fusion.2.refs_3_), channel_id=1, source_target_pairs={{0,1},{1,0},{2,3},{3,2},{4,5},{5,4},{6,7},{7,6},{8,9},{9,8},{10,11... | collective-permute-start | bytes 3538952 | tf_op jit(solution)/shard_map/ppermute | solution.py:56
  147.1 9.0 %collective-permute-start.22 = (bf16[16,192,384]{2,1,0:T(8,128)(2,1)}, bf16[16,192,384]{2,1,0:T(8,128)(2,1)S(1)}, u32[]{:S(2)}, u32[]{:S(2)}) collective-permute-start(bf16[16,192,384]{2,1,0:T(8,128)(2,1)} %get-tuple-element.133), channel_id=1, source_target_pairs={{0,1},{1,0},{2,3},{3,2},{4,5},{5,4},{6,7},{7,6},{8,9},{9,8},{10,11... | collective-permute-start | bytes 7077896 | tf_op jit(solution)/shard_map/ppermute | solution.py:56
  155.7 9.9 %collective-permute-start.23 = (bf16[16,48,1536]{2,1,0:T(8,128)(2,1)S(1)}, bf16[16,48,1536]{2,1,0:T(8,128)(2,1)S(1)}, u32[]{:S(2)}, u32[]{:S(2)}) collective-permute-start(bf16[16,48,1536]{2,1,0:T(8,128)(2,1)S(1)} %get-tuple-element.141), channel_id=1, source_target_pairs={{0,1},{1,0},{2,3},{3,2},{4,5},{5,4},{6,7},{7,6},{8,9},{9,8},{10,11... | collective-permute-start | bytes 7077896 | tf_op jit(solution)/shard_map/ppermute | solution.py:56
  156.4 16.3 %collective-permute-start.24 = (bf16[8,192,384]{2,1,0:T(8,128)(2,1)S(1)}, bf16[8,192,384]{2,1,0:T(8,128)(2,1)S(1)}, u32[]{:S(2)}, u32[]{:S(2)}) collective-permute-start(bf16[8,192,384]{2,1,0:T(8,128)(2,1)S(1)} %add_convert_fusion.1), channel_id=1, source_target_pairs={{0,4},{1,3},{2,6},{3,1},{4,0},{5,7},{6,2},{7,5},{8,12},{9,11},{10,... | collective-permute-start | bytes 3538952 | tf_op jit(solution)/shard_map/ppermute | solution.py:52
  167.0 31.3 %collective-permute-start.28 = (bf16[8,48,1536]{2,1,0:T(8,128)(2,1)}, bf16[8,48,1536]{2,1,0:T(8,128)(2,1)S(1)}, u32[]{:S(2)}, u32[]{:S(2)}) collective-permute-start(bf16[8,48,1536]{2,1,0:T(8,128)(2,1)} %add_convert_fusion), channel_id=1, source_target_pairs={{0,4},{1,3},{2,6},{3,1},{4,0},{5,7},{6,2},{7,5},{8,12},{9,11},{10,... | collective-permute-start | bytes 3538952 | tf_op jit(solution)/shard_map/ppermute | solution.py:52
  172.9 20.7 %collective-permute-start.25 = (bf16[4,192,384]{2,1,0:T(8,128)(2,1)S(1)}, bf16[4,192,384]{2,1,0:T(8,128)(2,1)S(1)}, u32[]{:S(2)}, u32[]{:S(2)}) collective-permute-start(bf16[4,192,384]{2,1,0:T(8,128)(2,1)S(1)} %add_convert_fusion.4), channel_id=1, source_target_pairs={{0,2},{1,5},{2,0},{3,7},{4,6},{5,1},{6,4},{7,3},{8,10},{9,13},{10,... | collective-permute-start | bytes 1769480 | tf_op jit(solution)/shard_map/ppermute | solution.py:52
  198.2 13.6 %collective-permute-start.26 = (bf16[16,48,1152]{2,1,0:T(8,128)(2,1)S(1)}, bf16[16,48,1152]{2,1,0:T(8,128)(2,1)S(1)}, u32[]{:S(2)}, u32[]{:S(2)}) collective-permute-start(bf16[16,48,1152]{2,1,0:T(8,128)(2,1)S(1)} %get-tuple-element.149), channel_id=1, source_target_pairs={{0,1},{1,0},{2,3},{3,2},{4,5},{5,4},{6,7},{7,6},{8,9},{9,8},{10,11... | collective-permute-start | bytes 5308424 | tf_op jit(solution)/shard_map/ppermute | solution.py:56
  198.5 9.9 %collective-permute-start.39 = (bf16[4,48,1536]{2,1,0:T(8,128)(2,1)S(1)}, bf16[4,48,1536]{2,1,0:T(8,128)(2,1)S(1)}, u32[]{:S(2)}, u32[]{:S(2)}) collective-permute-start(bf16[4,48,1536]{2,1,0:T(8,128)(2,1)S(1)} %add_convert_fusion.3), channel_id=1, source_target_pairs={{0,2},{1,5},{2,0},{3,7},{4,6},{5,1},{6,4},{7,3},{8,10},{9,13},{10,... | collective-permute-start | bytes 1769480 | tf_op jit(solution)/shard_map/ppermute | solution.py:52
  208.6 11.4 %collective-permute-start.40 = (bf16[2,48,1536]{2,1,0:T(8,128)(2,1)S(1)}, bf16[2,48,1536]{2,1,0:T(8,128)(2,1)S(1)}, u32[]{:S(2)}, u32[]{:S(2)}) collective-permute-start(bf16[2,48,1536]{2,1,0:T(8,128)(2,1)S(1)} %add_convert_fusion.7), channel_id=1, source_target_pairs={{0,16},{1,9},{2,18},{3,11},{4,20},{5,13},{6,22},{7,15},{8,24},{9,1... | collective-permute-start | bytes 884744 | tf_op jit(solution)/shard_map/ppermute | solution.py:52
  208.8 20.1 %collective-permute-start.37 = (bf16[2,192,384]{2,1,0:T(8,128)(2,1)S(1)}, bf16[2,192,384]{2,1,0:T(8,128)(2,1)S(1)}, u32[]{:S(2)}, u32[]{:S(2)}) collective-permute-start(bf16[2,192,384]{2,1,0:T(8,128)(2,1)S(1)} %add_convert_fusion.8), channel_id=1, source_target_pairs={{0,16},{1,9},{2,18},{3,11},{4,20},{5,13},{6,22},{7,15},{8,24},{9,1... | collective-permute-start | bytes 884744 | tf_op jit(solution)/shard_map/ppermute | solution.py:52
  214.0 6.2 %collective-permute-start.29 = (bf16[16,48,512]{2,1,0:T(8,128)(2,1)S(1)}, bf16[16,48,512]{2,1,0:T(8,128)(2,1)S(1)}, u32[]{:S(2)}, u32[]{:S(2)}) collective-permute-start(bf16[16,48,512]{2,1,0:T(8,128)(2,1)S(1)} %get-tuple-element.159), channel_id=1, source_target_pairs={{0,1},{1,0},{2,3},{3,2},{4,5},{5,4},{6,7},{7,6},{8,9},{9,8},{10,11... | collective-permute-start | bytes 2359304 | tf_op jit(solution)/shard_map/ppermute | solution.py:56
  214.3 14.5 %collective-permute-start.27 = (bf16[8,48,1152]{2,1,0:T(8,128)(2,1)S(1)}, bf16[8,48,1152]{2,1,0:T(8,128)(2,1)S(1)}, u32[]{:S(2)}, u32[]{:S(2)}) collective-permute-start(bf16[8,48,1152]{2,1,0:T(8,128)(2,1)S(1)} %add_convert_fusion.2), channel_id=1, source_target_pairs={{0,4},{1,3},{2,6},{3,1},{4,0},{5,7},{6,2},{7,5},{8,12},{9,11},{10,... | collective-permute-start | bytes 2654216 | tf_op jit(solution)/shard_map/ppermute | solution.py:52
  220.1 32.4 %collective-permute-start.41 = (bf16[1,48,1536]{2,1,0:T(8,128)(2,1)S(1)}, bf16[1,48,1536]{2,1,0:T(8,128)(2,1)S(1)}, u32[]{:S(2)}, u32[]{:S(2)}) collective-permute-start(bf16[1,48,1536]{2,1,0:T(8,128)(2,1)S(1)} %add_convert_fusion.11), channel_id=1, source_target_pairs={{0,8},{1,17},{2,10},{3,19},{4,12},{5,21},{6,14},{7,23},{8,0},{9,25... | collective-permute-start | bytes 442376 | tf_op jit(solution)/shard_map/ppermute | solution.py:52
  220.3 13.0 %collective-permute-start.33 = (bf16[8,48,512]{2,1,0:T(8,128)(2,1)S(1)}, bf16[8,48,512]{2,1,0:T(8,128)(2,1)S(1)}, u32[]{:S(2)}, u32[]{:S(2)}) collective-permute-start(bf16[8,48,512]{2,1,0:T(8,128)(2,1)S(1)} %add_convert_fusion.6), channel_id=1, source_target_pairs={{0,4},{1,3},{2,6},{3,1},{4,0},{5,7},{6,2},{7,5},{8,12},{9,11},{10,... | collective-permute-start | bytes 1179656 | tf_op jit(solution)/shard_map/ppermute | solution.py:52
  228.9 8.4 %collective-permute-start.30 = (bf16[4,48,1152]{2,1,0:T(8,128)(2,1)S(1)}, bf16[4,48,1152]{2,1,0:T(8,128)(2,1)S(1)}, u32[]{:S(2)}, u32[]{:S(2)}) collective-permute-start(bf16[4,48,1152]{2,1,0:T(8,128)(2,1)S(1)} %add_convert_fusion.5), channel_id=1, source_target_pairs={{0,2},{1,5},{2,0},{3,7},{4,6},{5,1},{6,4},{7,3},{8,10},{9,13},{10,... | collective-permute-start | bytes 1327112 | tf_op jit(solution)/shard_map/ppermute | solution.py:52
  229.1 23.5 %collective-permute-start.38 = (bf16[1,192,384]{2,1,0:T(8,128)(2,1)S(1)}, bf16[1,192,384]{2,1,0:T(8,128)(2,1)S(1)}, u32[]{:S(2)}, u32[]{:S(2)}) collective-permute-start(bf16[1,192,384]{2,1,0:T(8,128)(2,1)S(1)} %add_convert_fusion.12), channel_id=1, source_target_pairs={{0,8},{1,17},{2,10},{3,19},{4,12},{5,21},{6,14},{7,23},{8,0},{9,25... | collective-permute-start | bytes 442376 | tf_op jit(solution)/shard_map/ppermute | solution.py:52
  233.3 6.0 %collective-permute-start.34 = (bf16[4,48,512]{2,1,0:T(8,128)(2,1)S(1)}, bf16[4,48,512]{2,1,0:T(8,128)(2,1)S(1)}, u32[]{:S(2)}, u32[]{:S(2)}) collective-permute-start(bf16[4,48,512]{2,1,0:T(8,128)(2,1)S(1)} %add_convert_fusion.10), channel_id=1, source_target_pairs={{0,2},{1,5},{2,0},{3,7},{4,6},{5,1},{6,4},{7,3},{8,10},{9,13},{10,... | collective-permute-start | bytes 589832 | tf_op jit(solution)/shard_map/ppermute | solution.py:52
  237.4 12.9 %collective-permute-start.31 = (bf16[2,48,1152]{2,1,0:T(8,128)(2,1)S(1)}, bf16[2,48,1152]{2,1,0:T(8,128)(2,1)S(1)}, u32[]{:S(2)}, u32[]{:S(2)}) collective-permute-start(bf16[2,48,1152]{2,1,0:T(8,128)(2,1)S(1)} %add_convert_fusion.9), channel_id=1, source_target_pairs={{0,16},{1,9},{2,18},{3,11},{4,20},{5,13},{6,22},{7,15},{8,24},{9,1... | collective-permute-start | bytes 663560 | tf_op jit(solution)/shard_map/ppermute | solution.py:52
  239.4 12.8 %collective-permute-start.35 = (bf16[2,48,512]{2,1,0:T(8,128)(2,1)S(1)}, bf16[2,48,512]{2,1,0:T(8,128)(2,1)S(1)}, u32[]{:S(2)}, u32[]{:S(2)}) collective-permute-start(bf16[2,48,512]{2,1,0:T(8,128)(2,1)S(1)} %add_convert_fusion.14), channel_id=1, source_target_pairs={{0,16},{1,9},{2,18},{3,11},{4,20},{5,13},{6,22},{7,15},{8,24},{9,1... | collective-permute-start | bytes 294920 | tf_op jit(solution)/shard_map/ppermute | solution.py:52
  250.3 6.1 %collective-permute-start.32 = (bf16[1,48,1152]{2,1,0:T(8,128)(2,1)S(1)}, bf16[1,48,1152]{2,1,0:T(8,128)(2,1)S(1)}, u32[]{:S(2)}, u32[]{:S(2)}) collective-permute-start(bf16[1,48,1152]{2,1,0:T(8,128)(2,1)S(1)} %add_convert_fusion.13), channel_id=1, source_target_pairs={{0,8},{1,17},{2,10},{3,19},{4,12},{5,21},{6,14},{7,23},{8,0},{9,25... | collective-permute-start | bytes 331784 | tf_op jit(solution)/shard_map/ppermute | solution.py:52
  252.3 4.2 %collective-permute-start.36 = (bf16[1,48,512]{2,1,0:T(8,128)(2,1)S(1)}, bf16[1,48,512]{2,1,0:T(8,128)(2,1)S(1)}, u32[]{:S(2)}, u32[]{:S(2)}) collective-permute-start(bf16[1,48,512]{2,1,0:T(8,128)(2,1)S(1)} %add_convert_fusion.15), channel_id=1, source_target_pairs={{0,8},{1,17},{2,10},{3,19},{4,12},{5,21},{6,14},{7,23},{8,0},{9,25... | collective-permute-start | bytes 147464 | tf_op jit(solution)/shard_map/ppermute | solution.py:52
  258.6 4.1 %collective-permute-start.43 = (f32[8,128]{1,0:T(8,128)S(1)}, f32[8,128]{1,0:T(8,128)S(1)}, u32[]{:S(2)}, u32[]{:S(2)}) collective-permute-start(f32[8,128]{1,0:T(8,128)S(1)} %add.543), channel_id=1, source_target_pairs={{0,2},{1,3},{2,0},{3,1},{4,6},{5,7},{6,4},{7,5},{8,10},{9,11},{10,... | collective-permute-start | bytes 12296 | tf_op jit(solution)/shard_map/ppermute | solution.py:52
  258.6 4.1 %collective-permute-start.44 = (f32[8,128]{1,0:T(8,128)S(1)}, f32[8,128]{1,0:T(8,128)S(1)}, u32[]{:S(2)}, u32[]{:S(2)}) collective-permute-start(f32[8,128]{1,0:T(8,128)S(1)} %add.543), channel_id=1, source_target_pairs={{0,4},{1,5},{2,6},{3,7},{4,0},{5,1},{6,2},{7,3},{8,12},{9,13},{10,... | collective-permute-start | bytes 12296 | tf_op jit(solution)/shard_map/ppermute | solution.py:52
  260.1 4.5 %collective-permute-start.45 = (f32[8,128]{1,0:T(8,128)S(1)}, f32[8,128]{1,0:T(8,128)S(1)}, u32[]{:S(2)}, u32[]{:S(2)}) collective-permute-start(f32[8,128]{1,0:T(8,128)S(1)} %add.543), channel_id=1, source_target_pairs={{0,6},{1,7},{2,4},{3,5},{4,2},{5,3},{6,0},{7,1},{8,14},{9,15},{10,... | collective-permute-start | bytes 12296 | tf_op jit(solution)/shard_map/ppermute | solution.py:176
  262.1 10.2 %collective-permute-start.49 = (f32[96,384]{1,0:T(8,128)S(1)}, f32[96,384]{1,0:T(8,128)S(1)}, u32[]{:S(2)}, u32[]{:S(2)}) collective-permute-start(f32[96,384]{1,0:T(8,128)S(1)} %get-tuple-element.167), channel_id=1, source_target_pairs={{0,1},{1,0},{2,3},{3,2},{4,5},{5,4},{6,7},{7,6},{8,9},{9,8},{10,11... | collective-permute-start | bytes 442376 | tf_op jit(solution)/shard_map/ppermute | solution.py:56
  262.1 10.2 %collective-permute-start.50 = (f32[24,1536]{1,0:T(8,128)S(1)}, f32[24,1536]{1,0:T(8,128)S(1)}, u32[]{:S(2)}, u32[]{:S(2)}) collective-permute-start(f32[24,1536]{1,0:T(8,128)S(1)} %get-tuple-element.169), channel_id=1, source_target_pairs={{0,1},{1,0},{2,3},{3,2},{4,5},{5,4},{6,7},{7,6},{8,9},{9,8},{10,11... | collective-permute-start | bytes 442376 | tf_op jit(solution)/shard_map/ppermute | solution.py:56
  264.6 4.4 %collective-permute-start.46 = (f32[8,128]{1,0:T(8,128)S(1)}, f32[8,128]{1,0:T(8,128)S(1)}, u32[]{:S(2)}, u32[]{:S(2)}) collective-permute-start(f32[8,128]{1,0:T(8,128)S(1)} %select_add_fusion.1), channel_id=1, source_target_pairs={{0,8},{1,9},{2,10},{3,11},{4,12},{5,13},{6,14},{7,15},{8,0},{9,1},... | collective-permute-start | bytes 12296 | tf_op jit(solution)/shard_map/ppermute | solution.py:52
  264.8 4.5 %collective-permute-start.47 = (f32[8,128]{1,0:T(8,128)S(1)}, f32[8,128]{1,0:T(8,128)S(1)}, u32[]{:S(2)}, u32[]{:S(2)}) collective-permute-start(f32[8,128]{1,0:T(8,128)S(1)} %select_add_fusion.1), channel_id=1, source_target_pairs={{0,16},{1,17},{2,18},{3,19},{4,20},{5,21},{6,22},{7,23},{8,24},{9,... | collective-permute-start | bytes 12296 | tf_op jit(solution)/shard_map/ppermute | solution.py:52
  266.9 5.4 %collective-permute-start.48 = (f32[8,128]{1,0:T(8,128)S(1)}, f32[8,128]{1,0:T(8,128)S(1)}, u32[]{:S(2)}, u32[]{:S(2)}) collective-permute-start(f32[8,128]{1,0:T(8,128)S(1)} %select_add_fusion.1), channel_id=1, source_target_pairs={{0,24},{1,25},{2,26},{3,27},{4,28},{5,29},{6,30},{7,31},{8,16},{9,... | collective-permute-start | bytes 12296 | tf_op jit(solution)/shard_map/ppermute | solution.py:176
  269.0 3.3 %collective-permute-start.51 = (f32[24,1152]{1,0:T(8,128)S(1)}, f32[24,1152]{1,0:T(8,128)S(1)}, u32[]{:S(2)}, u32[]{:S(2)}) collective-permute-start(f32[24,1152]{1,0:T(8,128)S(1)} %get-tuple-element.171), channel_id=1, source_target_pairs={{0,1},{1,0},{2,3},{3,2},{4,5},{5,4},{6,7},{7,6},{8,9},{9,8},{10,11... | collective-permute-start | bytes 331784 | tf_op jit(solution)/shard_map/ppermute | solution.py:56
  (19 other events, 160.7 us)
